TPU v7x, 32 devices: a whole 2x2x4 slice. The times are simulated.
32 devices in a mesh: tm: 4 (over y, x), rows: 4 (over z), dp: 2 (over core).
Axes of the slice: x: 2, y: 2, z: 4, core: 2. Of those that a mesh axis runs over, the one named last changes fastest.
Arguments:
- latent_grad: bfloat16 [18432, 64], P(('dp', 'tm'), 'rows'), parts along dimension 0, may hold values from -6 to 6
- features: bfloat16 [16, 48, 96, 384], P(('dp', 'tm'), 'rows'), parts along dimension 0, may hold values from -6 to 6
- head_weight: bfloat16 [432, 384], replicated, may hold values from -0.0625 to 0.0625
Outputs:
- grad_features: bfloat16 [16, 48, 96, 384], P(('dp', 'tm'), 'rows'), parts along dimension 0
- head_weight_grad: float32 [864, 384], P('dp'), parts along dimension 0
There are 2 independent parts, one for each index of `dp`. A program takes and returns all parts, laid end to end along the dimension named above; an argument that names none is the same for every part. Nothing has to cross between parts.
All inputs are finite; a program needn't handle non-finite values.
Results may differ from a plain program's by a relative error of at most 0.0031.
Values may be sent and summed in bfloat16 or wider, within the bound.
No kernel may reach another device: no remote copies, remote signals or barrier semaphores. Data moves between devices by JAX's collectives and lax.ppermute only.
A program may use at most 64 MiB of HBM per device.

v0:
```python
import math

import jax
import jax.numpy as jnp
from jax import lax
from jax.sharding import PartitionSpec as P


def shifted(value, axis, steps):
    count = lax.axis_size(axis)
    leading, last = (max(0, -steps), min(count, count - steps))
    return lax.ppermute(value, axis, [(source, source + steps) for source in range(leading, last)])


def extended_2(value, sides, width):
    for axis, dim in sides:
        size, length = (lax.axis_size(axis), value.shape[dim])
        up = [(i, (i + 1) % size) for i in range(size - 1)]
        down = [(j, i) for i, j in up]
        last = lax.slice_in_dim(value, length - width, length, axis=dim)
        leading = lax.slice_in_dim(value, 0, width, axis=dim)
        before = lax.ppermute(last, axis, up)
        after = lax.ppermute(leading, axis, down)
        value = jnp.concatenate([before, value, after], axis=dim)
    return value


def shards(latent_grad, features, head_weight):
    n_time = lax.axis_size("tm")
    n_rows = lax.axis_size("rows")
    frames, rows_here, width, channels = features.shape
    feat_dev = latent_grad.shape[1]
    latent_ch = feat_dev * n_rows // 4
    cycle = 2 * n_time
    per_band = rows_here // 2 * (width // 2) // cycle
    outgoing = latent_grad.reshape(n_time, frames, n_rows, per_band, 2, feat_dev)
    outgoing = outgoing.transpose(0, 2, 1, 3, 4, 5)
    moved = lax.all_to_all(
        outgoing.reshape(n_time * n_rows, -1),
        ("tm", "rows"),
        split_axis=0,
        concat_axis=0,
        tiled=True,
    )
    moved = moved.reshape(n_time, n_rows, frames, per_band, 2, feat_dev)
    first = moved[:, :, :, :, 0, :]
    second = moved[::-1, :, :, :, 1, :]
    ordered = jnp.concatenate([first, second], axis=0)
    ordered = ordered.transpose(2, 3, 0, 1, 4)
    grid = ordered.reshape(frames, rows_here // 2, width // 2, latent_ch, 2, 2)
    grid = grid.transpose(0, 1, 4, 2, 5, 3).reshape(frames, rows_here, width, latent_ch)
    later = shifted(grid, "tm", -1)
    extended = jnp.concatenate([grid, later], axis=0)
    extended = extended_2(extended, (("rows", 1),), 1)
    extended = jnp.pad(extended, ((0, 0), (0, 0), (1, 1), (0, 0)))
    pieces = []
    for kt in range(3):
        for kh in range(3):
            for kw in range(3):
                pieces.append(
                    extended[
                        2 - kt : 2 - kt + frames,
                        2 - kh : 2 - kh + rows_here,
                        2 - kw : 2 - kw + width,
                        :,
                    ]
                )
    cols = jnp.concatenate(pieces, axis=-1).reshape(frames * rows_here * width, 27 * latent_ch)
    hidden = features.reshape(-1, channels).astype(jnp.float32)
    sig = jax.nn.sigmoid(hidden)
    act = (hidden * sig).astype(jnp.bfloat16)
    scale = 1.0 / math.sqrt(frames * n_time * rows_here * n_rows * width)
    partial_grad = (
        lax.dot_general(cols, act, (((0,), (0,)), ((), ())), preferred_element_type=jnp.float32)
        * scale
    )
    weight_grad = lax.psum(partial_grad, ("tm", "rows"))
    pre = jnp.dot(cols, head_weight, preferred_element_type=jnp.float32)
    grad_features = (pre * sig * (1.0 + hidden * (1.0 - sig))).astype(jnp.bfloat16)
    return (grad_features.reshape(features.shape), weight_grad)


def solution(mesh):
    return jax.shard_map(
        shards,
        mesh=mesh,
        in_specs=(P(("dp", "tm"), "rows"), P(("dp", "tm"), "rows", None, None), P()),
        out_specs=(P(("dp", "tm"), "rows", None, None), P("dp", None)),
        check_vma=False,
    )
```

profile of v0, /device:TPU:0, one launch (start us, length us, event | category | flops | bytes accessed | tf_op | source)
XLA Modules:
  0.0 189.5 jit_solution(13073665923411959111)
XLA Ops:
  7.2 0.0 copy-start
  7.2 0.0 all-reduce.3.cloned.1.call-start
  7.2 1.2 copy.65
  8.5 0.4 copy.66
  8.9 0.4 all_to_all.8
  9.3 0.5 broadcast.37
  9.8 1.1 reduce.1
  10.9 15.6 %all_to_all.10 = bf16[16,2,1152]{2,1,0:T(2,128)(2,1)S(1)} all-to-all(bf16[16,2,1152]{2,1,0:T(2,128)(2,1)S(1)} %reshape.65), channel_id=1, replica_groups=mesh['tm'=4,'rows'=4,'dp'=2] {'tm','rows'}, dimensions={0} | all-to-all | bytes 147456 | tf_op jit(solution)/shard_map/all_to_all | solution.py:38
  26.5 0.1 reshape.66
  26.5 0.4 reduce
  26.9 0.4 reshape.58
  27.4 0.8 fusion.26
  28.2 0.6 rev.3
  28.8 0.5 copy.69
  29.3 0.5 copy.68
  29.7 0.1 maximum_bitcast_fusion
  29.8 0.9 copy.70
  30.7 0.8 reshape.59
  31.5 0.5 copy.71
  32.0 0.2 copy.72
  32.2 1.3 collective-permute-start
  33.5 5.2 %collective-permute-done = bf16[2,12,96,16]{2,3,1,0:T(8,128)(2,1)S(1)} collective-permute-done((bf16[2,12,96,16]{2,3,1,0:T(8,128)(2,1)S(1)}, bf16[2,12,96,16]{2,3,1,0:T(8,128)(2,1)S(1)}, u32[]{:S(2)}, u32[]{:S(2)}) %collective-permute-start) | collective-permute-done | bytes 73760 | tf_op jit(solution)/shard_map/ppermute | solution.py:12
  38.7 0.3 copy.73
  39.1 2.9 %collective-permute-start.1 = (bf16[4,1,96,16]{3,2,1,0:T(8,128)(2,1)S(1)}, bf16[4,1,96,16]{3,2,1,0:T(8,128)(2,1)S(1)}, u32[]{:S(2)}, u32[]{:S(2)}) collective-permute-start(bf16[4,1,96,16]{3,2,1,0:T(8,128)(2,1)S(1)} %get-tuple-element.30), channel_id=1, source_target_pairs={{0,2},{2,4},{4,6},{1,3},{3,5},{5,7},{8,10},{10,12},{12,14},{9,11},... | collective-permute-start | bytes 36872 | tf_op jit(solution)/shard_map/ppermute | solution.py:22
  42.0 1.5 collective-permute-start.2
  43.4 0.9 pad_maximum_fusion.1
  44.4 0.0 collective-permute-done.1
  44.4 4.1 %collective-permute-done.2 = bf16[4,1,96,16]{3,2,1,0:T(8,128)(2,1)S(1)} collective-permute-done((bf16[4,1,96,16]{3,2,1,0:T(8,128)(2,1)S(1)}, bf16[4,1,96,16]{3,2,1,0:T(8,128)(2,1)S(1)}, u32[]{:S(2)}, u32[]{:S(2)}) %collective-permute-start.2) | collective-permute-done | bytes 12320 | tf_op jit(solution)/shard_map/ppermute | solution.py:23
  48.5 0.6 select_maximum_fusion
  49.0 4.4 %fusion.23 = (bf16[2,12,96,16]{3,2,1,0:T(8,128)(2,1)}, bf16[2,12,96,16]{3,2,1,0:T(8,128)(2,1)}, bf16[2,12,96,16]{3,2,1,0:T(8,128)(2,1)}, bf16[2,12,96,16]{3,2,1,...) fusion(bf16[4,14,98,16]{3,2,1,0:T(8,128)(2,1)S(1)} %select_maxi, ...), kind=kLoop, calls=%fused_computation.33 | loop fusion | bytes 2654208 | tf_op jit(solution)/shard_map/slice | solution.py:61
  53.4 0.3 maximum_maximum_fusion
  53.7 1.4 fusion.24
  55.2 14.1 %concatenate.112 = bf16[2,12,96,432]{3,2,1,0:T(8,128)(2,1)} concatenate(bf16[2,12,96,16]{3,2,1,0:T(8,128)(2,1)} %get-tuple-element.21, bf16[2,12,96,16]{3,2,1,0:T(8,128)(2,1)} %get-tuple-element.34, bf16[2,12,96,16]{3,2,1,0:T(8,128)(2,1)} %get-tuple-element.20, bf16[2,12,96,16]{3,2,1,0:T(8,128)(2,1)} %get-tuple-element.19, bf16[2,12,96,16]{3,2,1,0:T(8,128)(2,1)S(1)} %copy.73, ...), dimensions={3} | concatenate | bytes 3981312 | tf_op jit(solution)/shard_map/concatenate | solution.py:68
  69.3 4.3 %fusion.19 = f32[432,384]{1,0:T(8,128)} fusion(bf16[2,12,96,432]{3,2,1,0:T(8,128)(2,1)} %concatenate.112, bf16[2,12,96,384]{3,2,1,0:T(8,128)(2,1)} %param.4), kind=kOutput, calls=%fused_computation.27 | convolution fusion | flops 769886208 | bytes 4423680 | tf_op jit(solution)/shard_map/dot_general | solution.py:74
  73.7 0.0 all-reduce.3.cloned.1.call-update
  73.7 5.3 %fusion.8 = (f32[2304,384]{1,0:T(8,128)}, f32[2304,384]{1,0:T(8,128)}) fusion(bf16[2,12,96,384]{3,2,1,0:T(8,128)(2,1)} %param.4), kind=kLoop, calls=%fused_computation.15 | loop fusion | flops 6193152 | bytes 8847360 | tf_op jit(solution)/shard_map/div | solution.py:70
  79.0 14.2 %concatenate.111 = bf16[2304,432]{1,0:T(8,128)(2,1)} concatenate(bf16[2304,16]{1,0:T(8,128)(2,1)} %bitcast.93, bf16[2304,16]{1,0:T(8,128)(2,1)} %bitcast.72, bf16[2304,16]{1,0:T(8,128)(2,1)} %bitcast.92, bf16[2304,16]{1,0:T(8,128)(2,1)} %bitcast.91, bf16[2304,16]{1,0:T(8,128)(2,1)S(1)} %bitcast.68, bf16[2304,16]{1,0:T(8,128)(2,1)} %bitcast.90, bf16[2304,16]{1,0:T(8,128)(2,1)} %bitcast.89, ...), dimensions={1} | concatenate | bytes 3981312 | tf_op jit(solution)/shard_map/concatenate | solution.py:68
  93.3 0.0 copy-done
  93.3 6.5 %fusion.1 = bf16[2304,384]{1,0:T(8,128)(2,1)} fusion(f32[2304,384]{1,0:T(8,128)} %get-tuple-element.3, f32[2304,384]{1,0:T(8,128)} %get-tuple-element.2, bf16[2304,432]{1,0:T(8,128)(2,1)} %concatenate.111, bf16[432,384]{1,0:T(8,128)(2,1)S(1)} %copy-done), kind=kOutput, calls=%fused_computation.4 | convolution fusion | flops 767066112 | bytes 11169792 | tf_op jit(solution)/shard_map/dot_general | solution.py:78
  99.7 81.0 %all-reduce.3.cloned.1.call-done = f32[432,384]{1,0:T(8,128)} async-done(((f32[432,384]{1,0:T(8,128)}), f32[432,384]{1,0:T(8,128)}) %all-reduce.3.cloned.1.call-update) | async-done | bytes 663568 | tf_op jit(solution)/shard_map/psum | solution.py:77
  180.7 2.0 %copy.79 = f32[432,384]{1,0:T(8,128)} copy(f32[432,384]{1,0:T(8,128)} %all-reduce.3.cloned.1.call-done) | data formatting | bytes 1327104
  (2 shorter events, 0.1 us)
Async XLA Ops:
  7.2 86.1 %copy-start = (bf16[432,384]{1,0:T(8,128)(2,1)S(1)}, bf16[432,384]{1,0:T(8,128)(2,1)}, u32[]{:S(2)}) copy-start(bf16[432,384]{1,0:T(8,128)(2,1)} %param.5) | copy-start | bytes 995332
  7.2 173.5 %all-reduce.3.cloned.1.call-start = ((), (), s32[]{:S(2)}) async-start(), calls=%async_computation.1 | async-start | bytes 1327104 | tf_op jit(solution)/shard_map/psum | solution.py:77
  32.2 6.5 %collective-permute-start = (bf16[2,12,96,16]{2,3,1,0:T(8,128)(2,1)S(1)}, bf16[2,12,96,16]{2,3,1,0:T(8,128)(2,1)S(1)}, u32[]{:S(2)}, u32[]{:S(2)}) collective-permute-start(bf16[2,12,96,16]{2,3,1,0:T(8,128)(2,1)S(1)} %copy.72), channel_id=1, source_target_pairs={{8,0},{16,8},{24,16},{9,1},{17,9},{25,17},{10,2},{18,10},{26,18},{... | collective-permute-start | bytes 221192 | tf_op jit(solution)/shard_map/ppermute | solution.py:12
  39.1 5.3 %collective-permute-start.1 = (bf16[4,1,96,16]{3,2,1,0:T(8,128)(2,1)S(1)}, bf16[4,1,96,16]{3,2,1,0:T(8,128)(2,1)S(1)}, u32[]{:S(2)}, u32[]{:S(2)}) collective-permute-start(bf16[4,1,96,16]{3,2,1,0:T(8,128)(2,1)S(1)} %get-tuple-element.30), channel_id=1, source_target_pairs={{0,2},{2,4},{4,6},{1,3},{3,5},{5,7},{8,10},{10,12},{12,14},{9,11},... | collective-permute-start | bytes 36872 | tf_op jit(solution)/shard_map/ppermute | solution.py:22
  42.0 6.5 %collective-permute-start.2 = (bf16[4,1,96,16]{3,2,1,0:T(8,128)(2,1)S(1)}, bf16[4,1,96,16]{3,2,1,0:T(8,128)(2,1)S(1)}, u32[]{:S(2)}, u32[]{:S(2)}) collective-permute-start(bf16[4,1,96,16]{3,2,1,0:T(8,128)(2,1)S(1)} %get-tuple-element.31), channel_id=1, source_target_pairs={{2,0},{4,2},{6,4},{3,1},{5,3},{7,5},{10,8},{12,10},{14,12},{11,9},... | collective-permute-start | bytes 36872 | tf_op jit(solution)/shard_map/ppermute | solution.py:23
Sparse Core Ops, SparseCore 0:
  73.8 106.8 all-reduce.2
where the time goes:
time: 193 us; the launch traced here: 190 us
  waiting for transfers between devices  90.3 us (47%)
  local copies, waits for them, and re-layouts  44.3 us (23%)
  blocking collectives  15.6 us (8%)
  between operations  14.2 us (7%)
  matrix products  10.8 us (6%)
  other arithmetic  8.75 us (5%)
  starting transfers between devices  5.67 us (3%)
    psum x1, waiting for transfers between devices, shards(): weight_grad = lax.psum(partial_grad, ('tm', 'rows'))  81 us
    concatenate x2, local copies, waits for them, and re-layouts, shards(): jnp.concatenate(pieces, axis=-1)  28.4 us
    all_to_all x1, blocking collectives, shards(): lax.all_to_all(outgoing.reshape(n_time * n_rows, -1), ('tm', 'rows'), spl...  15.6 us
    dot_general x1, matrix products, shards(): pre = jnp.dot(cols, head_weight, preferred_element_type=jnp.float32)  6.46 us
    slice x2, local copies, waits for them, and re-layouts, shards(): extended[2 - kt:2 - kt + frames, 2 - kh:2 - kh + rows_here, 2 - kw:2 - kw...  5.82 us
    div x1, other arithmetic, shards(): sig = jax.nn.sigmoid(hidden)  5.34 us
    ppermute x1, waiting for transfers between devices, shifted(): lax.ppermute(value, axis, [(source, source + steps) for source in range(l...  5.21 us
    dot_general x1, matrix products, shards(): lax.dot_general(cols, act, (((0,), (0,)), ((), ())), preferred_element_ty...  4.34 us
  transfers between devices with their start and end apart: 4, of which 3 were waited for; matrix products, arithmetic and copies ran while one was open for 14% of the time, Pallas kernels for 0%

commit v1 on v0

v1 whole, which is shorter than its diff:
```python
import functools
import math

import jax
import jax.numpy as jnp
import numpy as np
from jax import lax
from jax.experimental import pallas as pl
from jax.experimental.pallas import tpu as pltpu
from jax.sharding import PartitionSpec as P

LANES = 128
TAPS = 27


class Sizes:
    def __init__(self, n_time, n_rows, latent_shape, features_shape):
        self.n_time, self.n_rows = n_time, n_rows
        self.frames, self.rows, self.width, self.channels = features_shape
        self.tokens, self.feat = latent_shape
        self.latent = self.feat * n_rows // 4
        self.cycle = 2 * n_time
        self.row_tokens = self.width // 2
        self.band = self.rows // 2
        self.band_x = self.band + 2
        self.frames_x = self.frames + 2
        self.all_frames = self.frames * n_time
        self.band_cycles = self.band * self.row_tokens // self.cycle
        self.halo_cycles = -(-self.row_tokens // self.cycle)
        self.halo = 2 * self.halo_cycles
        self.lanes = 2 * self.band_cycles + 2 * self.halo
        self.sources = n_time * n_rows
        self.grid_rows = self.frames * self.rows
        self.piece_taps = -(-TAPS // n_time)
        self.piece = self.piece_taps * self.latent
        self.cols = self.piece * n_time


def sort_rows(z):
    count = z.n_rows * z.frames_x * z.feat
    out = np.zeros((count, count), np.float32)
    part = z.feat // 4
    for r in range(z.n_rows):
        for t in range(z.frames_x):
            for e in range(part):
                for p in range(2):
                    for q in range(2):
                        source = (r * z.frames_x + t) * z.feat + 4 * e + 2 * p + q
                        target = ((q * 2 + p) * z.frames_x + t) * z.latent + r * part + e
                        out[target, source] = 1
    return jnp.asarray(out, jnp.bfloat16)


def place_lanes(z):
    out = np.zeros((2, z.n_time, LANES, z.band_x, LANES), np.float32)
    for q in range(2):
        for i in range(z.n_time):
            for lane in range(z.lanes):
                place = z.cycle - 1 - i if lane % 2 else i
                token = (lane // 2 - z.halo_cycles) * z.cycle + place + z.row_tokens
                if 0 <= token < z.band_x * z.row_tokens:
                    out[q, i, lane, token // z.row_tokens, 2 * (token % z.row_tokens) + q] = 1
    return jnp.asarray(out.reshape(2 * z.n_time * LANES, z.band_x * LANES), jnp.bfloat16)


def pack_kernel(z, latent_ref, out_ref):
    tiles = z.tokens // LANES
    zero = jnp.zeros((z.feat, LANES), jnp.float32)
    lane = lax.broadcasted_iota(jnp.int32, (z.feat, LANES), 1)

    def tile(index):
        if index < 0 or index >= tiles:
            return zero
        return latent_ref[:, index * LANES : (index + 1) * LANES].astype(jnp.float32)

    def window(t, r):
        start = 2 * (t * z.n_rows + r) * z.band_cycles - z.halo
        first, offset = start // LANES, start % LANES
        value = tile(first)
        if offset:
            value = jnp.concatenate([value, tile(first + 1)], axis=1)
            value = pltpu.roll(value, 2 * LANES - offset, 1)[:, :LANES]
        low = z.halo if r == 0 else 0
        high = z.lanes - z.halo if r == z.n_rows - 1 else z.lanes
        return jnp.where((lane >= low) & (lane < high), value, 0.0)

    for r in range(z.n_rows):
        held = [window(t, r) for t in range(z.all_frames)] + [zero, zero]
        for i in range(z.n_time):
            block = jnp.concatenate(held[i * z.frames : i * z.frames + z.frames_x], axis=0)
            out_ref[i * z.n_rows + r] = block.astype(jnp.bfloat16)


def fill_cols(z, moved_ref, sort_ref, place_ref, cols_ref):
    rows = z.n_rows * z.frames_x * z.feat
    moved = [moved_ref[i * z.n_rows : (i + 1) * z.n_rows].reshape(rows, LANES) for i in range(z.n_time)]
    ordered = jnp.dot(
        sort_ref[...], jnp.concatenate(moved, axis=1), preferred_element_type=jnp.float32
    ).astype(jnp.bfloat16)
    half = rows // 2
    pair = jnp.concatenate([ordered[:half], ordered[half:]], axis=1)
    grid = jnp.dot(pair, place_ref[...], preferred_element_type=jnp.float32)
    for a in range(z.band_x):
        block = grid[:, a * LANES : (a + 1) * LANES]
        for kw in range(3):
            turned = block if kw == 1 else pltpu.roll(block, LANES - 1 if kw == 0 else 1, 1)
            turned = turned.astype(jnp.bfloat16)
            for p in range(2):
                for t in range(z.frames_x):
                    at = (p * z.frames_x + t) * z.latent
                    value = turned[at : at + z.latent]
                    for kt in range(3):
                        for kh in range(3):
                            frame, row = t - 2 + kt, 2 * (a - 1) + p - 1 + kh
                            if 0 <= frame < z.frames and 0 <= row < z.rows:
                                tap = ((kt * 3 + kh) * 3 + kw) * z.latent
                                lane = (frame * z.rows + row) * LANES
                                cols_ref[tap : tap + z.latent, lane : lane + LANES] = value
    if z.cols > TAPS * z.latent:
        shape = (z.cols - TAPS * z.latent, z.grid_rows * LANES)
        cols_ref[TAPS * z.latent :, :] = jnp.zeros(shape, jnp.bfloat16)


def weight_kernel(z, moved_ref, sort_ref, place_ref, features_ref, *refs):
    own_ref, other_refs, (cols_ref, act_ref, total_ref) = refs[0], refs[1 : z.n_time], refs[z.n_time :]
    for row in range(z.grid_rows):
        hidden = features_ref[row * z.width : (row + 1) * z.width, :].astype(jnp.float32)
        act = hidden * (0.5 + 0.5 * jnp.tanh(0.5 * hidden))
        act_ref[row * LANES : row * LANES + z.width, :] = act.astype(jnp.bfloat16)
        shape = (LANES - z.width, z.channels)
        act_ref[row * LANES + z.width : (row + 1) * LANES, :] = jnp.zeros(shape, jnp.bfloat16)
    fill_cols(z, moved_ref, sort_ref, place_ref, cols_ref)
    total_ref[...] = jnp.dot(cols_ref[...], act_ref[...], preferred_element_type=jnp.float32)
    me = lax.axis_index("tm")
    for step in range(z.n_time):
        start = pl.multiple_of((me ^ step) * z.piece, z.piece)
        value = total_ref[pl.ds(start, z.piece), :]
        if step == 0:
            own_ref[...] = value
        else:
            other_refs[step - 1][...] = value.astype(jnp.bfloat16)


def features_kernel(z, moved_ref, sort_ref, place_ref, features_ref, weight_ref, out_ref, cols_ref):
    fill_cols(z, moved_ref, sort_ref, place_ref, cols_ref)
    step = 4
    for first in range(0, z.grid_rows, step):
        count = min(step, z.grid_rows - first)
        part = cols_ref[: TAPS * z.latent, first * LANES : (first + count) * LANES]
        product = lax.dot_general(
            part, weight_ref[...], (((0,), (0,)), ((), ())), preferred_element_type=jnp.float32
        )
        for k in range(count):
            row = first + k
            hidden = features_ref[row * z.width : (row + 1) * z.width, :].astype(jnp.float32)
            sig = 0.5 + 0.5 * jnp.tanh(0.5 * hidden)
            value = product[k * LANES : k * LANES + z.width] * sig * (1.0 + hidden * (1.0 - sig))
            out_ref[row * z.width : (row + 1) * z.width, :] = value.astype(jnp.bfloat16)


def join_kernel(z, *refs):
    piece_refs, out_ref, held_ref = refs[: z.n_time], refs[z.n_time], refs[z.n_time + 1]
    me = lax.axis_index("tm")
    for step, ref in enumerate(piece_refs):
        start = pl.multiple_of((me ^ step) * z.piece, z.piece)
        held_ref[pl.ds(start, z.piece), :] = ref[...].astype(jnp.float32)
    out_ref[...] = held_ref[: TAPS * z.latent, :]


def exchange(values, axis):
    size = lax.axis_size(axis)
    return [
        lax.ppermute(value, axis, [(i, i ^ step) for i in range(size)])
        for step, value in enumerate(values, 1)
    ]


def tree_sum(values):
    while len(values) > 1:
        values = [values[i] + values[i + 1] for i in range(0, len(values), 2)]
    return values[0]


def shards(latent_grad, features, head_weight):
    n_time, n_rows = lax.axis_size("tm"), lax.axis_size("rows")
    z = Sizes(n_time, n_rows, latent_grad.shape, features.shape)
    params = pltpu.CompilerParams(vmem_limit_bytes=32 * 1024 * 1024)
    f32, bf16 = jnp.float32, jnp.bfloat16
    cells = z.grid_rows * z.width
    packed = pl.pallas_call(
        functools.partial(pack_kernel, z),
        out_shape=jax.ShapeDtypeStruct((z.sources, z.frames_x * z.feat, LANES), bf16),
        compiler_params=params,
        name="pack_latents",
    )(latent_grad.T)
    moved = lax.all_to_all(packed, ("tm", "rows"), 0, 0, tiled=True)
    sort, place = sort_rows(z), place_lanes(z)
    flat = features.reshape(cells, z.channels)
    cols_scratch = pltpu.VMEM((z.cols, z.grid_rows * LANES), bf16)
    products = z.cols * z.grid_rows * LANES * z.channels
    pieces = pl.pallas_call(
        functools.partial(weight_kernel, z),
        out_shape=[
            jax.ShapeDtypeStruct((z.piece, z.channels), bf16 if s else f32) for s in range(n_time)
        ],
        scratch_shapes=[
            cols_scratch,
            pltpu.VMEM((z.grid_rows * LANES, z.channels), bf16),
            pltpu.VMEM((z.cols, z.channels), f32),
        ],
        compiler_params=params,
        cost_estimate=pl.CostEstimate(
            flops=2 * products, bytes_accessed=2 * cells * z.channels, transcendentals=cells * z.channels
        ),
        name="weight_term",
    )(moved, sort, place, flat)
    grad = pl.pallas_call(
        functools.partial(features_kernel, z),
        out_shape=jax.ShapeDtypeStruct((cells, z.channels), bf16),
        scratch_shapes=[cols_scratch],
        compiler_params=params,
        cost_estimate=pl.CostEstimate(
            flops=2 * products, bytes_accessed=4 * cells * z.channels, transcendentals=cells * z.channels
        ),
        name="features_grad",
    )(moved, sort, place, flat, head_weight)
    arrived = exchange(pieces[1:], "tm")
    mine = tree_sum([pieces[0]] + [value.astype(f32) for value in arrived]).astype(bf16)
    arrived = exchange([mine] * (n_rows - 1), "rows")
    whole = tree_sum([value.astype(f32) for value in [mine] + arrived])
    scale = 1.0 / math.sqrt(cells * n_time * n_rows)
    whole = (whole * scale).astype(bf16)
    arrived = exchange([whole] * (n_time - 1), "tm")
    weight_grad = pl.pallas_call(
        functools.partial(join_kernel, z),
        out_shape=jax.ShapeDtypeStruct((TAPS * z.latent, z.channels), f32),
        scratch_shapes=[pltpu.VMEM((z.cols, z.channels), f32)],
        compiler_params=params,
        name="join_pieces",
    )(whole, *arrived)
    return (grad.reshape(features.shape), weight_grad)


def solution(mesh):
    return jax.shard_map(
        shards,
        mesh=mesh,
        in_specs=(P(("dp", "tm"), "rows"), P(("dp", "tm"), "rows", None, None), P()),
        out_specs=(P(("dp", "tm"), "rows", None, None), P("dp", None)),
        check_vma=False,
    )
```

time: 193 us -> 51 us (0.26); the launches traced: 190 us -> 50.8 us
  waiting for transfers between devices: 90.3 us -> 6.79 us
  local copies, waits for them, and re-layouts: 44.3 us -> 4.85 us
  between operations: 14.2 us -> 0.68 us
  matrix products: 10.8 us -> 0 us
  other arithmetic: 8.75 us -> 0.1 us
  Pallas kernels: 0 us -> 8.08 us
  starting transfers between devices: 5.67 us -> 11.6 us
  blocking collectives: 15.6 us -> 18.7 us
    psum x1 -> x0, waiting for transfers between devices: 81 us -> none  [shards(): weight_grad = lax.psum(partial_grad, ('tm', 'rows'))]
    concatenate x2 -> x0, local copies, waits for them, and re-layouts: 28.4 us -> none  [shards(): jnp.concatenate(pieces, axis=-1)]
    dot_general x2 -> x0, matrix products: 10.8 us -> none  [the longest x1 6.46 us: shards(): pre = jnp.dot(cols, head_weight, preferred_element_type=jnp.float32)]
    pallas_call x0 -> x4, Pallas kernels: none -> 8.08 us  [the longest x1 4.53 us: shards(): pl.pallas_call(functools.partial(features_kernel, z), out_shape=jax.Shape...]
    slice x4 -> x0, local copies, waits for them, and re-layouts: 7.09 us -> none  [the longest x2 5.82 us: shards(): extended[2 - kt:2 - kt + frames, 2 - kh:2 - kh + rows_here, 2 - kw:2 - kw...]
    ppermute x3 -> x9, starting transfers between devices: 5.63 us -> 11.6 us  [exchange(): lax.ppermute(value, axis, [(i, i ^ step) for i in range(size)])]
    div x1 -> x0, other arithmetic: 5.34 us -> none  [shards(): sig = jax.nn.sigmoid(hidden)]
    all_to_all x1, blocking collectives: 15.6 us -> 18.7 us  [shards(): moved = lax.all_to_all(packed, ('tm', 'rows'), 0, 0, tiled=True)]
  transfers between devices with their start and end apart: 4 -> 9, of which waited for: 3 -> 5; matrix products, arithmetic and copies ran while one was open for 14% -> 0% of each run, Pallas kernels for 0% -> 9%
where the time goes in v1:
time: 51 us; the launch traced here: 50.8 us
  blocking collectives  18.7 us (37%)
  starting transfers between devices  11.6 us (23%)
  Pallas kernels  8.08 us (16%)
  waiting for transfers between devices  6.79 us (13%)
  local copies, waits for them, and re-layouts  4.85 us (10%)
  between operations  0.68 us (1%)
    all_to_all x1, blocking collectives, shards(): moved = lax.all_to_all(packed, ('tm', 'rows'), 0, 0, tiled=True)  18.7 us
    ppermute x9, starting transfers between devices, exchange(): lax.ppermute(value, axis, [(i, i ^ step) for i in range(size)])  11.6 us
    ppermute x9, waiting for transfers between devices, exchange(): lax.ppermute(value, axis, [(i, i ^ step) for i in range(size)])  6.79 us
    unnamed x10, local copies, waits for them, and re-layouts  4.85 us
    pallas_call x1, Pallas kernels, shards(): pl.pallas_call(functools.partial(features_kernel, z), out_shape=jax.Shape...  4.53 us
    pallas_call x1, Pallas kernels, shards(): pl.pallas_call(functools.partial(weight_kernel, z), out_shape=[jax.ShapeD...  2.47 us
  transfers between devices with their start and end apart: 9, of which 5 were waited for; matrix products, arithmetic and copies ran while one was open for 0% of the time, Pallas kernels for 9%

profile of v1, /device:TPU:0, one launch (start us, length us, event | category | flops | bytes accessed | tf_op | source)
XLA Modules:
  0.0 50.8 jit_solution(17066997989981951358)
XLA Ops:
  0.6 0.0 copy-start.4
  0.6 0.9 %copy-done.4 = bf16[2304,16]{0,1:T(8,128)(2,1)S(1)} copy-done((bf16[2304,16]{0,1:T(8,128)(2,1)S(1)}, bf16[2304,16]{0,1:T(8,128)(2,1)}, u32[]{:S(2)}) %copy-start.4) | copy-done | bytes 73752
  1.5 0.1 pack_latents.1
  1.7 18.7 %all_to_all.5.moved_ref = bf16[16,64,128]{2,1,0:T(8,128)(2,1)S(1)} all-to-all(bf16[16,64,128]{2,1,0:T(8,128)(2,1)S(1)} %pack_latents.1), channel_id=1, replica_groups=mesh['tm'=4,'rows'=4,'dp'=2] {'tm','rows'}, dimensions={0} | all-to-all | bytes 524288 | tf_op jit(solution)/shard_map/all_to_all | solution.py:196
  20.3 0.0 copy-start
  20.3 1.6 %copy-done = bf16[1024,1024]{1,0:T(8,128)(2,1)S(1)} copy-done((bf16[1024,1024]{1,0:T(8,128)(2,1)S(1)}, bf16[1024,1024]{1,0:T(8,128)(2,1)}, u32[]{:S(2)}) %copy-start) | copy-done | bytes 2097176
  21.9 0.0 copy-start.1
  21.9 1.5 %copy-done.1 = bf16[2,12,96,384]{3,2,1,0:T(8,128)(2,1)S(1)} copy-done((bf16[2,12,96,384]{3,2,1,0:T(8,128)(2,1)S(1)}, bf16[2,12,96,384]{3,2,1,0:T(8,128)(2,1)}, u32[]{:S(2)}) %copy-start.1) | copy-done | bytes 1769496
  23.4 0.0 copy-start.2
  23.4 0.9 %copy-done.2 = bf16[256,256]{1,0:T(8,128)(2,1)S(1)} copy-done((bf16[256,256]{1,0:T(8,128)(2,1)S(1)}, bf16[256,256]{1,0:T(8,128)(2,1)}, u32[]{:S(2)}) %copy-start.2) | copy-done | bytes 131096
  24.3 0.0 copy-start.3
  24.3 2.5 %weight_term.1 = (f32[112,384]{1,0:T(8,128)S(1)}, bf16[112,384]{1,0:T(8,128)(2,1)S(1)}, bf16[112,384]{1,0:T(8,128)(2,1)S(1)}, bf16[112,384]{1,0:T(8,128)(2,1)S(1)}) custom-call(bf16[16,64,128]{2,1,0:T(8,128)(2,1)S(1)} %all_to_all.5.moved_ref, bf16[256,256]{1,0:T(8,128)(2,1)S(1)} %copy-done.2, bf16[1024,1024]{1,0:T(8,128)(2,1)S(1)} %copy-done, ...), custom_call_target="tpu_custom_call" | custom-call | flops 1056964608 | bytes 1769472 | tf_op jit(solution)/shard_map/weight_term/pallas_call | solution.py:201
  26.8 0.1 collective-permute-start
  26.9 1.1 %collective-permute-start.1 = (bf16[112,384]{1,0:T(8,128)(2,1)S(1)}, bf16[112,384]{1,0:T(8,128)(2,1)S(1)}, u32[]{:S(2)}, u32[]{:S(2)}) collective-permute-start(bf16[112,384]{1,0:T(8,128)(2,1)S(1)} %get-tuple-element.8), channel_id=1, source_target_pairs={{0,16},{8,24},{16,0},{24,8},{1,17},{9,25},{17,1},{25,9},{2,18},{10... | collective-permute-start | bytes 258056 | tf_op jit(solution)/shard_map/ppermute | solution.py:173
  28.0 2.3 %collective-permute-start.2 = (bf16[112,384]{1,0:T(8,128)(2,1)S(1)}, bf16[112,384]{1,0:T(8,128)(2,1)S(1)}, u32[]{:S(2)}, u32[]{:S(2)}) collective-permute-start(bf16[112,384]{1,0:T(8,128)(2,1)S(1)} %get-tuple-element.9), channel_id=1, source_target_pairs={{0,24},{8,16},{16,8},{24,0},{1,25},{9,17},{17,9},{25,1},{2,26},{10... | collective-permute-start | bytes 258056 | tf_op jit(solution)/shard_map/ppermute | solution.py:173
  30.4 1.0 %collective-permute-done = bf16[112,384]{1,0:T(8,128)(2,1)S(1)} collective-permute-done((bf16[112,384]{1,0:T(8,128)(2,1)S(1)}, bf16[112,384]{1,0:T(8,128)(2,1)S(1)}, u32[]{:S(2)}, u32[]{:S(2)}) %collective-permute-start) | collective-permute-done | bytes 86048 | tf_op jit(solution)/shard_map/ppermute | solution.py:173
  31.3 0.1 collective-permute-done.1
  31.4 2.0 %collective-permute-done.2 = bf16[112,384]{1,0:T(8,128)(2,1)S(1)} collective-permute-done((bf16[112,384]{1,0:T(8,128)(2,1)S(1)}, bf16[112,384]{1,0:T(8,128)(2,1)S(1)}, u32[]{:S(2)}, u32[]{:S(2)}) %collective-permute-start.2) | collective-permute-done | bytes 86048 | tf_op jit(solution)/shard_map/ppermute | solution.py:173
  33.5 1.5 %collective-permute-start.5 = (bf16[112,384]{1,0:T(8,128)(2,1)S(1)}, bf16[112,384]{1,0:T(8,128)(2,1)S(1)}, u32[]{:S(2)}, u32[]{:S(2)}) collective-permute-start(bf16[112,384]{1,0:T(8,128)(2,1)S(1)} %add_convert_fusion), channel_id=1, source_target_pairs={{0,6},{2,4},{4,2},{6,0},{1,7},{3,5},{5,3},{7,1},{8,14},{10,12},{12... | collective-permute-start | bytes 258056 | tf_op jit(solution)/shard_map/ppermute | solution.py:173
  35.0 0.4 collective-permute-start.4
  35.4 2.5 %collective-permute-start.3 = (bf16[112,384]{1,0:T(8,128)(2,1)S(1)}, bf16[112,384]{1,0:T(8,128)(2,1)S(1)}, u32[]{:S(2)}, u32[]{:S(2)}) collective-permute-start(bf16[112,384]{1,0:T(8,128)(2,1)S(1)} %add_convert_fusion), channel_id=1, source_target_pairs={{0,2},{2,0},{4,6},{6,4},{1,3},{3,1},{5,7},{7,5},{8,10},{10,8},{12,... | collective-permute-start | bytes 258056 | tf_op jit(solution)/shard_map/ppermute | solution.py:173
  37.9 2.0 %collective-permute-done.5 = bf16[112,384]{1,0:T(8,128)(2,1)S(1)} collective-permute-done((bf16[112,384]{1,0:T(8,128)(2,1)S(1)}, bf16[112,384]{1,0:T(8,128)(2,1)S(1)}, u32[]{:S(2)}, u32[]{:S(2)}) %collective-permute-start.5) | collective-permute-done | bytes 86048 | tf_op jit(solution)/shard_map/ppermute | solution.py:173
  39.9 1.8 %collective-permute-done.4 = bf16[112,384]{1,0:T(8,128)(2,1)S(1)} collective-permute-done((bf16[112,384]{1,0:T(8,128)(2,1)S(1)}, bf16[112,384]{1,0:T(8,128)(2,1)S(1)}, u32[]{:S(2)}, u32[]{:S(2)}) %collective-permute-start.4) | collective-permute-done | bytes 86048 | tf_op jit(solution)/shard_map/ppermute | solution.py:173
  41.6 0.0 collective-permute-done.3
  41.6 0.1 multiply_convert_fusion.refs_0_
  41.7 2.0 %collective-permute-start.8 = (bf16[112,384]{1,0:T(8,128)(2,1)S(1)}, bf16[112,384]{1,0:T(8,128)(2,1)S(1)}, u32[]{:S(2)}, u32[]{:S(2)}) collective-permute-start(bf16[112,384]{1,0:T(8,128)(2,1)S(1)} %multiply_convert_fusion.refs_0_), channel_id=1, source_target_pairs={{0,24},{8,16},{16,8},{24,0},{1,25},{9,17},{17,9},{25,1},{2,26},{10... | collective-permute-start | bytes 258056 | tf_op jit(solution)/shard_map/ppermute | solution.py:173
  43.7 0.8 %collective-permute-start.7 = (bf16[112,384]{1,0:T(8,128)(2,1)S(1)}, bf16[112,384]{1,0:T(8,128)(2,1)S(1)}, u32[]{:S(2)}, u32[]{:S(2)}) collective-permute-start(bf16[112,384]{1,0:T(8,128)(2,1)S(1)} %multiply_convert_fusion.refs_0_), channel_id=1, source_target_pairs={{0,16},{8,24},{16,0},{24,8},{1,17},{9,25},{17,1},{25,9},{2,18},{10... | collective-permute-start | bytes 258056 | tf_op jit(solution)/shard_map/ppermute | solution.py:173
  44.5 0.8 %collective-permute-start.6 = (bf16[112,384]{1,0:T(8,128)(2,1)S(1)}, bf16[112,384]{1,0:T(8,128)(2,1)S(1)}, u32[]{:S(2)}, u32[]{:S(2)}) collective-permute-start(bf16[112,384]{1,0:T(8,128)(2,1)S(1)} %multiply_convert_fusion.refs_0_), channel_id=1, source_target_pairs={{0,8},{8,0},{16,24},{24,16},{1,9},{9,1},{17,25},{25,17},{2,10},{10... | collective-permute-start | bytes 258056 | tf_op jit(solution)/shard_map/ppermute | solution.py:173
  45.3 0.0 copy-done.3
  45.3 4.5 %features_grad.1 = bf16[2304,384]{1,0:T(8,128)(2,1)} custom-call(bf16[16,64,128]{2,1,0:T(8,128)(2,1)S(1)} %all_to_all.5.moved_ref, bf16[256,256]{1,0:T(8,128)(2,1)S(1)} %copy-done.2, bf16[1024,1024]{1,0:T(8,128)(2,1)S(1)} %copy-done, bf16[2304,384]{1,0:T(8,128)(2,1)S(1)} %bitcast.4, bf16[432,384]{1,0:T(8,128)(2,1)S(1)} %copy-done.3), custom_call_target="tpu_custom_call" | custom-call | flops 1056964608 | bytes 3538944 | tf_op jit(solution)/shard_map/features_grad/pallas_call | solution.py:217
  49.8 0.0 collective-permute-done.8.refs_3_
  49.8 0.0 collective-permute-done.7.refs_2_
  49.8 0.0 collective-permute-done.6.refs_1_
  49.8 0.9 %join_pieces.1 = f32[432,384]{1,0:T(8,128)} custom-call(bf16[112,384]{1,0:T(8,128)(2,1)S(1)} %multiply_convert_fusion.refs_0_, bf16[112,384]{1,0:T(8,128)(2,1)S(1)} %collective-permute-done.6.refs_1_, bf16[112,384]{1,0:T(8,128)(2,1)S(1)} %collective-permute-done.7.refs_2_, bf16[112,384]{1,0:T(8,128)(2,1)S(1)} %collective-permute-done.8.refs_3_), custom_call_target="tpu_custom_call" | custom-call | tf_op jit(solution)/shard_map/join_pieces/pallas_call | solution.py:234
  (1 shorter events, 0.0 us)
Async XLA Ops:
  0.6 0.9 %copy-start.4 = (bf16[2304,16]{0,1:T(8,128)(2,1)S(1)}, bf16[2304,16]{0,1:T(8,128)(2,1)}, u32[]{:S(2)}) copy-start(bf16[2304,16]{0,1:T(8,128)(2,1)} %param.5) | copy-start | bytes 221188
  20.3 1.6 %copy-start = (bf16[1024,1024]{1,0:T(8,128)(2,1)S(1)}, bf16[1024,1024]{1,0:T(8,128)(2,1)}, u32[]{:S(2)}) copy-start(bf16[1024,1024]{1,0:T(8,128)(2,1)} %constant.7.clone.place_ref) | copy-start | bytes 6291460
  21.9 1.5 %copy-start.1 = (bf16[2,12,96,384]{3,2,1,0:T(8,128)(2,1)S(1)}, bf16[2,12,96,384]{3,2,1,0:T(8,128)(2,1)}, u32[]{:S(2)}) copy-start(bf16[2,12,96,384]{3,2,1,0:T(8,128)(2,1)} %param.6) | copy-start | bytes 5308420
  23.4 0.9 %copy-start.2 = (bf16[256,256]{1,0:T(8,128)(2,1)S(1)}, bf16[256,256]{1,0:T(8,128)(2,1)}, u32[]{:S(2)}) copy-start(bf16[256,256]{1,0:T(8,128)(2,1)} %constant.6.clone.sort_ref) | copy-start | bytes 393220
  24.3 21.0 %copy-start.3 = (bf16[432,384]{1,0:T(8,128)(2,1)S(1)}, bf16[432,384]{1,0:T(8,128)(2,1)}, u32[]{:S(2)}) copy-start(bf16[432,384]{1,0:T(8,128)(2,1)} %weight_ref.1) | copy-start | bytes 995332
  26.8 4.6 %collective-permute-start = (bf16[112,384]{1,0:T(8,128)(2,1)S(1)}, bf16[112,384]{1,0:T(8,128)(2,1)S(1)}, u32[]{:S(2)}, u32[]{:S(2)}) collective-permute-start(bf16[112,384]{1,0:T(8,128)(2,1)S(1)} %get-tuple-element.7), channel_id=1, source_target_pairs={{0,8},{8,0},{16,24},{24,16},{1,9},{9,1},{17,25},{25,17},{2,10},{10... | collective-permute-start | bytes 258056 | tf_op jit(solution)/shard_map/ppermute | solution.py:173
  26.9 4.6 %collective-permute-start.1 = (bf16[112,384]{1,0:T(8,128)(2,1)S(1)}, bf16[112,384]{1,0:T(8,128)(2,1)S(1)}, u32[]{:S(2)}, u32[]{:S(2)}) collective-permute-start(bf16[112,384]{1,0:T(8,128)(2,1)S(1)} %get-tuple-element.8), channel_id=1, source_target_pairs={{0,16},{8,24},{16,0},{24,8},{1,17},{9,25},{17,1},{25,9},{2,18},{10... | collective-permute-start | bytes 258056 | tf_op jit(solution)/shard_map/ppermute | solution.py:173
  28.0 5.4 %collective-permute-start.2 = (bf16[112,384]{1,0:T(8,128)(2,1)S(1)}, bf16[112,384]{1,0:T(8,128)(2,1)S(1)}, u32[]{:S(2)}, u32[]{:S(2)}) collective-permute-start(bf16[112,384]{1,0:T(8,128)(2,1)S(1)} %get-tuple-element.9), channel_id=1, source_target_pairs={{0,24},{8,16},{16,8},{24,0},{1,25},{9,17},{17,9},{25,1},{2,26},{10... | collective-permute-start | bytes 258056 | tf_op jit(solution)/shard_map/ppermute | solution.py:173
  33.5 6.4 %collective-permute-start.5 = (bf16[112,384]{1,0:T(8,128)(2,1)S(1)}, bf16[112,384]{1,0:T(8,128)(2,1)S(1)}, u32[]{:S(2)}, u32[]{:S(2)}) collective-permute-start(bf16[112,384]{1,0:T(8,128)(2,1)S(1)} %add_convert_fusion), channel_id=1, source_target_pairs={{0,6},{2,4},{4,2},{6,0},{1,7},{3,5},{5,3},{7,1},{8,14},{10,12},{12... | collective-permute-start | bytes 258056 | tf_op jit(solution)/shard_map/ppermute | solution.py:173
  35.0 6.7 %collective-permute-start.4 = (bf16[112,384]{1,0:T(8,128)(2,1)S(1)}, bf16[112,384]{1,0:T(8,128)(2,1)S(1)}, u32[]{:S(2)}, u32[]{:S(2)}) collective-permute-start(bf16[112,384]{1,0:T(8,128)(2,1)S(1)} %add_convert_fusion), channel_id=1, source_target_pairs={{0,4},{2,6},{4,0},{6,2},{1,5},{3,7},{5,1},{7,3},{8,12},{10,14},{12... | collective-permute-start | bytes 258056 | tf_op jit(solution)/shard_map/ppermute | solution.py:173
  35.4 6.3 %collective-permute-start.3 = (bf16[112,384]{1,0:T(8,128)(2,1)S(1)}, bf16[112,384]{1,0:T(8,128)(2,1)S(1)}, u32[]{:S(2)}, u32[]{:S(2)}) collective-permute-start(bf16[112,384]{1,0:T(8,128)(2,1)S(1)} %add_convert_fusion), channel_id=1, source_target_pairs={{0,2},{2,0},{4,6},{6,4},{1,3},{3,1},{5,7},{7,5},{8,10},{10,8},{12,... | collective-permute-start | bytes 258056 | tf_op jit(solution)/shard_map/ppermute | solution.py:173
  41.7 8.1 %collective-permute-start.8 = (bf16[112,384]{1,0:T(8,128)(2,1)S(1)}, bf16[112,384]{1,0:T(8,128)(2,1)S(1)}, u32[]{:S(2)}, u32[]{:S(2)}) collective-permute-start(bf16[112,384]{1,0:T(8,128)(2,1)S(1)} %multiply_convert_fusion.refs_0_), channel_id=1, source_target_pairs={{0,24},{8,16},{16,8},{24,0},{1,25},{9,17},{17,9},{25,1},{2,26},{10... | collective-permute-start | bytes 258056 | tf_op jit(solution)/shard_map/ppermute | solution.py:173
  43.7 6.1 %collective-permute-start.7 = (bf16[112,384]{1,0:T(8,128)(2,1)S(1)}, bf16[112,384]{1,0:T(8,128)(2,1)S(1)}, u32[]{:S(2)}, u32[]{:S(2)}) collective-permute-start(bf16[112,384]{1,0:T(8,128)(2,1)S(1)} %multiply_convert_fusion.refs_0_), channel_id=1, source_target_pairs={{0,16},{8,24},{16,0},{24,8},{1,17},{9,25},{17,1},{25,9},{2,18},{10... | collective-permute-start | bytes 258056 | tf_op jit(solution)/shard_map/ppermute | solution.py:173
  44.5 5.3 %collective-permute-start.6 = (bf16[112,384]{1,0:T(8,128)(2,1)S(1)}, bf16[112,384]{1,0:T(8,128)(2,1)S(1)}, u32[]{:S(2)}, u32[]{:S(2)}) collective-permute-start(bf16[112,384]{1,0:T(8,128)(2,1)S(1)} %multiply_convert_fusion.refs_0_), channel_id=1, source_target_pairs={{0,8},{8,0},{16,24},{24,16},{1,9},{9,1},{17,25},{25,17},{2,10},{10... | collective-permute-start | bytes 258056 | tf_op jit(solution)/shard_map/ppermute | solution.py:173

commit v2 on v1

--- a/solution.py
+++ b/solution.py
@@ -63,39 +63,80 @@
     return jnp.asarray(out.reshape(2 * z.n_time * LANES, z.band_x * LANES), jnp.bfloat16)
 
 
-def pack_kernel(z, latent_ref, out_ref):
-    tiles = z.tokens // LANES
-    zero = jnp.zeros((z.feat, LANES), jnp.float32)
+def window_kernel(z, source_ref, *refs):
+    out_refs, tokens_ref, sem = refs[:-2], refs[-2], refs[-1]
+    load = pltpu.make_async_copy(source_ref, tokens_ref, sem)
+    load.start()
+    load.wait()
+    band = lax.axis_index("rows")
     lane = lax.broadcasted_iota(jnp.int32, (z.feat, LANES), 1)
-
-    def tile(index):
-        if index < 0 or index >= tiles:
-            return zero
-        return latent_ref[:, index * LANES : (index + 1) * LANES].astype(jnp.float32)
-
-    def window(t, r):
-        start = 2 * (t * z.n_rows + r) * z.band_cycles - z.halo
-        first, offset = start // LANES, start % LANES
-        value = tile(first)
-        if offset:
-            value = jnp.concatenate([value, tile(first + 1)], axis=1)
-            value = pltpu.roll(value, 2 * LANES - offset, 1)[:, :LANES]
-        low = z.halo if r == 0 else 0
-        high = z.lanes - z.halo if r == z.n_rows - 1 else z.lanes
-        return jnp.where((lane >= low) & (lane < high), value, 0.0)
-
-    for r in range(z.n_rows):
-        held = [window(t, r) for t in range(z.all_frames)] + [zero, zero]
-        for i in range(z.n_time):
-            block = jnp.concatenate(held[i * z.frames : i * z.frames + z.frames_x], axis=0)
-            out_ref[i * z.n_rows + r] = block.astype(jnp.bfloat16)
-
-
-def fill_cols(z, moved_ref, sort_ref, place_ref, cols_ref):
+    last = z.tokens // LANES - 2
+    for step, out_ref in enumerate(out_refs):
+        r = lax.rem(band + step, z.n_rows)
+        low = jnp.where(r == 0, z.halo, 0)
+        high = jnp.where(r == z.n_rows - 1, z.lanes - z.halo, z.lanes)
+        inside = (lane >= low) & (lane < high)
+        held = []
+        for t in range(z.all_frames):
+            start = 2 * (t * z.n_rows + r) * z.band_cycles - z.halo
+            tile = jnp.clip(start >> 7, 0, last)
+            turn = (2 * LANES - (start - tile * LANES)) & (2 * LANES - 1)
+            value = tokens_ref[:, pl.ds(pl.multiple_of(tile * LANES, LANES), 2 * LANES)]
+            value = pltpu.roll(value.astype(jnp.float32), turn, 1)[:, :LANES]
+            held.append(jnp.where(inside, value, 0.0))
+        out_ref[...] = jnp.concatenate(held, axis=0).astype(jnp.bfloat16)
+
+
+def frames_kernel(z, *refs):
+    band_refs, out_refs = refs[: z.n_rows], refs[z.n_rows :]
+    time, band = lax.axis_index("tm"), lax.axis_index("rows")
+    own, later = z.frames * z.feat, 2 * z.feat
+    for step, out_ref in enumerate(out_refs):
+        i = time ^ step
+        after = jnp.minimum((i + 1) * z.frames, z.all_frames - 2) * z.feat
+        for back, ref in enumerate(band_refs):
+            r = lax.rem(band + z.n_rows - back, z.n_rows)
+            out_ref[r, :own] = ref[pl.ds(pl.multiple_of(i * own, own), own)]
+            value = ref[pl.ds(pl.multiple_of(after, later), later)]
+            out_ref[r, own:] = jnp.where(i < z.n_time - 1, value, jnp.zeros_like(value))
+
+
+def prepare_kernel(z, features_ref, sort_ref, place_ref, act_ref, slope_ref, sort_out, place_out, held_ref, sems):
+    cells = z.rows * z.width
+    frames = [slice(t * cells, (t + 1) * cells) for t in range(z.frames)]
+    loads = [
+        pltpu.make_async_copy(features_ref.at[here], held_ref.at[here], sems.at[2 + t])
+        for t, here in enumerate(frames)
+    ]
+    copies = [
+        pltpu.make_async_copy(sort_ref, sort_out, sems.at[0]),
+        pltpu.make_async_copy(place_ref, place_out, sems.at[1]),
+    ]
+    for copy in loads + copies:
+        copy.start()
+    for row in range(z.grid_rows):
+        if row % z.rows == 0:
+            loads[row // z.rows].wait()
+        here = slice(row * z.width, (row + 1) * z.width)
+        hidden = held_ref[here, :].astype(jnp.float32)
+        sig = 0.5 + 0.5 * jnp.tanh(0.5 * hidden)
+        act = hidden * sig
+        act_ref[row * LANES : row * LANES + z.width, :] = act.astype(jnp.bfloat16)
+        shape = (LANES - z.width, z.channels)
+        act_ref[row * LANES + z.width : (row + 1) * LANES, :] = jnp.zeros(shape, jnp.bfloat16)
+        slope_ref[here, :] = sig * (1.0 + hidden * (1.0 - sig))
+    for copy in copies:
+        copy.wait()
+
+
+def fill_cols(z, moved_refs, sort_ref, place_ref, cols_ref, held_ref):
     rows = z.n_rows * z.frames_x * z.feat
-    moved = [moved_ref[i * z.n_rows : (i + 1) * z.n_rows].reshape(rows, LANES) for i in range(z.n_time)]
+    time = lax.axis_index("tm")
+    for step, ref in enumerate(moved_refs):
+        start = pl.multiple_of((time ^ step) * LANES, LANES)
+        held_ref[:, pl.ds(start, LANES)] = ref[...].reshape(rows, LANES)
     ordered = jnp.dot(
-        sort_ref[...], jnp.concatenate(moved, axis=1), preferred_element_type=jnp.float32
+        sort_ref[...], held_ref[...], preferred_element_type=jnp.float32
     ).astype(jnp.bfloat16)
     half = rows // 2
     pair = jnp.concatenate([ordered[:half], ordered[half:]], axis=1)
@@ -121,15 +162,11 @@
         cols_ref[TAPS * z.latent :, :] = jnp.zeros(shape, jnp.bfloat16)
 
 
-def weight_kernel(z, moved_ref, sort_ref, place_ref, features_ref, *refs):
-    own_ref, other_refs, (cols_ref, act_ref, total_ref) = refs[0], refs[1 : z.n_time], refs[z.n_time :]
-    for row in range(z.grid_rows):
-        hidden = features_ref[row * z.width : (row + 1) * z.width, :].astype(jnp.float32)
-        act = hidden * (0.5 + 0.5 * jnp.tanh(0.5 * hidden))
-        act_ref[row * LANES : row * LANES + z.width, :] = act.astype(jnp.bfloat16)
-        shape = (LANES - z.width, z.channels)
-        act_ref[row * LANES + z.width : (row + 1) * LANES, :] = jnp.zeros(shape, jnp.bfloat16)
-    fill_cols(z, moved_ref, sort_ref, place_ref, cols_ref)
+def weight_kernel(z, *refs):
+    moved_refs, (sort_ref, place_ref, act_ref) = refs[: z.n_time], refs[z.n_time : z.n_time + 3]
+    own_ref, other_refs = refs[z.n_time + 3], refs[z.n_time + 4 : -3]
+    cols_ref, held_ref, total_ref = refs[-3:]
+    fill_cols(z, moved_refs, sort_ref, place_ref, cols_ref, held_ref)
     total_ref[...] = jnp.dot(cols_ref[...], act_ref[...], preferred_element_type=jnp.float32)
     me = lax.axis_index("tm")
     for step in range(z.n_time):
@@ -141,8 +178,7 @@
             other_refs[step - 1][...] = value.astype(jnp.bfloat16)
 
 
-def features_kernel(z, moved_ref, sort_ref, place_ref, features_ref, weight_ref, out_ref, cols_ref):
-    fill_cols(z, moved_ref, sort_ref, place_ref, cols_ref)
+def features_kernel(z, cols_ref, slope_ref, weight_ref, out_ref):
     step = 4
     for first in range(0, z.grid_rows, step):
         count = min(step, z.grid_rows - first)
@@ -151,11 +187,9 @@
             part, weight_ref[...], (((0,), (0,)), ((), ())), preferred_element_type=jnp.float32
         )
         for k in range(count):
-            row = first + k
-            hidden = features_ref[row * z.width : (row + 1) * z.width, :].astype(jnp.float32)
-            sig = 0.5 + 0.5 * jnp.tanh(0.5 * hidden)
-            value = product[k * LANES : k * LANES + z.width] * sig * (1.0 + hidden * (1.0 - sig))
-            out_ref[row * z.width : (row + 1) * z.width, :] = value.astype(jnp.bfloat16)
+            here = slice((first + k) * z.width, (first + k + 1) * z.width)
+            value = product[k * LANES : k * LANES + z.width] * slope_ref[here, :]
+            out_ref[here, :] = value.astype(jnp.bfloat16)
 
 
 def join_kernel(z, *refs):
@@ -167,6 +201,10 @@
     out_ref[...] = held_ref[: TAPS * z.latent, :]
 
 
+def in_hbm(value):
+    return pltpu.with_memory_space_constraint(value, pltpu.HBM)
+
+
 def exchange(values, axis):
     size = lax.axis_size(axis)
     return [
@@ -175,9 +213,18 @@
     ]
 
 
-def tree_sum(values):
+def rotate(values, axis):
+    size = lax.axis_size(axis)
+    return [
+        lax.ppermute(value, axis, [(i, (i + step) % size) for i in range(size)])
+        for step, value in enumerate(values, 1)
+    ]
+
+
+def coset_sum(values):
     while len(values) > 1:
-        values = [values[i] + values[i + 1] for i in range(0, len(values), 2)]
+        half = len(values) // 2
+        values = [values[i] + values[i + half] for i in range(half)]
     return values[0]
 
 
@@ -186,48 +233,71 @@
     z = Sizes(n_time, n_rows, latent_grad.shape, features.shape)
     params = pltpu.CompilerParams(vmem_limit_bytes=32 * 1024 * 1024)
     f32, bf16 = jnp.float32, jnp.bfloat16
+    hbm, vmem = pl.BlockSpec(memory_space=pltpu.HBM), pl.BlockSpec(memory_space=pltpu.VMEM)
     cells = z.grid_rows * z.width
-    packed = pl.pallas_call(
-        functools.partial(pack_kernel, z),
-        out_shape=jax.ShapeDtypeStruct((z.sources, z.frames_x * z.feat, LANES), bf16),
-        compiler_params=params,
-        name="pack_latents",
-    )(latent_grad.T)
-    moved = lax.all_to_all(packed, ("tm", "rows"), 0, 0, tiled=True)
+    elements = cells * z.channels
+    products = z.cols * z.grid_rows * LANES * z.channels
+    flat = features.reshape(cells, z.channels)
+    windows = pl.pallas_call(
+        functools.partial(window_kernel, z),
+        out_shape=[jax.ShapeDtypeStruct((z.all_frames * z.feat, LANES), bf16)] * n_rows,
+        in_specs=[hbm],
+        scratch_shapes=[pltpu.VMEM((z.feat, z.tokens), bf16), pltpu.SemaphoreType.DMA],
+        compiler_params=params,
+        name="band_windows",
+    )(in_hbm(latent_grad.T))
+    bands = [windows[0]] + rotate(windows[1:], "rows")
     sort, place = sort_rows(z), place_lanes(z)
-    flat = features.reshape(cells, z.channels)
-    cols_scratch = pltpu.VMEM((z.cols, z.grid_rows * LANES), bf16)
-    products = z.cols * z.grid_rows * LANES * z.channels
+    act, slope, sort, place = pl.pallas_call(
+        functools.partial(prepare_kernel, z),
+        out_shape=[
+            jax.ShapeDtypeStruct((z.grid_rows * LANES, z.channels), bf16),
+            jax.ShapeDtypeStruct((cells, z.channels), f32),
+            jax.ShapeDtypeStruct(sort.shape, bf16),
+            jax.ShapeDtypeStruct(place.shape, bf16),
+        ],
+        in_specs=[hbm] * 3,
+        out_specs=[vmem] * 4,
+        scratch_shapes=[pltpu.VMEM((cells, z.channels), bf16), pltpu.SemaphoreType.DMA((2 + z.frames,))],
+        compiler_params=params,
+        cost_estimate=pl.CostEstimate(
+            flops=10 * elements, bytes_accessed=9 * elements, transcendentals=elements
+        ),
+        name="act_and_slope",
+    )(in_hbm(flat), in_hbm(sort), in_hbm(place))
+    parts = pl.pallas_call(
+        functools.partial(frames_kernel, z),
+        out_shape=[jax.ShapeDtypeStruct((n_rows, z.frames_x * z.feat, LANES), bf16)] * n_time,
+        compiler_params=params,
+        name="frame_windows",
+    )(*bands)
+    moved = [parts[0]] + exchange(parts[1:], "tm")
     pieces = pl.pallas_call(
         functools.partial(weight_kernel, z),
         out_shape=[
             jax.ShapeDtypeStruct((z.piece, z.channels), bf16 if s else f32) for s in range(n_time)
-        ],
+        ]
+        + [jax.ShapeDtypeStruct((z.cols, z.grid_rows * LANES), bf16)],
         scratch_shapes=[
-            cols_scratch,
-            pltpu.VMEM((z.grid_rows * LANES, z.channels), bf16),
+            pltpu.VMEM((n_rows * z.frames_x * z.feat, n_time * LANES), bf16),
             pltpu.VMEM((z.cols, z.channels), f32),
         ],
         compiler_params=params,
-        cost_estimate=pl.CostEstimate(
-            flops=2 * products, bytes_accessed=2 * cells * z.channels, transcendentals=cells * z.channels
-        ),
+        cost_estimate=pl.CostEstimate(flops=2 * products, bytes_accessed=4 * elements, transcendentals=0),
         name="weight_term",
-    )(moved, sort, place, flat)
+    )(*moved, sort, place, act)
+    *pieces, cols = pieces
     grad = pl.pallas_call(
         functools.partial(features_kernel, z),
         out_shape=jax.ShapeDtypeStruct((cells, z.channels), bf16),
-        scratch_shapes=[cols_scratch],
-        compiler_params=params,
-        cost_estimate=pl.CostEstimate(
-            flops=2 * products, bytes_accessed=4 * cells * z.channels, transcendentals=cells * z.channels
-        ),
+        compiler_params=params,
+        cost_estimate=pl.CostEstimate(flops=2 * products, bytes_accessed=8 * elements, transcendentals=0),
         name="features_grad",
-    )(moved, sort, place, flat, head_weight)
+    )(cols, slope, head_weight)
     arrived = exchange(pieces[1:], "tm")
-    mine = tree_sum([pieces[0]] + [value.astype(f32) for value in arrived]).astype(bf16)
-    arrived = exchange([mine] * (n_rows - 1), "rows")
-    whole = tree_sum([value.astype(f32) for value in [mine] + arrived])
+    mine = coset_sum([pieces[0]] + [value.astype(f32) for value in arrived]).astype(bf16)
+    arrived = rotate([mine] * (n_rows - 1), "rows")
+    whole = coset_sum([value.astype(f32) for value in [mine] + arrived])
     scale = 1.0 / math.sqrt(cells * n_time * n_rows)
     whole = (whole * scale).astype(bf16)
     arrived = exchange([whole] * (n_time - 1), "tm")

time: 51 us -> 46.7 us (0.916)
  blocking collectives: 18.7 us -> 0 us
  starting transfers between devices: 11.6 us -> 21.5 us
  waiting for transfers between devices: 6.79 us -> 14.3 us
  local copies, waits for them, and re-layouts: 4.85 us -> 0.01 us
  Pallas kernels: 8.08 us -> 9.96 us
    all_to_all x1 -> x0, blocking collectives: 18.7 us -> none  [shards(): moved = lax.all_to_all(packed, ('tm', 'rows'), 0, 0, tiled=True)]
    ppermute x0 -> x6, starting transfers between devices: none -> 10.8 us  [rotate(): lax.ppermute(value, axis, [(i, (i + step) % size) for i in range(size)])]
    ppermute x0 -> x6, waiting for transfers between devices: none -> 8.25 us  [rotate(): lax.ppermute(value, axis, [(i, (i + step) % size) for i in range(size)])]
    unnamed x10 -> x2, local copies, waits for them, and re-layouts: 4.85 us -> 0.01 us
    pallas_call x1 -> x3, Pallas kernels: 0.13 us -> 3.6 us  [the longest x1 2.45 us: shards(): pl.pallas_call(functools.partial(prepare_kernel, z), out_shape=[jax.Shape...]
    pallas_call x1, Pallas kernels: 4.53 us -> 3.08 us  [shards(): pl.pallas_call(functools.partial(features_kernel, z), out_shape=jax.Shape...]
    ppermute x9, starting transfers between devices: 11.6 us -> 10.7 us  [exchange(): lax.ppermute(value, axis, [(i, i ^ step) for i in range(size)])]
    ppermute x9, waiting for transfers between devices: 6.79 us -> 6.02 us  [exchange(): lax.ppermute(value, axis, [(i, i ^ step) for i in range(size)])]
  transfers between devices with their start and end apart: 9 -> 15, of which waited for: 5 -> 10; matrix products, arithmetic and copies ran while one was open for 0% -> 0% of each run, Pallas kernels for 9% -> 12%
where the time goes in v2:
time: 46.7 us; the launch traced here: 46.5 us
  starting transfers between devices  21.5 us (46%)
  waiting for transfers between devices  14.3 us (31%)
  Pallas kernels  9.96 us (21%)
  between operations  0.69 us (1%)
    ppermute x6, starting transfers between devices, rotate(): lax.ppermute(value, axis, [(i, (i + step) % size) for i in range(size)])  10.8 us
    ppermute x9, starting transfers between devices, exchange(): lax.ppermute(value, axis, [(i, i ^ step) for i in range(size)])  10.7 us
    ppermute x6, waiting for transfers between devices, rotate(): lax.ppermute(value, axis, [(i, (i + step) % size) for i in range(size)])  8.25 us
    ppermute x9, waiting for transfers between devices, exchange(): lax.ppermute(value, axis, [(i, i ^ step) for i in range(size)])  6.02 us
    pallas_call x1, Pallas kernels, shards(): pl.pallas_call(functools.partial(features_kernel, z), out_shape=jax.Shape...  3.08 us
    pallas_call x1, Pallas kernels, shards(): pl.pallas_call(functools.partial(prepare_kernel, z), out_shape=[jax.Shape...  2.45 us
    pallas_call x1, Pallas kernels, shards(): pl.pallas_call(functools.partial(weight_kernel, z), out_shape=[jax.ShapeD...  2.34 us
    pallas_call x1, Pallas kernels, shards(): pl.pallas_call(functools.partial(window_kernel, z), out_shape=[jax.ShapeD...  1.11 us
  transfers between devices with their start and end apart: 15, of which 10 were waited for; matrix products, arithmetic and copies ran while one was open for 0% of the time, Pallas kernels for 12%

profile of v2, /device:TPU:0, one launch (start us, length us, event | category | flops | bytes accessed | tf_op | source)
XLA Modules:
  0.0 46.5 jit_solution(3837978390311580864)
XLA Ops:
  0.6 1.1 %band_windows.1 = (bf16[128,128]{1,0:T(8,128)(2,1)S(1)}, bf16[128,128]{1,0:T(8,128)(2,1)S(1)}, bf16[128,128]{1,0:T(8,128)(2,1)S(1)}, bf16[128,128]{1,0:T(8,128)(2,1)S(1)}) custom-call(bf16[16,2304]{1,0:T(8,128)(2,1)} %bitcast.5), custom_call_target="tpu_custom_call" | custom-call | tf_op jit(solution)/shard_map/band_windows/pallas_call | solution.py:241
  1.7 3.1 %collective-permute-start = (bf16[128,128]{1,0:T(8,128)(2,1)S(1)}, bf16[128,128]{1,0:T(8,128)(2,1)S(1)}, u32[]{:S(2)}, u32[]{:S(2)}) collective-permute-start(bf16[128,128]{1,0:T(8,128)(2,1)S(1)} %get-tuple-element.20), channel_id=1, source_target_pairs={{0,2},{2,4},{4,6},{6,0},{1,3},{3,5},{5,7},{7,1},{8,10},{10,12},{12... | collective-permute-start | bytes 98312 | tf_op jit(solution)/shard_map/ppermute | solution.py:219
  4.8 2.6 %collective-permute-start.1 = (bf16[128,128]{1,0:T(8,128)(2,1)S(1)}, bf16[128,128]{1,0:T(8,128)(2,1)S(1)}, u32[]{:S(2)}, u32[]{:S(2)}) collective-permute-start(bf16[128,128]{1,0:T(8,128)(2,1)S(1)} %get-tuple-element.21), channel_id=1, source_target_pairs={{0,4},{2,6},{4,0},{6,2},{1,5},{3,7},{5,1},{7,3},{8,12},{10,14},{12... | collective-permute-start | bytes 98312 | tf_op jit(solution)/shard_map/ppermute | solution.py:219
  7.4 1.3 %collective-permute-start.2 = (bf16[128,128]{1,0:T(8,128)(2,1)S(1)}, bf16[128,128]{1,0:T(8,128)(2,1)S(1)}, u32[]{:S(2)}, u32[]{:S(2)}) collective-permute-start(bf16[128,128]{1,0:T(8,128)(2,1)S(1)} %get-tuple-element.22), channel_id=1, source_target_pairs={{0,6},{2,0},{4,2},{6,4},{1,7},{3,1},{5,3},{7,5},{8,14},{10,8},{12,... | collective-permute-start | bytes 98312 | tf_op jit(solution)/shard_map/ppermute | solution.py:219
  8.8 0.0 collective-permute-done.refs_1_
  8.8 1.2 %collective-permute-done.1.refs_2_ = bf16[128,128]{1,0:T(8,128)(2,1)S(1)} collective-permute-done((bf16[128,128]{1,0:T(8,128)(2,1)S(1)}, bf16[128,128]{1,0:T(8,128)(2,1)S(1)}, u32[]{:S(2)}, u32[]{:S(2)}) %collective-permute-start.1) | collective-permute-done | bytes 32800 | tf_op jit(solution)/shard_map/ppermute | solution.py:219
  10.0 1.3 %collective-permute-done.2.refs_3_ = bf16[128,128]{1,0:T(8,128)(2,1)S(1)} collective-permute-done((bf16[128,128]{1,0:T(8,128)(2,1)S(1)}, bf16[128,128]{1,0:T(8,128)(2,1)S(1)}, u32[]{:S(2)}, u32[]{:S(2)}) %collective-permute-start.2) | collective-permute-done | bytes 32800 | tf_op jit(solution)/shard_map/ppermute | solution.py:219
  11.4 1.6 %collective-permute-start.3 = (bf16[4,64,128]{2,1,0:T(8,128)(2,1)S(1)}, bf16[4,64,128]{2,1,0:T(8,128)(2,1)S(1)}, u32[]{:S(2)}, u32[]{:S(2)}) collective-permute-start(bf16[4,64,128]{2,1,0:T(8,128)(2,1)S(1)} %get-tuple-element.24), channel_id=1, source_target_pairs={{0,8},{8,0},{16,24},{24,16},{1,9},{9,1},{17,25},{25,17},{2,10},{10... | collective-permute-start | bytes 196616 | tf_op jit(solution)/shard_map/ppermute | solution.py:211
  12.9 1.5 %collective-permute-start.4 = (bf16[4,64,128]{2,1,0:T(8,128)(2,1)S(1)}, bf16[4,64,128]{2,1,0:T(8,128)(2,1)S(1)}, u32[]{:S(2)}, u32[]{:S(2)}) collective-permute-start(bf16[4,64,128]{2,1,0:T(8,128)(2,1)S(1)} %get-tuple-element.25), channel_id=1, source_target_pairs={{0,16},{8,24},{16,0},{24,8},{1,17},{9,25},{17,1},{25,9},{2,18},{10... | collective-permute-start | bytes 196616 | tf_op jit(solution)/shard_map/ppermute | solution.py:211
  14.4 0.5 %collective-permute-start.5 = (bf16[4,64,128]{2,1,0:T(8,128)(2,1)S(1)}, bf16[4,64,128]{2,1,0:T(8,128)(2,1)S(1)}, u32[]{:S(2)}, u32[]{:S(2)}) collective-permute-start(bf16[4,64,128]{2,1,0:T(8,128)(2,1)S(1)} %get-tuple-element.26), channel_id=1, source_target_pairs={{0,24},{8,16},{16,8},{24,0},{1,25},{9,17},{17,9},{25,1},{2,26},{10... | collective-permute-start | bytes 196616 | tf_op jit(solution)/shard_map/ppermute | solution.py:211
  14.9 2.5 %act_and_slope.1 = (bf16[3072,384]{1,0:T(8,128)(2,1)S(1)}, f32[2304,384]{1,0:T(8,128)S(1)}, bf16[256,256]{1,0:T(8,128)(2,1)S(1)}, bf16[1024,1024]{1,0:T(8,128)(2,1)S(1)}) custom-call(bf16[2304,384]{1,0:T(8,128)(2,1)} %bitcast.3, bf16[256,256]{1,0:T(8,128)(2,1)} %constant.6.clone.sort_ref, bf16[1024,1024]{1,0:T(8,128)(2,1)} %constant.7.clone.place_ref), custom_call_target="tpu_custom_call" | custom-call | flops 8847360 | bytes 7962624 | tf_op jit(solution)/shard_map/act_and_slope/pallas_call | solution.py:251
  17.4 0.0 collective-permute-done.3.refs_1_
  17.4 0.3 collective-permute-done.4.refs_2_
  17.7 1.9 %collective-permute-done.5.refs_3_ = bf16[4,64,128]{2,1,0:T(8,128)(2,1)S(1)} collective-permute-done((bf16[4,64,128]{2,1,0:T(8,128)(2,1)S(1)}, bf16[4,64,128]{2,1,0:T(8,128)(2,1)S(1)}, u32[]{:S(2)}, u32[]{:S(2)}) %collective-permute-start.5) | collective-permute-done | bytes 65568 | tf_op jit(solution)/shard_map/ppermute | solution.py:211
  19.6 0.0 copy-start
  19.6 2.3 %weight_term.1 = (f32[112,384]{1,0:T(8,128)S(1)}, bf16[112,384]{1,0:T(8,128)(2,1)S(1)}, bf16[112,384]{1,0:T(8,128)(2,1)S(1)}, bf16[112,384]{1,0:T(8,128)(2,1)S(1)}, bf16[448,3072]{1,0:T(8,128)(2,1)S(1)}) custom-call(bf16[4,64,128]{2,1,0:T(8,128)(2,1)S(1)} %get-tuple-element.23.refs_0_, bf16[4,64,128]{2,1,0:T(8,128)(2,1)S(1)} %collective-permute-done.3.refs_1_, ...), custom_call_target="tpu_custom_call" | custom-call | flops 1056964608 | bytes 3538944 | tf_op jit(solution)/shard_map/weight_term/pallas_call | solution.py:275
  22.0 0.6 %collective-permute-start.6 = (bf16[112,384]{1,0:T(8,128)(2,1)S(1)}, bf16[112,384]{1,0:T(8,128)(2,1)S(1)}, u32[]{:S(2)}, u32[]{:S(2)}) collective-permute-start(bf16[112,384]{1,0:T(8,128)(2,1)S(1)} %get-tuple-element.33), channel_id=1, source_target_pairs={{0,16},{8,24},{16,0},{24,8},{1,17},{9,25},{17,1},{25,9},{2,18},{10... | collective-permute-start | bytes 258056 | tf_op jit(solution)/shard_map/ppermute | solution.py:211
  22.5 0.5 %collective-permute-start.7 = (bf16[112,384]{1,0:T(8,128)(2,1)S(1)}, bf16[112,384]{1,0:T(8,128)(2,1)S(1)}, u32[]{:S(2)}, u32[]{:S(2)}) collective-permute-start(bf16[112,384]{1,0:T(8,128)(2,1)S(1)} %get-tuple-element.34), channel_id=1, source_target_pairs={{0,8},{8,0},{16,24},{24,16},{1,9},{9,1},{17,25},{25,17},{2,10},{10... | collective-permute-start | bytes 258056 | tf_op jit(solution)/shard_map/ppermute | solution.py:211
  23.1 2.4 %collective-permute-start.8 = (bf16[112,384]{1,0:T(8,128)(2,1)S(1)}, bf16[112,384]{1,0:T(8,128)(2,1)S(1)}, u32[]{:S(2)}, u32[]{:S(2)}) collective-permute-start(bf16[112,384]{1,0:T(8,128)(2,1)S(1)} %get-tuple-element.35), channel_id=1, source_target_pairs={{0,24},{8,16},{16,8},{24,0},{1,25},{9,17},{17,9},{25,1},{2,26},{10... | collective-permute-start | bytes 258056 | tf_op jit(solution)/shard_map/ppermute | solution.py:211
  25.5 1.0 %collective-permute-done.6 = bf16[112,384]{1,0:T(8,128)(2,1)S(1)} collective-permute-done((bf16[112,384]{1,0:T(8,128)(2,1)S(1)}, bf16[112,384]{1,0:T(8,128)(2,1)S(1)}, u32[]{:S(2)}, u32[]{:S(2)}) %collective-permute-start.6) | collective-permute-done | bytes 86048 | tf_op jit(solution)/shard_map/ppermute | solution.py:211
  26.5 0.5 %collective-permute-done.7 = bf16[112,384]{1,0:T(8,128)(2,1)S(1)} collective-permute-done((bf16[112,384]{1,0:T(8,128)(2,1)S(1)}, bf16[112,384]{1,0:T(8,128)(2,1)S(1)}, u32[]{:S(2)}, u32[]{:S(2)}) %collective-permute-start.7) | collective-permute-done | bytes 86048 | tf_op jit(solution)/shard_map/ppermute | solution.py:211
  27.0 1.9 %collective-permute-done.8 = bf16[112,384]{1,0:T(8,128)(2,1)S(1)} collective-permute-done((bf16[112,384]{1,0:T(8,128)(2,1)S(1)}, bf16[112,384]{1,0:T(8,128)(2,1)S(1)}, u32[]{:S(2)}, u32[]{:S(2)}) %collective-permute-start.8) | collective-permute-done | bytes 86048 | tf_op jit(solution)/shard_map/ppermute | solution.py:211
  28.9 0.1 add_convert_fusion
  29.0 3.2 %collective-permute-start.11 = (bf16[112,384]{1,0:T(8,128)(2,1)S(1)}, bf16[112,384]{1,0:T(8,128)(2,1)S(1)}, u32[]{:S(2)}, u32[]{:S(2)}) collective-permute-start(bf16[112,384]{1,0:T(8,128)(2,1)S(1)} %add_convert_fusion), channel_id=1, source_target_pairs={{0,6},{2,0},{4,2},{6,4},{1,7},{3,1},{5,3},{7,5},{8,14},{10,8},{12,... | collective-permute-start | bytes 258056 | tf_op jit(solution)/shard_map/ppermute | solution.py:219
  32.2 0.0 collective-permute-start.10
  32.2 0.6 %collective-permute-start.9 = (bf16[112,384]{1,0:T(8,128)(2,1)S(1)}, bf16[112,384]{1,0:T(8,128)(2,1)S(1)}, u32[]{:S(2)}, u32[]{:S(2)}) collective-permute-start(bf16[112,384]{1,0:T(8,128)(2,1)S(1)} %add_convert_fusion), channel_id=1, source_target_pairs={{0,4},{2,6},{4,0},{6,2},{1,5},{3,7},{5,1},{7,3},{8,12},{10,14},{12... | collective-permute-start | bytes 258056 | tf_op jit(solution)/shard_map/ppermute | solution.py:219
  32.8 1.5 %collective-permute-done.11 = bf16[112,384]{1,0:T(8,128)(2,1)S(1)} collective-permute-done((bf16[112,384]{1,0:T(8,128)(2,1)S(1)}, bf16[112,384]{1,0:T(8,128)(2,1)S(1)}, u32[]{:S(2)}, u32[]{:S(2)}) %collective-permute-start.11) | collective-permute-done | bytes 86048 | tf_op jit(solution)/shard_map/ppermute | solution.py:219
  34.3 4.2 %collective-permute-done.10 = bf16[112,384]{1,0:T(8,128)(2,1)S(1)} collective-permute-done((bf16[112,384]{1,0:T(8,128)(2,1)S(1)}, bf16[112,384]{1,0:T(8,128)(2,1)S(1)}, u32[]{:S(2)}, u32[]{:S(2)}) %collective-permute-start.10) | collective-permute-done | bytes 86048 | tf_op jit(solution)/shard_map/ppermute | solution.py:219
  38.5 0.0 collective-permute-done.9
  38.5 0.1 multiply_convert_fusion.refs_0_
  38.5 2.1 %collective-permute-start.14 = (bf16[112,384]{1,0:T(8,128)(2,1)S(1)}, bf16[112,384]{1,0:T(8,128)(2,1)S(1)}, u32[]{:S(2)}, u32[]{:S(2)}) collective-permute-start(bf16[112,384]{1,0:T(8,128)(2,1)S(1)} %multiply_convert_fusion.refs_0_), channel_id=1, source_target_pairs={{0,24},{8,16},{16,8},{24,0},{1,25},{9,17},{17,9},{25,1},{2,26},{10... | collective-permute-start | bytes 258056 | tf_op jit(solution)/shard_map/ppermute | solution.py:211
  40.6 0.5 %collective-permute-start.13 = (bf16[112,384]{1,0:T(8,128)(2,1)S(1)}, bf16[112,384]{1,0:T(8,128)(2,1)S(1)}, u32[]{:S(2)}, u32[]{:S(2)}) collective-permute-start(bf16[112,384]{1,0:T(8,128)(2,1)S(1)} %multiply_convert_fusion.refs_0_), channel_id=1, source_target_pairs={{0,16},{8,24},{16,0},{24,8},{1,17},{9,25},{17,1},{25,9},{2,18},{10... | collective-permute-start | bytes 258056 | tf_op jit(solution)/shard_map/ppermute | solution.py:211
  41.1 1.0 %collective-permute-start.12 = (bf16[112,384]{1,0:T(8,128)(2,1)S(1)}, bf16[112,384]{1,0:T(8,128)(2,1)S(1)}, u32[]{:S(2)}, u32[]{:S(2)}) collective-permute-start(bf16[112,384]{1,0:T(8,128)(2,1)S(1)} %multiply_convert_fusion.refs_0_), channel_id=1, source_target_pairs={{0,8},{8,0},{16,24},{24,16},{1,9},{9,1},{17,25},{25,17},{2,10},{10... | collective-permute-start | bytes 258056 | tf_op jit(solution)/shard_map/ppermute | solution.py:211
  42.1 0.0 copy-done
  42.1 3.1 %features_grad.1 = bf16[2304,384]{1,0:T(8,128)(2,1)} custom-call(bf16[448,3072]{1,0:T(8,128)(2,1)S(1)} %get-tuple-element.30.cols_ref, f32[2304,384]{1,0:T(8,128)S(1)} %get-tuple-element.31.slope_ref, bf16[432,384]{1,0:T(8,128)(2,1)S(1)} %copy-done), custom_call_target="tpu_custom_call" | custom-call | flops 1056964608 | bytes 7077888 | tf_op jit(solution)/shard_map/features_grad/pallas_call | solution.py:290
  45.2 0.0 collective-permute-done.14.refs_3_
  45.2 0.0 collective-permute-done.13.refs_2_
  45.2 0.4 collective-permute-done.12.refs_1_
  45.6 0.9 %join_pieces.1 = f32[432,384]{1,0:T(8,128)} custom-call(bf16[112,384]{1,0:T(8,128)(2,1)S(1)} %multiply_convert_fusion.refs_0_, bf16[112,384]{1,0:T(8,128)(2,1)S(1)} %collective-permute-done.12.refs_1_, bf16[112,384]{1,0:T(8,128)(2,1)S(1)} %collective-permute-done.13.refs_2_, bf16[112,384]{1,0:T(8,128)(2,1)S(1)} %collective-permute-done.14.refs_3_), custom_call_target="tpu_custom_call" | custom-call | tf_op jit(solution)/shard_map/join_pieces/pallas_call | solution.py:304
  (1 shorter events, 0.0 us)
Async XLA Ops:
  1.7 7.0 %collective-permute-start = (bf16[128,128]{1,0:T(8,128)(2,1)S(1)}, bf16[128,128]{1,0:T(8,128)(2,1)S(1)}, u32[]{:S(2)}, u32[]{:S(2)}) collective-permute-start(bf16[128,128]{1,0:T(8,128)(2,1)S(1)} %get-tuple-element.20), channel_id=1, source_target_pairs={{0,2},{2,4},{4,6},{6,0},{1,3},{3,5},{5,7},{7,1},{8,10},{10,12},{12... | collective-permute-start | bytes 98312 | tf_op jit(solution)/shard_map/ppermute | solution.py:219
  4.8 5.2 %collective-permute-start.1 = (bf16[128,128]{1,0:T(8,128)(2,1)S(1)}, bf16[128,128]{1,0:T(8,128)(2,1)S(1)}, u32[]{:S(2)}, u32[]{:S(2)}) collective-permute-start(bf16[128,128]{1,0:T(8,128)(2,1)S(1)} %get-tuple-element.21), channel_id=1, source_target_pairs={{0,4},{2,6},{4,0},{6,2},{1,5},{3,7},{5,1},{7,3},{8,12},{10,14},{12... | collective-permute-start | bytes 98312 | tf_op jit(solution)/shard_map/ppermute | solution.py:219
  7.4 3.9 %collective-permute-start.2 = (bf16[128,128]{1,0:T(8,128)(2,1)S(1)}, bf16[128,128]{1,0:T(8,128)(2,1)S(1)}, u32[]{:S(2)}, u32[]{:S(2)}) collective-permute-start(bf16[128,128]{1,0:T(8,128)(2,1)S(1)} %get-tuple-element.22), channel_id=1, source_target_pairs={{0,6},{2,0},{4,2},{6,4},{1,7},{3,1},{5,3},{7,5},{8,14},{10,8},{12,... | collective-permute-start | bytes 98312 | tf_op jit(solution)/shard_map/ppermute | solution.py:219
  11.4 6.0 %collective-permute-start.3 = (bf16[4,64,128]{2,1,0:T(8,128)(2,1)S(1)}, bf16[4,64,128]{2,1,0:T(8,128)(2,1)S(1)}, u32[]{:S(2)}, u32[]{:S(2)}) collective-permute-start(bf16[4,64,128]{2,1,0:T(8,128)(2,1)S(1)} %get-tuple-element.24), channel_id=1, source_target_pairs={{0,8},{8,0},{16,24},{24,16},{1,9},{9,1},{17,25},{25,17},{2,10},{10... | collective-permute-start | bytes 196616 | tf_op jit(solution)/shard_map/ppermute | solution.py:211
  12.9 4.8 %collective-permute-start.4 = (bf16[4,64,128]{2,1,0:T(8,128)(2,1)S(1)}, bf16[4,64,128]{2,1,0:T(8,128)(2,1)S(1)}, u32[]{:S(2)}, u32[]{:S(2)}) collective-permute-start(bf16[4,64,128]{2,1,0:T(8,128)(2,1)S(1)} %get-tuple-element.25), channel_id=1, source_target_pairs={{0,16},{8,24},{16,0},{24,8},{1,17},{9,25},{17,1},{25,9},{2,18},{10... | collective-permute-start | bytes 196616 | tf_op jit(solution)/shard_map/ppermute | solution.py:211
  14.4 5.2 %collective-permute-start.5 = (bf16[4,64,128]{2,1,0:T(8,128)(2,1)S(1)}, bf16[4,64,128]{2,1,0:T(8,128)(2,1)S(1)}, u32[]{:S(2)}, u32[]{:S(2)}) collective-permute-start(bf16[4,64,128]{2,1,0:T(8,128)(2,1)S(1)} %get-tuple-element.26), channel_id=1, source_target_pairs={{0,24},{8,16},{16,8},{24,0},{1,25},{9,17},{17,9},{25,1},{2,26},{10... | collective-permute-start | bytes 196616 | tf_op jit(solution)/shard_map/ppermute | solution.py:211
  19.6 22.5 %copy-start = (bf16[432,384]{1,0:T(8,128)(2,1)S(1)}, bf16[432,384]{1,0:T(8,128)(2,1)}, u32[]{:S(2)}) copy-start(bf16[432,384]{1,0:T(8,128)(2,1)} %weight_ref.1) | copy-start | bytes 995332
  22.0 4.6 %collective-permute-start.6 = (bf16[112,384]{1,0:T(8,128)(2,1)S(1)}, bf16[112,384]{1,0:T(8,128)(2,1)S(1)}, u32[]{:S(2)}, u32[]{:S(2)}) collective-permute-start(bf16[112,384]{1,0:T(8,128)(2,1)S(1)} %get-tuple-element.33), channel_id=1, source_target_pairs={{0,16},{8,24},{16,0},{24,8},{1,17},{9,25},{17,1},{25,9},{2,18},{10... | collective-permute-start | bytes 258056 | tf_op jit(solution)/shard_map/ppermute | solution.py:211
  22.5 4.5 %collective-permute-start.7 = (bf16[112,384]{1,0:T(8,128)(2,1)S(1)}, bf16[112,384]{1,0:T(8,128)(2,1)S(1)}, u32[]{:S(2)}, u32[]{:S(2)}) collective-permute-start(bf16[112,384]{1,0:T(8,128)(2,1)S(1)} %get-tuple-element.34), channel_id=1, source_target_pairs={{0,8},{8,0},{16,24},{24,16},{1,9},{9,1},{17,25},{25,17},{2,10},{10... | collective-permute-start | bytes 258056 | tf_op jit(solution)/shard_map/ppermute | solution.py:211
  23.1 5.8 %collective-permute-start.8 = (bf16[112,384]{1,0:T(8,128)(2,1)S(1)}, bf16[112,384]{1,0:T(8,128)(2,1)S(1)}, u32[]{:S(2)}, u32[]{:S(2)}) collective-permute-start(bf16[112,384]{1,0:T(8,128)(2,1)S(1)} %get-tuple-element.35), channel_id=1, source_target_pairs={{0,24},{8,16},{16,8},{24,0},{1,25},{9,17},{17,9},{25,1},{2,26},{10... | collective-permute-start | bytes 258056 | tf_op jit(solution)/shard_map/ppermute | solution.py:211
  29.0 5.3 %collective-permute-start.11 = (bf16[112,384]{1,0:T(8,128)(2,1)S(1)}, bf16[112,384]{1,0:T(8,128)(2,1)S(1)}, u32[]{:S(2)}, u32[]{:S(2)}) collective-permute-start(bf16[112,384]{1,0:T(8,128)(2,1)S(1)} %add_convert_fusion), channel_id=1, source_target_pairs={{0,6},{2,0},{4,2},{6,4},{1,7},{3,1},{5,3},{7,5},{8,14},{10,8},{12,... | collective-permute-start | bytes 258056 | tf_op jit(solution)/shard_map/ppermute | solution.py:219
  32.2 6.3 %collective-permute-start.10 = (bf16[112,384]{1,0:T(8,128)(2,1)S(1)}, bf16[112,384]{1,0:T(8,128)(2,1)S(1)}, u32[]{:S(2)}, u32[]{:S(2)}) collective-permute-start(bf16[112,384]{1,0:T(8,128)(2,1)S(1)} %add_convert_fusion), channel_id=1, source_target_pairs={{0,2},{2,4},{4,6},{6,0},{1,3},{3,5},{5,7},{7,1},{8,10},{10,12},{12... | collective-permute-start | bytes 258056 | tf_op jit(solution)/shard_map/ppermute | solution.py:219
  32.2 6.3 %collective-permute-start.9 = (bf16[112,384]{1,0:T(8,128)(2,1)S(1)}, bf16[112,384]{1,0:T(8,128)(2,1)S(1)}, u32[]{:S(2)}, u32[]{:S(2)}) collective-permute-start(bf16[112,384]{1,0:T(8,128)(2,1)S(1)} %add_convert_fusion), channel_id=1, source_target_pairs={{0,4},{2,6},{4,0},{6,2},{1,5},{3,7},{5,1},{7,3},{8,12},{10,14},{12... | collective-permute-start | bytes 258056 | tf_op jit(solution)/shard_map/ppermute | solution.py:219
  38.5 6.6 %collective-permute-start.14 = (bf16[112,384]{1,0:T(8,128)(2,1)S(1)}, bf16[112,384]{1,0:T(8,128)(2,1)S(1)}, u32[]{:S(2)}, u32[]{:S(2)}) collective-permute-start(bf16[112,384]{1,0:T(8,128)(2,1)S(1)} %multiply_convert_fusion.refs_0_), channel_id=1, source_target_pairs={{0,24},{8,16},{16,8},{24,0},{1,25},{9,17},{17,9},{25,1},{2,26},{10... | collective-permute-start | bytes 258056 | tf_op jit(solution)/shard_map/ppermute | solution.py:211
  40.6 4.6 %collective-permute-start.13 = (bf16[112,384]{1,0:T(8,128)(2,1)S(1)}, bf16[112,384]{1,0:T(8,128)(2,1)S(1)}, u32[]{:S(2)}, u32[]{:S(2)}) collective-permute-start(bf16[112,384]{1,0:T(8,128)(2,1)S(1)} %multiply_convert_fusion.refs_0_), channel_id=1, source_target_pairs={{0,16},{8,24},{16,0},{24,8},{1,17},{9,25},{17,1},{25,9},{2,18},{10... | collective-permute-start | bytes 258056 | tf_op jit(solution)/shard_map/ppermute | solution.py:211
  41.1 4.5 %collective-permute-start.12 = (bf16[112,384]{1,0:T(8,128)(2,1)S(1)}, bf16[112,384]{1,0:T(8,128)(2,1)S(1)}, u32[]{:S(2)}, u32[]{:S(2)}) collective-permute-start(bf16[112,384]{1,0:T(8,128)(2,1)S(1)} %multiply_convert_fusion.refs_0_), channel_id=1, source_target_pairs={{0,8},{8,0},{16,24},{24,16},{1,9},{9,1},{17,25},{25,17},{2,10},{10... | collective-permute-start | bytes 258056 | tf_op jit(solution)/shard_map/ppermute | solution.py:211

commit v3 on v2

v3 whole, which is shorter than its diff:
```python
import functools
import math

import jax
import jax.numpy as jnp
import numpy as np
from jax import lax
from jax.experimental import pallas as pl
from jax.experimental.pallas import tpu as pltpu
from jax.sharding import PartitionSpec as P

LANES = 128
TAPS = 27


class Sizes:
    def __init__(self, n_time, n_rows, latent_shape, features_shape):
        self.n_time, self.n_rows = n_time, n_rows
        self.frames, self.rows, self.width, self.channels = features_shape
        self.tokens, self.feat = latent_shape
        self.latent = self.feat * n_rows // 4
        self.cycle = 2 * n_time
        self.row_tokens = self.width // 2
        self.band = self.rows // 2
        self.band_x = self.band + 2
        self.frames_x = self.frames + 2
        self.all_frames = self.frames * n_time
        self.band_cycles = self.band * self.row_tokens // self.cycle
        self.halo_cycles = -(-self.row_tokens // self.cycle)
        self.halo = 2 * self.halo_cycles
        self.lanes = 2 * self.band_cycles + 2 * self.halo
        self.sources = n_time * n_rows
        self.grid_rows = self.frames * self.rows
        self.piece_taps = -(-TAPS // n_time)
        self.piece = self.piece_taps * self.latent
        self.cols = self.piece * n_time


def sort_rows(z):
    count = z.n_rows * z.frames_x * z.feat
    out = np.zeros((count, count), np.float32)
    part = z.feat // 4
    for r in range(z.n_rows):
        for t in range(z.frames_x):
            for e in range(part):
                for p in range(2):
                    for q in range(2):
                        source = (r * z.frames_x + t) * z.feat + 4 * e + 2 * p + q
                        target = ((q * 2 + p) * z.frames_x + t) * z.latent + r * part + e
                        out[target, source] = 1
    return jnp.asarray(out, jnp.bfloat16)


def place_lanes(z):
    out = np.zeros((2, z.n_time, LANES, z.band_x, LANES), np.float32)
    for q in range(2):
        for i in range(z.n_time):
            for lane in range(z.lanes):
                place = z.cycle - 1 - i if lane % 2 else i
                token = (lane // 2 - z.halo_cycles) * z.cycle + place + z.row_tokens
                if 0 <= token < z.band_x * z.row_tokens:
                    out[q, i, lane, token // z.row_tokens, 2 * (token % z.row_tokens) + q] = 1
    return jnp.asarray(out.reshape(2 * z.n_time * LANES, z.band_x * LANES), jnp.bfloat16)


def window_kernel(z, *refs):
    token_refs, out_refs = refs[: z.n_time], refs[z.n_time :]
    time, band = lax.axis_index("tm"), lax.axis_index("rows")
    lane = lax.broadcasted_iota(jnp.int32, (z.feat, LANES), 1)
    last = z.tokens // LANES - 2
    for step, out_ref in enumerate(out_refs):
        r = band ^ step
        low = jnp.where(r == 0, z.halo, 0)
        high = jnp.where(r == z.n_rows - 1, z.lanes - z.halo, z.lanes)
        inside = (lane >= low) & (lane < high)
        blocks = [[] for _ in token_refs]
        for t in range(z.frames_x):
            frame = time * z.frames + t
            start = 2 * (frame * z.n_rows + r) * z.band_cycles - z.halo
            tile = jnp.clip(start >> 7, 0, last)
            turn = (2 * LANES - (start - tile * LANES)) & (2 * LANES - 1)
            kept = inside & (frame < z.all_frames)
            for ref, held in zip(token_refs, blocks):
                value = ref[:, pl.ds(pl.multiple_of(tile * LANES, LANES), 2 * LANES)]
                value = pltpu.roll(value.astype(jnp.float32), turn, 1)[:, :LANES]
                held.append(jnp.where(kept, value, 0.0))
        for i, held in enumerate(blocks):
            out_ref[time ^ i] = jnp.concatenate(held, axis=0).astype(jnp.bfloat16)


def prepare_kernel(
    z, features_ref, sort_ref, place_ref, tokens_ref, act_ref, slope_ref, sort_out, place_out, tokens_out, held_ref, sems
):
    cells = z.rows * z.width
    frames = [slice(t * cells, (t + 1) * cells) for t in range(z.frames)]
    loads = [
        pltpu.make_async_copy(features_ref.at[here], held_ref.at[here], sems.at[3 + t])
        for t, here in enumerate(frames)
    ]
    copies = [
        pltpu.make_async_copy(sort_ref, sort_out, sems.at[0]),
        pltpu.make_async_copy(place_ref, place_out, sems.at[1]),
        pltpu.make_async_copy(tokens_ref, tokens_out, sems.at[2]),
    ]
    for copy in loads + copies:
        copy.start()
    for row in range(z.grid_rows):
        if row % z.rows == 0:
            loads[row // z.rows].wait()
        here = slice(row * z.width, (row + 1) * z.width)
        hidden = held_ref[here, :].astype(jnp.float32)
        sig = 0.5 + 0.5 * jnp.tanh(0.5 * hidden)
        act = hidden * sig
        act_ref[row * LANES : row * LANES + z.width, :] = act.astype(jnp.bfloat16)
        shape = (LANES - z.width, z.channels)
        act_ref[row * LANES + z.width : (row + 1) * LANES, :] = jnp.zeros(shape, jnp.bfloat16)
        slope_ref[here, :] = sig * (1.0 + hidden * (1.0 - sig))
    for copy in copies:
        copy.wait()


def slot_start(z, piece):
    return pl.multiple_of((lax.axis_index("tm") ^ piece) * z.piece, z.piece)


def last_first(count):
    return [count - 1, *range(1, count - 1)]


def fill_cols(z, moved_refs, sort_ref, place_ref, cols_ref, held_ref):
    count = z.frames_x * z.feat
    rows = z.n_rows * count
    band = lax.axis_index("rows")
    for step, ref in zip([0] + last_first(z.n_rows), moved_refs):
        start = pl.multiple_of((band ^ step) * count, count)
        for i in range(z.n_time):
            held_ref[pl.ds(start, count), i * LANES : (i + 1) * LANES] = ref[i]
    ordered = jnp.dot(
        sort_ref[...], held_ref[...], preferred_element_type=jnp.float32
    ).astype(jnp.bfloat16)
    half = rows // 2
    pair = jnp.concatenate([ordered[:half], ordered[half:]], axis=1)
    grid = jnp.dot(pair, place_ref[...], preferred_element_type=jnp.float32)
    slots = [slot_start(z, piece) for piece in range(z.n_time)]

    def tap_rows(tap):
        start = slots[tap // z.piece_taps] + tap % z.piece_taps * z.latent
        return pl.ds(pl.multiple_of(start, z.latent), z.latent)

    for a in range(z.band_x):
        block = grid[:, a * LANES : (a + 1) * LANES]
        for kw in range(3):
            turned = block if kw == 1 else pltpu.roll(block, LANES - 1 if kw == 0 else 1, 1)
            turned = turned.astype(jnp.bfloat16)
            for p in range(2):
                for t in range(z.frames_x):
                    at = (p * z.frames_x + t) * z.latent
                    value = turned[at : at + z.latent]
                    for kt in range(3):
                        for kh in range(3):
                            frame, row = t - 2 + kt, 2 * (a - 1) + p - 1 + kh
                            if 0 <= frame < z.frames and 0 <= row < z.rows:
                                tap = (kt * 3 + kh) * 3 + kw
                                lane = (frame * z.rows + row) * LANES
                                cols_ref[tap_rows(tap), lane : lane + LANES] = value
    for tap in range(TAPS, z.n_time * z.piece_taps):
        cols_ref[tap_rows(tap), :] = jnp.zeros((z.latent, z.grid_rows * LANES), jnp.bfloat16)


def weight_kernel(z, *refs):
    moved_refs, (sort_ref, place_ref, act_ref) = refs[: z.n_rows], refs[z.n_rows : z.n_rows + 3]
    out_refs, cols_ref, held_ref = refs[z.n_rows + 3 : -2], refs[-2], refs[-1]
    fill_cols(z, moved_refs, sort_ref, place_ref, cols_ref, held_ref)
    total = jnp.dot(cols_ref[z.piece :, :], act_ref[...], preferred_element_type=jnp.float32)
    for step, ref in enumerate(out_refs):
        ref[...] = total[step * z.piece : (step + 1) * z.piece].astype(jnp.bfloat16)


def own_kernel(z, cols_ref, act_ref, out_ref):
    out_ref[...] = jnp.dot(cols_ref[: z.piece, :], act_ref[...], preferred_element_type=jnp.float32)


def features_kernel(z, cols_ref, slope_ref, weight_ref, out_ref, held_ref):
    for piece in range(z.n_time):
        first = piece * z.piece
        count = max(0, min(z.piece, TAPS * z.latent - first))
        start = slot_start(z, piece)
        if count:
            held_ref[pl.ds(start, count), :] = weight_ref[first : first + count, :]
        if count < z.piece:
            start = pl.multiple_of(start + count, z.latent)
            held_ref[pl.ds(start, z.piece - count), :] = jnp.zeros((z.piece - count, z.channels), jnp.bfloat16)
    step = 4
    for first in range(0, z.grid_rows, step):
        count = min(step, z.grid_rows - first)
        part = cols_ref[:, first * LANES : (first + count) * LANES]
        product = lax.dot_general(
            part, held_ref[...], (((0,), (0,)), ((), ())), preferred_element_type=jnp.float32
        )
        for k in range(count):
            here = slice((first + k) * z.width, (first + k + 1) * z.width)
            value = product[k * LANES : k * LANES + z.width] * slope_ref[here, :]
            out_ref[here, :] = value.astype(jnp.bfloat16)


def join_kernel(z, *refs):
    piece_refs, (out_ref, held_ref, sems) = refs[: z.n_time], refs[z.n_time :]
    me = lax.axis_index("tm")
    whole, tail = divmod(TAPS * z.latent, z.piece)

    def each(act):
        for step in range(z.n_time):
            place = me ^ step
            start = pl.multiple_of(place * z.piece, z.piece)

            def copy(count):
                source = held_ref.at[step, pl.ds(0, count)]
                act(pltpu.make_async_copy(source, out_ref.at[pl.ds(start, count)], sems.at[step]))

            pl.when(place < whole)(functools.partial(copy, z.piece))
            if tail:
                pl.when(place == whole)(functools.partial(copy, tail))

    for step, ref in enumerate(piece_refs):
        held_ref[step] = ref[...].astype(jnp.float32)
    each(lambda copy: copy.start())
    each(lambda copy: copy.wait())


def in_hbm(value):
    return pltpu.with_memory_space_constraint(value, pltpu.HBM)


def exchange(values, axis):
    size = lax.axis_size(axis)
    return [
        lax.ppermute(value, axis, [(i, i ^ step) for i in range(size)])
        for step, value in enumerate(values, 1)
    ]


def coset_sum(values):
    while len(values) > 1:
        half = len(values) // 2
        values = [values[i] + values[i + half] for i in range(half)]
    return values[0]


def shards(latent_grad, features, head_weight):
    n_time, n_rows = lax.axis_size("tm"), lax.axis_size("rows")
    z = Sizes(n_time, n_rows, latent_grad.shape, features.shape)
    params = pltpu.CompilerParams(vmem_limit_bytes=32 * 1024 * 1024)
    f32, bf16 = jnp.float32, jnp.bfloat16
    hbm, vmem = pl.BlockSpec(memory_space=pltpu.HBM), pl.BlockSpec(memory_space=pltpu.VMEM)
    cells = z.grid_rows * z.width
    elements = cells * z.channels
    products = z.cols * z.grid_rows * LANES * z.channels
    flat = features.reshape(cells, z.channels)
    tokens = latent_grad.T
    arrived = exchange([tokens] * (n_time - 1), "tm")
    sort, place = sort_rows(z), place_lanes(z)
    act, slope, sort, place, tokens = pl.pallas_call(
        functools.partial(prepare_kernel, z),
        out_shape=[
            jax.ShapeDtypeStruct((z.grid_rows * LANES, z.channels), bf16),
            jax.ShapeDtypeStruct((cells, z.channels), f32),
            jax.ShapeDtypeStruct(sort.shape, bf16),
            jax.ShapeDtypeStruct(place.shape, bf16),
            jax.ShapeDtypeStruct(tokens.shape, bf16),
        ],
        in_specs=[hbm] * 4,
        out_specs=[vmem] * 5,
        scratch_shapes=[pltpu.VMEM((cells, z.channels), bf16), pltpu.SemaphoreType.DMA((3 + z.frames,))],
        compiler_params=params,
        cost_estimate=pl.CostEstimate(
            flops=10 * elements, bytes_accessed=9 * elements, transcendentals=elements
        ),
        name="act_and_slope",
    )(in_hbm(flat), in_hbm(sort), in_hbm(place), in_hbm(tokens))
    windows = pl.pallas_call(
        functools.partial(window_kernel, z),
        out_shape=[jax.ShapeDtypeStruct((n_time, z.frames_x * z.feat, LANES), bf16)] * n_rows,
        compiler_params=params,
        name="latent_windows",
    )(tokens, *arrived)
    arrived = exchange(windows[1:], "rows")
    moved = [windows[0]] + [arrived[step - 1] for step in last_first(n_rows)]
    *pieces, cols = pl.pallas_call(
        functools.partial(weight_kernel, z),
        out_shape=[jax.ShapeDtypeStruct((z.piece, z.channels), bf16)] * (n_time - 1)
        + [jax.ShapeDtypeStruct((z.cols, z.grid_rows * LANES), bf16)],
        scratch_shapes=[pltpu.VMEM((n_rows * z.frames_x * z.feat, n_time * LANES), bf16)],
        compiler_params=params,
        cost_estimate=pl.CostEstimate(flops=2 * products, bytes_accessed=4 * elements, transcendentals=0),
        name="weight_term",
    )(*moved, sort, place, act)
    arrived = exchange(pieces, "tm")
    own = pl.pallas_call(
        functools.partial(own_kernel, z),
        out_shape=jax.ShapeDtypeStruct((z.piece, z.channels), f32),
        compiler_params=params,
        cost_estimate=pl.CostEstimate(
            flops=2 * products // n_time, bytes_accessed=2 * elements, transcendentals=0
        ),
        name="own_piece",
    )(cols, act)
    for step in last_first(n_time):
        own = own + arrived[step - 1].astype(f32)
    mine = own.astype(bf16)
    cols, mine = lax.optimization_barrier((cols, mine))
    grad = pl.pallas_call(
        functools.partial(features_kernel, z),
        out_shape=jax.ShapeDtypeStruct((cells, z.channels), bf16),
        scratch_shapes=[pltpu.VMEM((z.cols, z.channels), bf16)],
        compiler_params=params,
        cost_estimate=pl.CostEstimate(flops=2 * products, bytes_accessed=8 * elements, transcendentals=0),
        name="features_grad",
    )(cols, slope, head_weight)
    arrived = exchange([mine] * (n_rows - 1), "rows")
    whole = coset_sum([value.astype(f32) for value in [mine] + arrived])
    scale = 1.0 / math.sqrt(cells * n_time * n_rows)
    whole = (whole * scale).astype(bf16)
    whole, grad = lax.optimization_barrier((whole, grad))
    pieces = [whole] + exchange([whole] * (n_time - 1), "tm")
    weight_grad = pl.pallas_call(
        functools.partial(join_kernel, z),
        out_shape=jax.ShapeDtypeStruct((TAPS * z.latent, z.channels), f32),
        in_specs=[vmem] * n_time,
        out_specs=hbm,
        scratch_shapes=[
            pltpu.VMEM((n_time, z.piece, z.channels), f32),
            pltpu.SemaphoreType.DMA((n_time,)),
        ],
        compiler_params=params,
        name="join_pieces",
    )(*pieces)
    return (grad.reshape(features.shape), weight_grad)


def solution(mesh):
    return jax.shard_map(
        shards,
        mesh=mesh,
        in_specs=(P(("dp", "tm"), "rows"), P(("dp", "tm"), "rows", None, None), P()),
        out_specs=(P(("dp", "tm"), "rows", None, None), P("dp", None)),
        check_vma=False,
    )
```

time: 46.7 us -> 44.6 us (0.955)
  starting transfers between devices: 21.5 us -> 20.6 us
  waiting for transfers between devices: 14.3 us -> 13.6 us
  Pallas kernels: 9.96 us -> 9.36 us
    ppermute x6 -> x0, starting transfers between devices: 10.8 us -> none  [rotate(): lax.ppermute(value, axis, [(i, (i + step) % size) for i in range(size)])]
    ppermute x9 -> x15, starting transfers between devices: 10.7 us -> 20.6 us  [exchange(): lax.ppermute(value, axis, [(i, i ^ step) for i in range(size)])]
    ppermute x6 -> x0, waiting for transfers between devices: 8.25 us -> none  [rotate(): lax.ppermute(value, axis, [(i, (i + step) % size) for i in range(size)])]
    ppermute x9 -> x15, waiting for transfers between devices: 6.02 us -> 13.6 us  [exchange(): lax.ppermute(value, axis, [(i, i ^ step) for i in range(size)])]
    pallas_call x1, Pallas kernels: 1.11 us -> 0.22 us  [shards(): pl.pallas_call(functools.partial(window_kernel, z), out_shape=[jax.ShapeD...]
    pallas_call x1, Pallas kernels: 0.04 us -> 0.55 us  [shards(): pl.pallas_call(functools.partial(own_kernel, z), out_shape=jax.ShapeDtype...]
  transfers between devices with their start and end apart: 15 -> 15, of which waited for: 10 -> 12; matrix products, arithmetic and copies ran while one was open for 0% -> 0% of each run, Pallas kernels for 12% -> 14%
where the time goes in v3:
time: 44.6 us; the launch traced here: 44.4 us
  starting transfers between devices  20.6 us (46%)
  waiting for transfers between devices  13.6 us (30%)
  Pallas kernels  9.36 us (21%)
  between operations  0.68 us (2%)
    ppermute x15, starting transfers between devices, exchange(): lax.ppermute(value, axis, [(i, i ^ step) for i in range(size)])  20.6 us
    ppermute x15, waiting for transfers between devices, exchange(): lax.ppermute(value, axis, [(i, i ^ step) for i in range(size)])  13.6 us
    pallas_call x1, Pallas kernels, shards(): pl.pallas_call(functools.partial(features_kernel, z), out_shape=jax.Shape...  3.11 us
    pallas_call x1, Pallas kernels, shards(): pl.pallas_call(functools.partial(prepare_kernel, z), out_shape=[jax.Shape...  2.46 us
    pallas_call x1, Pallas kernels, shards(): pl.pallas_call(functools.partial(weight_kernel, z), out_shape=[jax.ShapeD...  2.11 us
    pallas_call x1, Pallas kernels, shards(): pl.pallas_call(functools.partial(join_kernel, z), out_shape=jax.ShapeDtyp...  0.91 us
  transfers between devices with their start and end apart: 15, of which 12 were waited for; matrix products, arithmetic and copies ran while one was open for 0% of the time, Pallas kernels for 14%

profile of v3, /device:TPU:0, one launch (start us, length us, event | category | flops | bytes accessed | tf_op | source)
XLA Modules:
  0.0 44.4 jit_solution(5075833405839732267)
XLA Ops:
  0.6 4.0 %collective-permute-start.2 = (bf16[16,2304]{1,0:T(8,128)(2,1)}, bf16[16,2304]{1,0:T(8,128)(2,1)S(1)}, u32[]{:S(2)}, u32[]{:S(2)}) collective-permute-start(bf16[16,2304]{1,0:T(8,128)(2,1)} %bitcast.5), channel_id=1, source_target_pairs={{0,24},{8,16},{16,8},{24,0},{1,25},{9,17},{17,9},{25,1},{2,26},{10... | collective-permute-start | bytes 221192 | tf_op jit(solution)/shard_map/ppermute | solution.py:237
  4.6 0.5 %collective-permute-start.1 = (bf16[16,2304]{1,0:T(8,128)(2,1)}, bf16[16,2304]{1,0:T(8,128)(2,1)S(1)}, u32[]{:S(2)}, u32[]{:S(2)}) collective-permute-start(bf16[16,2304]{1,0:T(8,128)(2,1)} %bitcast.6), channel_id=1, source_target_pairs={{0,16},{8,24},{16,0},{24,8},{1,17},{9,25},{17,1},{25,9},{2,18},{10... | collective-permute-start | bytes 221192 | tf_op jit(solution)/shard_map/ppermute | solution.py:237
  5.1 0.1 collective-permute-start
  5.2 2.5 %act_and_slope.1 = (bf16[3072,384]{1,0:T(8,128)(2,1)S(1)}, f32[2304,384]{1,0:T(8,128)S(1)}, bf16[256,256]{1,0:T(8,128)(2,1)S(1)}, bf16[1024,1024]{1,0:T(8,128)(2,1)S(1)}, bf16[16,2304]{1,0:T(8,128)(2,1)S(1)}) custom-call(bf16[2304,384]{1,0:T(8,128)(2,1)} %bitcast.3, bf16[256,256]{1,0:T(8,128)(2,1)} %constant.6.clone.sort_ref, ...), custom_call_target="tpu_custom_call" | custom-call | flops 8847360 | bytes 7962624 | tf_op jit(solution)/shard_map/act_and_slope/pallas_call | solution.py:262
  7.7 0.0 collective-permute-done.2.refs_3_
  7.7 1.4 %collective-permute-done.1.refs_2_ = bf16[16,2304]{1,0:T(8,128)(2,1)S(1)} collective-permute-done((bf16[16,2304]{1,0:T(8,128)(2,1)}, bf16[16,2304]{1,0:T(8,128)(2,1)S(1)}, u32[]{:S(2)}, u32[]{:S(2)}) %collective-permute-start.1) | collective-permute-done | bytes 73760 | tf_op jit(solution)/shard_map/ppermute | solution.py:237
  9.2 0.5 %collective-permute-done.refs_1_ = bf16[16,2304]{1,0:T(8,128)(2,1)S(1)} collective-permute-done((bf16[16,2304]{1,0:T(8,128)(2,1)}, bf16[16,2304]{1,0:T(8,128)(2,1)S(1)}, u32[]{:S(2)}, u32[]{:S(2)}) %collective-permute-start) | collective-permute-done | bytes 73760 | tf_op jit(solution)/shard_map/ppermute | solution.py:237
  9.7 0.2 latent_windows.1
  9.9 3.7 %collective-permute-start.3 = (bf16[4,64,128]{2,1,0:T(8,128)(2,1)S(1)}, bf16[4,64,128]{2,1,0:T(8,128)(2,1)S(1)}, u32[]{:S(2)}, u32[]{:S(2)}) collective-permute-start(bf16[4,64,128]{2,1,0:T(8,128)(2,1)S(1)} %get-tuple-element.21), channel_id=1, source_target_pairs={{0,6},{2,4},{4,2},{6,0},{1,7},{3,5},{5,3},{7,1},{8,14},{10,12},{12... | collective-permute-start | bytes 196616 | tf_op jit(solution)/shard_map/ppermute | solution.py:237
  13.5 0.0 collective-permute-start.4
  13.6 0.8 %collective-permute-start.5 = (bf16[4,64,128]{2,1,0:T(8,128)(2,1)S(1)}, bf16[4,64,128]{2,1,0:T(8,128)(2,1)S(1)}, u32[]{:S(2)}, u32[]{:S(2)}) collective-permute-start(bf16[4,64,128]{2,1,0:T(8,128)(2,1)S(1)} %get-tuple-element.23), channel_id=1, source_target_pairs={{0,4},{2,6},{4,0},{6,2},{1,5},{3,7},{5,1},{7,3},{8,12},{10,14},{12... | collective-permute-start | bytes 196616 | tf_op jit(solution)/shard_map/ppermute | solution.py:237
  14.3 1.8 %collective-permute-done.3.refs_1_ = bf16[4,64,128]{2,1,0:T(8,128)(2,1)S(1)} collective-permute-done((bf16[4,64,128]{2,1,0:T(8,128)(2,1)S(1)}, bf16[4,64,128]{2,1,0:T(8,128)(2,1)S(1)}, u32[]{:S(2)}, u32[]{:S(2)}) %collective-permute-start.3) | collective-permute-done | bytes 65568 | tf_op jit(solution)/shard_map/ppermute | solution.py:237
  16.1 1.7 %collective-permute-done.4.refs_2_ = bf16[4,64,128]{2,1,0:T(8,128)(2,1)S(1)} collective-permute-done((bf16[4,64,128]{2,1,0:T(8,128)(2,1)S(1)}, bf16[4,64,128]{2,1,0:T(8,128)(2,1)S(1)}, u32[]{:S(2)}, u32[]{:S(2)}) %collective-permute-start.4) | collective-permute-done | bytes 65568 | tf_op jit(solution)/shard_map/ppermute | solution.py:237
  17.8 0.9 %collective-permute-done.5.refs_3_ = bf16[4,64,128]{2,1,0:T(8,128)(2,1)S(1)} collective-permute-done((bf16[4,64,128]{2,1,0:T(8,128)(2,1)S(1)}, bf16[4,64,128]{2,1,0:T(8,128)(2,1)S(1)}, u32[]{:S(2)}, u32[]{:S(2)}) %collective-permute-start.5) | collective-permute-done | bytes 65568 | tf_op jit(solution)/shard_map/ppermute | solution.py:237
  18.7 2.1 %weight_term.1 = (bf16[112,384]{1,0:T(8,128)(2,1)S(1)}, bf16[112,384]{1,0:T(8,128)(2,1)S(1)}, bf16[112,384]{1,0:T(8,128)(2,1)S(1)}, bf16[448,3072]{1,0:T(8,128)(2,1)S(1)}) custom-call(bf16[4,64,128]{2,1,0:T(8,128)(2,1)S(1)} %get-tuple-element.20.refs_0_, bf16[4,64,128]{2,1,0:T(8,128)(2,1)S(1)} %collective-permute-done.3.refs_1_, ...), custom_call_target="tpu_custom_call" | custom-call | flops 1056964608 | bytes 3538944 | tf_op jit(solution)/shard_map/weight_term/pallas_call | solution.py:288
  20.8 1.6 %collective-permute-start.6 = (bf16[112,384]{1,0:T(8,128)(2,1)S(1)}, bf16[112,384]{1,0:T(8,128)(2,1)S(1)}, u32[]{:S(2)}, u32[]{:S(2)}) collective-permute-start(bf16[112,384]{1,0:T(8,128)(2,1)S(1)} %get-tuple-element.28), channel_id=1, source_target_pairs={{0,24},{8,16},{16,8},{24,0},{1,25},{9,17},{17,9},{25,1},{2,26},{10... | collective-permute-start | bytes 258056 | tf_op jit(solution)/shard_map/ppermute | solution.py:237
  22.4 1.5 %collective-permute-start.7 = (bf16[112,384]{1,0:T(8,128)(2,1)S(1)}, bf16[112,384]{1,0:T(8,128)(2,1)S(1)}, u32[]{:S(2)}, u32[]{:S(2)}) collective-permute-start(bf16[112,384]{1,0:T(8,128)(2,1)S(1)} %get-tuple-element.29), channel_id=1, source_target_pairs={{0,8},{8,0},{16,24},{24,16},{1,9},{9,1},{17,25},{25,17},{2,10},{10... | collective-permute-start | bytes 258056 | tf_op jit(solution)/shard_map/ppermute | solution.py:237
  23.9 0.5 %collective-permute-start.8 = (bf16[112,384]{1,0:T(8,128)(2,1)S(1)}, bf16[112,384]{1,0:T(8,128)(2,1)S(1)}, u32[]{:S(2)}, u32[]{:S(2)}) collective-permute-start(bf16[112,384]{1,0:T(8,128)(2,1)S(1)} %get-tuple-element.30), channel_id=1, source_target_pairs={{0,16},{8,24},{16,0},{24,8},{1,17},{9,25},{17,1},{25,9},{2,18},{10... | collective-permute-start | bytes 258056 | tf_op jit(solution)/shard_map/ppermute | solution.py:237
  24.4 0.0 copy-start
  24.4 0.6 %own_piece.1 = f32[112,384]{1,0:T(8,128)S(1)} custom-call(bf16[448,3072]{1,0:T(8,128)(2,1)S(1)} %get-tuple-element.32.cols_ref, bf16[3072,384]{1,0:T(8,128)(2,1)S(1)} %get-tuple-element.26.refs_6_.act_ref), custom_call_target="tpu_custom_call" | custom-call | flops 264241152 | bytes 1769472 | tf_op jit(solution)/shard_map/own_piece/pallas_call | solution.py:298
  25.0 1.3 %collective-permute-done.6 = bf16[112,384]{1,0:T(8,128)(2,1)S(1)} collective-permute-done((bf16[112,384]{1,0:T(8,128)(2,1)S(1)}, bf16[112,384]{1,0:T(8,128)(2,1)S(1)}, u32[]{:S(2)}, u32[]{:S(2)}) %collective-permute-start.6) | collective-permute-done | bytes 86048 | tf_op jit(solution)/shard_map/ppermute | solution.py:237
  26.3 1.0 %collective-permute-done.7 = bf16[112,384]{1,0:T(8,128)(2,1)S(1)} collective-permute-done((bf16[112,384]{1,0:T(8,128)(2,1)S(1)}, bf16[112,384]{1,0:T(8,128)(2,1)S(1)}, u32[]{:S(2)}, u32[]{:S(2)}) %collective-permute-start.7) | collective-permute-done | bytes 86048 | tf_op jit(solution)/shard_map/ppermute | solution.py:237
  27.3 1.1 %collective-permute-done.8 = bf16[112,384]{1,0:T(8,128)(2,1)S(1)} collective-permute-done((bf16[112,384]{1,0:T(8,128)(2,1)S(1)}, bf16[112,384]{1,0:T(8,128)(2,1)S(1)}, u32[]{:S(2)}, u32[]{:S(2)}) %collective-permute-start.8) | collective-permute-done | bytes 86048 | tf_op jit(solution)/shard_map/ppermute | solution.py:237
  28.4 3.0 %collective-permute-start.11 = (bf16[112,384]{1,0:T(8,128)(2,1)S(1)}, bf16[112,384]{1,0:T(8,128)(2,1)S(1)}, u32[]{:S(2)}, u32[]{:S(2)}) collective-permute-start(bf16[112,384]{1,0:T(8,128)(2,1)S(1)} %add_convert_fusion), channel_id=1, source_target_pairs={{0,6},{2,4},{4,2},{6,0},{1,7},{3,5},{5,3},{7,1},{8,14},{10,12},{12... | collective-permute-start | bytes 258056 | tf_op jit(solution)/shard_map/ppermute | solution.py:237
  31.4 0.0 collective-permute-start.10
  31.4 1.5 %collective-permute-start.9 = (bf16[112,384]{1,0:T(8,128)(2,1)S(1)}, bf16[112,384]{1,0:T(8,128)(2,1)S(1)}, u32[]{:S(2)}, u32[]{:S(2)}) collective-permute-start(bf16[112,384]{1,0:T(8,128)(2,1)S(1)} %add_convert_fusion), channel_id=1, source_target_pairs={{0,4},{2,6},{4,0},{6,2},{1,5},{3,7},{5,1},{7,3},{8,12},{10,14},{12... | collective-permute-start | bytes 258056 | tf_op jit(solution)/shard_map/ppermute | solution.py:237
  32.9 0.0 copy-done
  32.9 3.1 %features_grad.1 = bf16[2304,384]{1,0:T(8,128)(2,1)} custom-call(bf16[448,3072]{1,0:T(8,128)(2,1)S(1)} %get-tuple-element.32.cols_ref, f32[2304,384]{1,0:T(8,128)S(1)} %get-tuple-element.33.slope_ref, bf16[432,384]{1,0:T(8,128)(2,1)S(1)} %copy-done), custom_call_target="tpu_custom_call" | custom-call | flops 1056964608 | bytes 7077888 | tf_op jit(solution)/shard_map/features_grad/pallas_call | solution.py:311
  36.0 0.0 collective-permute-done.11
  36.0 0.0 collective-permute-done.10
  36.0 0.8 %collective-permute-done.9 = bf16[112,384]{1,0:T(8,128)(2,1)S(1)} collective-permute-done((bf16[112,384]{1,0:T(8,128)(2,1)S(1)}, bf16[112,384]{1,0:T(8,128)(2,1)S(1)}, u32[]{:S(2)}, u32[]{:S(2)}) %collective-permute-start.9) | collective-permute-done | bytes 86048 | tf_op jit(solution)/shard_map/ppermute | solution.py:237
  36.8 0.1 multiply_convert_fusion.refs_0_
  36.9 1.0 %collective-permute-start.14 = (bf16[112,384]{1,0:T(8,128)(2,1)S(1)}, bf16[112,384]{1,0:T(8,128)(2,1)S(1)}, u32[]{:S(2)}, u32[]{:S(2)}) collective-permute-start(bf16[112,384]{1,0:T(8,128)(2,1)S(1)} %multiply_convert_fusion.refs_0_), channel_id=1, source_target_pairs={{0,24},{8,16},{16,8},{24,0},{1,25},{9,17},{17,9},{25,1},{2,26},{10... | collective-permute-start | bytes 258056 | tf_op jit(solution)/shard_map/ppermute | solution.py:237
  37.9 1.1 %collective-permute-start.13 = (bf16[112,384]{1,0:T(8,128)(2,1)S(1)}, bf16[112,384]{1,0:T(8,128)(2,1)S(1)}, u32[]{:S(2)}, u32[]{:S(2)}) collective-permute-start(bf16[112,384]{1,0:T(8,128)(2,1)S(1)} %multiply_convert_fusion.refs_0_), channel_id=1, source_target_pairs={{0,16},{8,24},{16,0},{24,8},{1,17},{9,25},{17,1},{25,9},{2,18},{10... | collective-permute-start | bytes 258056 | tf_op jit(solution)/shard_map/ppermute | solution.py:237
  39.0 1.4 %collective-permute-start.12 = (bf16[112,384]{1,0:T(8,128)(2,1)S(1)}, bf16[112,384]{1,0:T(8,128)(2,1)S(1)}, u32[]{:S(2)}, u32[]{:S(2)}) collective-permute-start(bf16[112,384]{1,0:T(8,128)(2,1)S(1)} %multiply_convert_fusion.refs_0_), channel_id=1, source_target_pairs={{0,8},{8,0},{16,24},{24,16},{1,9},{9,1},{17,25},{25,17},{2,10},{10... | collective-permute-start | bytes 258056 | tf_op jit(solution)/shard_map/ppermute | solution.py:237
  40.4 2.0 %collective-permute-done.14.refs_3_ = bf16[112,384]{1,0:T(8,128)(2,1)S(1)} collective-permute-done((bf16[112,384]{1,0:T(8,128)(2,1)S(1)}, bf16[112,384]{1,0:T(8,128)(2,1)S(1)}, u32[]{:S(2)}, u32[]{:S(2)}) %collective-permute-start.14) | collective-permute-done | bytes 86048 | tf_op jit(solution)/shard_map/ppermute | solution.py:237
  42.4 0.8 %collective-permute-done.13.refs_2_ = bf16[112,384]{1,0:T(8,128)(2,1)S(1)} collective-permute-done((bf16[112,384]{1,0:T(8,128)(2,1)S(1)}, bf16[112,384]{1,0:T(8,128)(2,1)S(1)}, u32[]{:S(2)}, u32[]{:S(2)}) %collective-permute-start.13) | collective-permute-done | bytes 86048 | tf_op jit(solution)/shard_map/ppermute | solution.py:237
  43.2 0.2 collective-permute-done.12.refs_1_
  43.5 0.9 %join_pieces.1 = f32[432,384]{1,0:T(8,128)} custom-call(bf16[112,384]{1,0:T(8,128)(2,1)S(1)} %multiply_convert_fusion.refs_0_, bf16[112,384]{1,0:T(8,128)(2,1)S(1)} %collective-permute-done.12.refs_1_, bf16[112,384]{1,0:T(8,128)(2,1)S(1)} %collective-permute-done.13.refs_2_, bf16[112,384]{1,0:T(8,128)(2,1)S(1)} %collective-permute-done.14.refs_3_), custom_call_target="tpu_custom_call" | custom-call | tf_op jit(solution)/shard_map/join_pieces/pallas_call | solution.py:325
  (1 shorter events, 0.0 us)
Async XLA Ops:
  0.6 7.1 %collective-permute-start.2 = (bf16[16,2304]{1,0:T(8,128)(2,1)}, bf16[16,2304]{1,0:T(8,128)(2,1)S(1)}, u32[]{:S(2)}, u32[]{:S(2)}) collective-permute-start(bf16[16,2304]{1,0:T(8,128)(2,1)} %bitcast.5), channel_id=1, source_target_pairs={{0,24},{8,16},{16,8},{24,0},{1,25},{9,17},{17,9},{25,1},{2,26},{10... | collective-permute-start | bytes 221192 | tf_op jit(solution)/shard_map/ppermute | solution.py:237
  4.6 4.6 %collective-permute-start.1 = (bf16[16,2304]{1,0:T(8,128)(2,1)}, bf16[16,2304]{1,0:T(8,128)(2,1)S(1)}, u32[]{:S(2)}, u32[]{:S(2)}) collective-permute-start(bf16[16,2304]{1,0:T(8,128)(2,1)} %bitcast.6), channel_id=1, source_target_pairs={{0,16},{8,24},{16,0},{24,8},{1,17},{9,25},{17,1},{25,9},{2,18},{10... | collective-permute-start | bytes 221192 | tf_op jit(solution)/shard_map/ppermute | solution.py:237
  5.1 4.6 %collective-permute-start = (bf16[16,2304]{1,0:T(8,128)(2,1)}, bf16[16,2304]{1,0:T(8,128)(2,1)S(1)}, u32[]{:S(2)}, u32[]{:S(2)}) collective-permute-start(bf16[16,2304]{1,0:T(8,128)(2,1)} %bitcast.7), channel_id=1, source_target_pairs={{0,8},{8,0},{16,24},{24,16},{1,9},{9,1},{17,25},{25,17},{2,10},{10... | collective-permute-start | bytes 221192 | tf_op jit(solution)/shard_map/ppermute | solution.py:237
  9.9 6.3 %collective-permute-start.3 = (bf16[4,64,128]{2,1,0:T(8,128)(2,1)S(1)}, bf16[4,64,128]{2,1,0:T(8,128)(2,1)S(1)}, u32[]{:S(2)}, u32[]{:S(2)}) collective-permute-start(bf16[4,64,128]{2,1,0:T(8,128)(2,1)S(1)} %get-tuple-element.21), channel_id=1, source_target_pairs={{0,6},{2,4},{4,2},{6,0},{1,7},{3,5},{5,3},{7,1},{8,14},{10,12},{12... | collective-permute-start | bytes 196616 | tf_op jit(solution)/shard_map/ppermute | solution.py:237
  13.5 4.3 %collective-permute-start.4 = (bf16[4,64,128]{2,1,0:T(8,128)(2,1)S(1)}, bf16[4,64,128]{2,1,0:T(8,128)(2,1)S(1)}, u32[]{:S(2)}, u32[]{:S(2)}) collective-permute-start(bf16[4,64,128]{2,1,0:T(8,128)(2,1)S(1)} %get-tuple-element.22), channel_id=1, source_target_pairs={{0,2},{2,0},{4,6},{6,4},{1,3},{3,1},{5,7},{7,5},{8,10},{10,8},{12,... | collective-permute-start | bytes 196616 | tf_op jit(solution)/shard_map/ppermute | solution.py:237
  13.6 5.2 %collective-permute-start.5 = (bf16[4,64,128]{2,1,0:T(8,128)(2,1)S(1)}, bf16[4,64,128]{2,1,0:T(8,128)(2,1)S(1)}, u32[]{:S(2)}, u32[]{:S(2)}) collective-permute-start(bf16[4,64,128]{2,1,0:T(8,128)(2,1)S(1)} %get-tuple-element.23), channel_id=1, source_target_pairs={{0,4},{2,6},{4,0},{6,2},{1,5},{3,7},{5,1},{7,3},{8,12},{10,14},{12... | collective-permute-start | bytes 196616 | tf_op jit(solution)/shard_map/ppermute | solution.py:237
  20.8 5.4 %collective-permute-start.6 = (bf16[112,384]{1,0:T(8,128)(2,1)S(1)}, bf16[112,384]{1,0:T(8,128)(2,1)S(1)}, u32[]{:S(2)}, u32[]{:S(2)}) collective-permute-start(bf16[112,384]{1,0:T(8,128)(2,1)S(1)} %get-tuple-element.28), channel_id=1, source_target_pairs={{0,24},{8,16},{16,8},{24,0},{1,25},{9,17},{17,9},{25,1},{2,26},{10... | collective-permute-start | bytes 258056 | tf_op jit(solution)/shard_map/ppermute | solution.py:237
  22.4 4.9 %collective-permute-start.7 = (bf16[112,384]{1,0:T(8,128)(2,1)S(1)}, bf16[112,384]{1,0:T(8,128)(2,1)S(1)}, u32[]{:S(2)}, u32[]{:S(2)}) collective-permute-start(bf16[112,384]{1,0:T(8,128)(2,1)S(1)} %get-tuple-element.29), channel_id=1, source_target_pairs={{0,8},{8,0},{16,24},{24,16},{1,9},{9,1},{17,25},{25,17},{2,10},{10... | collective-permute-start | bytes 258056 | tf_op jit(solution)/shard_map/ppermute | solution.py:237
  23.9 4.5 %collective-permute-start.8 = (bf16[112,384]{1,0:T(8,128)(2,1)S(1)}, bf16[112,384]{1,0:T(8,128)(2,1)S(1)}, u32[]{:S(2)}, u32[]{:S(2)}) collective-permute-start(bf16[112,384]{1,0:T(8,128)(2,1)S(1)} %get-tuple-element.30), channel_id=1, source_target_pairs={{0,16},{8,24},{16,0},{24,8},{1,17},{9,25},{17,1},{25,9},{2,18},{10... | collective-permute-start | bytes 258056 | tf_op jit(solution)/shard_map/ppermute | solution.py:237
  24.4 8.5 %copy-start = (bf16[432,384]{1,0:T(8,128)(2,1)S(1)}, bf16[432,384]{1,0:T(8,128)(2,1)}, u32[]{:S(2)}) copy-start(bf16[432,384]{1,0:T(8,128)(2,1)} %weight_ref.1) | copy-start | bytes 995332
  28.4 7.6 %collective-permute-start.11 = (bf16[112,384]{1,0:T(8,128)(2,1)S(1)}, bf16[112,384]{1,0:T(8,128)(2,1)S(1)}, u32[]{:S(2)}, u32[]{:S(2)}) collective-permute-start(bf16[112,384]{1,0:T(8,128)(2,1)S(1)} %add_convert_fusion), channel_id=1, source_target_pairs={{0,6},{2,4},{4,2},{6,0},{1,7},{3,5},{5,3},{7,1},{8,14},{10,12},{12... | collective-permute-start | bytes 258056 | tf_op jit(solution)/shard_map/ppermute | solution.py:237
  31.4 4.6 %collective-permute-start.10 = (bf16[112,384]{1,0:T(8,128)(2,1)S(1)}, bf16[112,384]{1,0:T(8,128)(2,1)S(1)}, u32[]{:S(2)}, u32[]{:S(2)}) collective-permute-start(bf16[112,384]{1,0:T(8,128)(2,1)S(1)} %add_convert_fusion), channel_id=1, source_target_pairs={{0,2},{2,0},{4,6},{6,4},{1,3},{3,1},{5,7},{7,5},{8,10},{10,8},{12,... | collective-permute-start | bytes 258056 | tf_op jit(solution)/shard_map/ppermute | solution.py:237
  31.4 5.4 %collective-permute-start.9 = (bf16[112,384]{1,0:T(8,128)(2,1)S(1)}, bf16[112,384]{1,0:T(8,128)(2,1)S(1)}, u32[]{:S(2)}, u32[]{:S(2)}) collective-permute-start(bf16[112,384]{1,0:T(8,128)(2,1)S(1)} %add_convert_fusion), channel_id=1, source_target_pairs={{0,4},{2,6},{4,0},{6,2},{1,5},{3,7},{5,1},{7,3},{8,12},{10,14},{12... | collective-permute-start | bytes 258056 | tf_op jit(solution)/shard_map/ppermute | solution.py:237
  36.9 5.5 %collective-permute-start.14 = (bf16[112,384]{1,0:T(8,128)(2,1)S(1)}, bf16[112,384]{1,0:T(8,128)(2,1)S(1)}, u32[]{:S(2)}, u32[]{:S(2)}) collective-permute-start(bf16[112,384]{1,0:T(8,128)(2,1)S(1)} %multiply_convert_fusion.refs_0_), channel_id=1, source_target_pairs={{0,24},{8,16},{16,8},{24,0},{1,25},{9,17},{17,9},{25,1},{2,26},{10... | collective-permute-start | bytes 258056 | tf_op jit(solution)/shard_map/ppermute | solution.py:237
  37.9 5.4 %collective-permute-start.13 = (bf16[112,384]{1,0:T(8,128)(2,1)S(1)}, bf16[112,384]{1,0:T(8,128)(2,1)S(1)}, u32[]{:S(2)}, u32[]{:S(2)}) collective-permute-start(bf16[112,384]{1,0:T(8,128)(2,1)S(1)} %multiply_convert_fusion.refs_0_), channel_id=1, source_target_pairs={{0,16},{8,24},{16,0},{24,8},{1,17},{9,25},{17,1},{25,9},{2,18},{10... | collective-permute-start | bytes 258056 | tf_op jit(solution)/shard_map/ppermute | solution.py:237
  39.0 4.5 %collective-permute-start.12 = (bf16[112,384]{1,0:T(8,128)(2,1)S(1)}, bf16[112,384]{1,0:T(8,128)(2,1)S(1)}, u32[]{:S(2)}, u32[]{:S(2)}) collective-permute-start(bf16[112,384]{1,0:T(8,128)(2,1)S(1)} %multiply_convert_fusion.refs_0_), channel_id=1, source_target_pairs={{0,8},{8,0},{16,24},{24,16},{1,9},{9,1},{17,25},{25,17},{2,10},{10... | collective-permute-start | bytes 258056 | tf_op jit(solution)/shard_map/ppermute | solution.py:237

commit v4 on v3

--- a/solution.py
+++ b/solution.py
@@ -127,7 +127,7 @@
     return [count - 1, *range(1, count - 1)]
 
 
-def fill_cols(z, moved_refs, sort_ref, place_ref, cols_ref, held_ref):
+def turned_grid(z, moved_refs, sort_ref, place_ref, held_ref):
     count = z.frames_x * z.feat
     rows = z.n_rows * count
     band = lax.axis_index("rows")
@@ -141,46 +141,54 @@
     half = rows // 2
     pair = jnp.concatenate([ordered[:half], ordered[half:]], axis=1)
     grid = jnp.dot(pair, place_ref[...], preferred_element_type=jnp.float32)
-    slots = [slot_start(z, piece) for piece in range(z.n_time)]
-
-    def tap_rows(tap):
-        start = slots[tap // z.piece_taps] + tap % z.piece_taps * z.latent
-        return pl.ds(pl.multiple_of(start, z.latent), z.latent)
-
+    turned = {}
     for a in range(z.band_x):
         block = grid[:, a * LANES : (a + 1) * LANES]
-        for kw in range(3):
-            turned = block if kw == 1 else pltpu.roll(block, LANES - 1 if kw == 0 else 1, 1)
-            turned = turned.astype(jnp.bfloat16)
-            for p in range(2):
-                for t in range(z.frames_x):
-                    at = (p * z.frames_x + t) * z.latent
-                    value = turned[at : at + z.latent]
-                    for kt in range(3):
-                        for kh in range(3):
-                            frame, row = t - 2 + kt, 2 * (a - 1) + p - 1 + kh
-                            if 0 <= frame < z.frames and 0 <= row < z.rows:
-                                tap = (kt * 3 + kh) * 3 + kw
-                                lane = (frame * z.rows + row) * LANES
-                                cols_ref[tap_rows(tap), lane : lane + LANES] = value
-    for tap in range(TAPS, z.n_time * z.piece_taps):
-        cols_ref[tap_rows(tap), :] = jnp.zeros((z.latent, z.grid_rows * LANES), jnp.bfloat16)
+        for kw, turn in enumerate((LANES - 1, 0, 1)):
+            value = pltpu.roll(block, turn, 1) if turn else block
+            turned[a, kw] = value.astype(jnp.bfloat16)
+    return turned
+
+
+def fill_cols(z, turned, frame, cols_ref):
+    for tap in range(z.n_time * z.piece_taps):
+        start = slot_start(z, tap // z.piece_taps) + tap % z.piece_taps * z.latent
+        here = pl.ds(pl.multiple_of(start, z.latent), z.latent)
+        if tap >= TAPS:
+            cols_ref[here, :] = jnp.zeros((z.latent, z.rows * LANES), jnp.bfloat16)
+            continue
+        kt, kh, kw = tap // 9, tap // 3 % 3, tap % 3
+        t = frame + 2 - kt
+        for row in range(z.rows):
+            a, p = divmod(row + 1 - kh + 2, 2)
+            at = (p * z.frames_x + t) * z.latent
+            cols_ref[here, row * LANES : (row + 1) * LANES] = turned[a, kw][at : at + z.latent]
 
 
 def weight_kernel(z, *refs):
     moved_refs, (sort_ref, place_ref, act_ref) = refs[: z.n_rows], refs[z.n_rows : z.n_rows + 3]
-    out_refs, cols_ref, held_ref = refs[z.n_rows + 3 : -2], refs[-2], refs[-1]
-    fill_cols(z, moved_refs, sort_ref, place_ref, cols_ref, held_ref)
-    total = jnp.dot(cols_ref[z.piece :, :], act_ref[...], preferred_element_type=jnp.float32)
+    out_refs, cols_refs, held_ref = refs[z.n_rows + 3 : -1 - z.frames], refs[-1 - z.frames : -1], refs[-1]
+    turned = turned_grid(z, moved_refs, sort_ref, place_ref, held_ref)
+    total = 0.0
+    for frame, cols_ref in enumerate(cols_refs):
+        fill_cols(z, turned, frame, cols_ref)
+        act = act_ref[frame * z.rows * LANES : (frame + 1) * z.rows * LANES, :]
+        total = total + jnp.dot(cols_ref[z.piece :, :], act, preferred_element_type=jnp.float32)
     for step, ref in enumerate(out_refs):
         ref[...] = total[step * z.piece : (step + 1) * z.piece].astype(jnp.bfloat16)
 
 
-def own_kernel(z, cols_ref, act_ref, out_ref):
-    out_ref[...] = jnp.dot(cols_ref[: z.piece, :], act_ref[...], preferred_element_type=jnp.float32)
-
-
-def features_kernel(z, cols_ref, slope_ref, weight_ref, out_ref, held_ref):
+def own_kernel(z, *refs):
+    cols_refs, (act_ref, out_ref) = refs[: z.frames], refs[z.frames :]
+    total = 0.0
+    for frame, cols_ref in enumerate(cols_refs):
+        act = act_ref[frame * z.rows * LANES : (frame + 1) * z.rows * LANES, :]
+        total = total + jnp.dot(cols_ref[: z.piece, :], act, preferred_element_type=jnp.float32)
+    out_ref[...] = total
+
+
+def features_kernel(z, *refs):
+    cols_refs, (slope_ref, weight_ref, out_ref, held_ref) = refs[: z.frames], refs[z.frames :]
     for piece in range(z.n_time):
         first = piece * z.piece
         count = max(0, min(z.piece, TAPS * z.latent - first))
@@ -191,16 +199,18 @@
             start = pl.multiple_of(start + count, z.latent)
             held_ref[pl.ds(start, z.piece - count), :] = jnp.zeros((z.piece - count, z.channels), jnp.bfloat16)
     step = 4
-    for first in range(0, z.grid_rows, step):
-        count = min(step, z.grid_rows - first)
-        part = cols_ref[:, first * LANES : (first + count) * LANES]
-        product = lax.dot_general(
-            part, held_ref[...], (((0,), (0,)), ((), ())), preferred_element_type=jnp.float32
-        )
-        for k in range(count):
-            here = slice((first + k) * z.width, (first + k + 1) * z.width)
-            value = product[k * LANES : k * LANES + z.width] * slope_ref[here, :]
-            out_ref[here, :] = value.astype(jnp.bfloat16)
+    for frame, cols_ref in enumerate(cols_refs):
+        for first in range(0, z.rows, step):
+            count = min(step, z.rows - first)
+            part = cols_ref[:, first * LANES : (first + count) * LANES]
+            product = lax.dot_general(
+                part, held_ref[...], (((0,), (0,)), ((), ())), preferred_element_type=jnp.float32
+            )
+            for k in range(count):
+                row = frame * z.rows + first + k
+                here = slice(row * z.width, (row + 1) * z.width)
+                value = product[k * LANES : k * LANES + z.width] * slope_ref[here, :]
+                out_ref[here, :] = value.astype(jnp.bfloat16)
 
 
 def join_kernel(z, *refs):
@@ -208,23 +218,23 @@
     me = lax.axis_index("tm")
     whole, tail = divmod(TAPS * z.latent, z.piece)
 
-    def each(act):
-        for step in range(z.n_time):
-            place = me ^ step
-            start = pl.multiple_of(place * z.piece, z.piece)
-
-            def copy(count):
-                source = held_ref.at[step, pl.ds(0, count)]
-                act(pltpu.make_async_copy(source, out_ref.at[pl.ds(start, count)], sems.at[step]))
-
-            pl.when(place < whole)(functools.partial(copy, z.piece))
-            if tail:
-                pl.when(place == whole)(functools.partial(copy, tail))
+    def each(step, act):
+        place = me ^ step
+        start = pl.multiple_of(place * z.piece, z.piece)
+
+        def copy(count):
+            source = held_ref.at[step, pl.ds(0, count)]
+            act(pltpu.make_async_copy(source, out_ref.at[pl.ds(start, count)], sems.at[step]))
+
+        pl.when(place < whole)(functools.partial(copy, z.piece))
+        if tail:
+            pl.when(place == whole)(functools.partial(copy, tail))
 
     for step, ref in enumerate(piece_refs):
         held_ref[step] = ref[...].astype(jnp.float32)
-    each(lambda copy: copy.start())
-    each(lambda copy: copy.wait())
+        each(step, lambda copy: copy.start())
+    for step in range(z.n_time):
+        each(step, lambda copy: copy.wait())
 
 
 def in_hbm(value):
@@ -285,15 +295,16 @@
     )(tokens, *arrived)
     arrived = exchange(windows[1:], "rows")
     moved = [windows[0]] + [arrived[step - 1] for step in last_first(n_rows)]
-    *pieces, cols = pl.pallas_call(
+    outs = pl.pallas_call(
         functools.partial(weight_kernel, z),
         out_shape=[jax.ShapeDtypeStruct((z.piece, z.channels), bf16)] * (n_time - 1)
-        + [jax.ShapeDtypeStruct((z.cols, z.grid_rows * LANES), bf16)],
+        + [jax.ShapeDtypeStruct((z.cols, z.rows * LANES), bf16)] * z.frames,
         scratch_shapes=[pltpu.VMEM((n_rows * z.frames_x * z.feat, n_time * LANES), bf16)],
         compiler_params=params,
         cost_estimate=pl.CostEstimate(flops=2 * products, bytes_accessed=4 * elements, transcendentals=0),
         name="weight_term",
     )(*moved, sort, place, act)
+    pieces, cols = outs[: n_time - 1], outs[n_time - 1 :]
     arrived = exchange(pieces, "tm")
     own = pl.pallas_call(
         functools.partial(own_kernel, z),
@@ -303,7 +314,7 @@
             flops=2 * products // n_time, bytes_accessed=2 * elements, transcendentals=0
         ),
         name="own_piece",
-    )(cols, act)
+    )(*cols, act)
     for step in last_first(n_time):
         own = own + arrived[step - 1].astype(f32)
     mine = own.astype(bf16)
@@ -315,7 +326,7 @@
         compiler_params=params,
         cost_estimate=pl.CostEstimate(flops=2 * products, bytes_accessed=8 * elements, transcendentals=0),
         name="features_grad",
-    )(cols, slope, head_weight)
+    )(*cols, slope, head_weight)
     arrived = exchange([mine] * (n_rows - 1), "rows")
     whole = coset_sum([value.astype(f32) for value in [mine] + arrived])
     scale = 1.0 / math.sqrt(cells * n_time * n_rows)

time: 44.6 us -> 44.5 us (level)
  no operation moved by 1% of the time
where the time goes in v4:
time: 44.5 us; the launch traced here: 44.3 us
  starting transfers between devices  20.6 us (46%)
  waiting for transfers between devices  13.6 us (31%)
  Pallas kernels  9.27 us (21%)
  between operations  0.69 us (2%)
    ppermute x15, starting transfers between devices, exchange(): lax.ppermute(value, axis, [(i, i ^ step) for i in range(size)])  20.6 us
    ppermute x15, waiting for transfers between devices, exchange(): lax.ppermute(value, axis, [(i, i ^ step) for i in range(size)])  13.6 us
    pallas_call x1, Pallas kernels, shards(): pl.pallas_call(functools.partial(features_kernel, z), out_shape=jax.Shape...  3.11 us
    pallas_call x1, Pallas kernels, shards(): pl.pallas_call(functools.partial(prepare_kernel, z), out_shape=[jax.Shape...  2.46 us
    pallas_call x1, Pallas kernels, shards(): pl.pallas_call(functools.partial(weight_kernel, z), out_shape=[jax.ShapeD...  2.06 us
  transfers between devices with their start and end apart: 15, of which 12 were waited for; matrix products, arithmetic and copies ran while one was open for 0% of the time, Pallas kernels for 14%

profile of v4, /device:TPU:0, one launch (start us, length us, event | category | flops | bytes accessed | tf_op | source)
XLA Modules:
  0.0 44.3 jit_solution(6607401870615200245)
XLA Ops:
  0.6 4.0 %collective-permute-start.2 = (bf16[16,2304]{1,0:T(8,128)(2,1)}, bf16[16,2304]{1,0:T(8,128)(2,1)S(1)}, u32[]{:S(2)}, u32[]{:S(2)}) collective-permute-start(bf16[16,2304]{1,0:T(8,128)(2,1)} %bitcast.5), channel_id=1, source_target_pairs={{0,24},{8,16},{16,8},{24,0},{1,25},{9,17},{17,9},{25,1},{2,26},{10... | collective-permute-start | bytes 221192 | tf_op jit(solution)/shard_map/ppermute | solution.py:247
  4.6 0.5 %collective-permute-start.1 = (bf16[16,2304]{1,0:T(8,128)(2,1)}, bf16[16,2304]{1,0:T(8,128)(2,1)S(1)}, u32[]{:S(2)}, u32[]{:S(2)}) collective-permute-start(bf16[16,2304]{1,0:T(8,128)(2,1)} %bitcast.6), channel_id=1, source_target_pairs={{0,16},{8,24},{16,0},{24,8},{1,17},{9,25},{17,1},{25,9},{2,18},{10... | collective-permute-start | bytes 221192 | tf_op jit(solution)/shard_map/ppermute | solution.py:247
  5.1 0.1 collective-permute-start
  5.2 2.5 %act_and_slope.1 = (bf16[3072,384]{1,0:T(8,128)(2,1)S(1)}, f32[2304,384]{1,0:T(8,128)S(1)}, bf16[256,256]{1,0:T(8,128)(2,1)S(1)}, bf16[1024,1024]{1,0:T(8,128)(2,1)S(1)}, bf16[16,2304]{1,0:T(8,128)(2,1)S(1)}) custom-call(bf16[2304,384]{1,0:T(8,128)(2,1)} %bitcast.3, bf16[256,256]{1,0:T(8,128)(2,1)} %constant.6.clone.sort_ref, ...), custom_call_target="tpu_custom_call" | custom-call | flops 8847360 | bytes 7962624 | tf_op jit(solution)/shard_map/act_and_slope/pallas_call | solution.py:272
  7.7 0.0 collective-permute-done.2.refs_3_
  7.7 1.4 %collective-permute-done.1.refs_2_ = bf16[16,2304]{1,0:T(8,128)(2,1)S(1)} collective-permute-done((bf16[16,2304]{1,0:T(8,128)(2,1)}, bf16[16,2304]{1,0:T(8,128)(2,1)S(1)}, u32[]{:S(2)}, u32[]{:S(2)}) %collective-permute-start.1) | collective-permute-done | bytes 73760 | tf_op jit(solution)/shard_map/ppermute | solution.py:247
  9.2 0.5 %collective-permute-done.refs_1_ = bf16[16,2304]{1,0:T(8,128)(2,1)S(1)} collective-permute-done((bf16[16,2304]{1,0:T(8,128)(2,1)}, bf16[16,2304]{1,0:T(8,128)(2,1)S(1)}, u32[]{:S(2)}, u32[]{:S(2)}) %collective-permute-start) | collective-permute-done | bytes 73760 | tf_op jit(solution)/shard_map/ppermute | solution.py:247
  9.7 0.2 latent_windows.1
  9.9 3.7 %collective-permute-start.3 = (bf16[4,64,128]{2,1,0:T(8,128)(2,1)S(1)}, bf16[4,64,128]{2,1,0:T(8,128)(2,1)S(1)}, u32[]{:S(2)}, u32[]{:S(2)}) collective-permute-start(bf16[4,64,128]{2,1,0:T(8,128)(2,1)S(1)} %get-tuple-element.23), channel_id=1, source_target_pairs={{0,6},{2,4},{4,2},{6,0},{1,7},{3,5},{5,3},{7,1},{8,14},{10,12},{12... | collective-permute-start | bytes 196616 | tf_op jit(solution)/shard_map/ppermute | solution.py:247
  13.5 0.0 collective-permute-start.4
  13.6 0.8 %collective-permute-start.5 = (bf16[4,64,128]{2,1,0:T(8,128)(2,1)S(1)}, bf16[4,64,128]{2,1,0:T(8,128)(2,1)S(1)}, u32[]{:S(2)}, u32[]{:S(2)}) collective-permute-start(bf16[4,64,128]{2,1,0:T(8,128)(2,1)S(1)} %get-tuple-element.25), channel_id=1, source_target_pairs={{0,4},{2,6},{4,0},{6,2},{1,5},{3,7},{5,1},{7,3},{8,12},{10,14},{12... | collective-permute-start | bytes 196616 | tf_op jit(solution)/shard_map/ppermute | solution.py:247
  14.3 1.8 %collective-permute-done.3.refs_1_ = bf16[4,64,128]{2,1,0:T(8,128)(2,1)S(1)} collective-permute-done((bf16[4,64,128]{2,1,0:T(8,128)(2,1)S(1)}, bf16[4,64,128]{2,1,0:T(8,128)(2,1)S(1)}, u32[]{:S(2)}, u32[]{:S(2)}) %collective-permute-start.3) | collective-permute-done | bytes 65568 | tf_op jit(solution)/shard_map/ppermute | solution.py:247
  16.1 1.7 %collective-permute-done.4.refs_2_ = bf16[4,64,128]{2,1,0:T(8,128)(2,1)S(1)} collective-permute-done((bf16[4,64,128]{2,1,0:T(8,128)(2,1)S(1)}, bf16[4,64,128]{2,1,0:T(8,128)(2,1)S(1)}, u32[]{:S(2)}, u32[]{:S(2)}) %collective-permute-start.4) | collective-permute-done | bytes 65568 | tf_op jit(solution)/shard_map/ppermute | solution.py:247
  17.8 0.9 %collective-permute-done.5.refs_3_ = bf16[4,64,128]{2,1,0:T(8,128)(2,1)S(1)} collective-permute-done((bf16[4,64,128]{2,1,0:T(8,128)(2,1)S(1)}, bf16[4,64,128]{2,1,0:T(8,128)(2,1)S(1)}, u32[]{:S(2)}, u32[]{:S(2)}) %collective-permute-start.5) | collective-permute-done | bytes 65568 | tf_op jit(solution)/shard_map/ppermute | solution.py:247
  18.7 2.1 %weight_term.1 = (bf16[112,384]{1,0:T(8,128)(2,1)S(1)}, bf16[112,384]{1,0:T(8,128)(2,1)S(1)}, bf16[112,384]{1,0:T(8,128)(2,1)S(1)}, bf16[448,1536]{1,0:T(8,128)(2,1)S(1)}, bf16[448,1536]{1,0:T(8,128)(2,1)S(1)}) custom-call(bf16[4,64,128]{2,1,0:T(8,128)(2,1)S(1)} %get-tuple-element.22.refs_0_, bf16[4,64,128]{2,1,0:T(8,128)(2,1)S(1)} %collective-permute-done.3.refs_1_, ...), custom_call_target="tpu_custom_call" | custom-call | flops 1056964608 | bytes 3538944 | tf_op jit(solution)/shard_map/weight_term/pallas_call | solution.py:298
  20.8 1.6 %collective-permute-start.6 = (bf16[112,384]{1,0:T(8,128)(2,1)S(1)}, bf16[112,384]{1,0:T(8,128)(2,1)S(1)}, u32[]{:S(2)}, u32[]{:S(2)}) collective-permute-start(bf16[112,384]{1,0:T(8,128)(2,1)S(1)} %get-tuple-element.31), channel_id=1, source_target_pairs={{0,24},{8,16},{16,8},{24,0},{1,25},{9,17},{17,9},{25,1},{2,26},{10... | collective-permute-start | bytes 258056 | tf_op jit(solution)/shard_map/ppermute | solution.py:247
  22.3 1.5 %collective-permute-start.7 = (bf16[112,384]{1,0:T(8,128)(2,1)S(1)}, bf16[112,384]{1,0:T(8,128)(2,1)S(1)}, u32[]{:S(2)}, u32[]{:S(2)}) collective-permute-start(bf16[112,384]{1,0:T(8,128)(2,1)S(1)} %get-tuple-element.32), channel_id=1, source_target_pairs={{0,8},{8,0},{16,24},{24,16},{1,9},{9,1},{17,25},{25,17},{2,10},{10... | collective-permute-start | bytes 258056 | tf_op jit(solution)/shard_map/ppermute | solution.py:247
  23.8 0.5 %collective-permute-start.8 = (bf16[112,384]{1,0:T(8,128)(2,1)S(1)}, bf16[112,384]{1,0:T(8,128)(2,1)S(1)}, u32[]{:S(2)}, u32[]{:S(2)}) collective-permute-start(bf16[112,384]{1,0:T(8,128)(2,1)S(1)} %get-tuple-element.33), channel_id=1, source_target_pairs={{0,16},{8,24},{16,0},{24,8},{1,17},{9,25},{17,1},{25,9},{2,18},{10... | collective-permute-start | bytes 258056 | tf_op jit(solution)/shard_map/ppermute | solution.py:247
  24.3 0.0 copy-start
  24.3 0.5 %own_piece.1 = f32[112,384]{1,0:T(8,128)S(1)} custom-call(bf16[448,1536]{1,0:T(8,128)(2,1)S(1)} %get-tuple-element.35.refs_0_, bf16[448,1536]{1,0:T(8,128)(2,1)S(1)} %get-tuple-element.36.refs_1_, bf16[3072,384]{1,0:T(8,128)(2,1)S(1)} %get-tuple-element.28.refs_6_.refs_2_), custom_call_target="tpu_custom_call" | custom-call | flops 264241152 | bytes 1769472 | tf_op jit(solution)/shard_map/own_piece/pallas_call | solution.py:309
  24.9 1.3 %collective-permute-done.6 = bf16[112,384]{1,0:T(8,128)(2,1)S(1)} collective-permute-done((bf16[112,384]{1,0:T(8,128)(2,1)S(1)}, bf16[112,384]{1,0:T(8,128)(2,1)S(1)}, u32[]{:S(2)}, u32[]{:S(2)}) %collective-permute-start.6) | collective-permute-done | bytes 86048 | tf_op jit(solution)/shard_map/ppermute | solution.py:247
  26.2 1.0 %collective-permute-done.7 = bf16[112,384]{1,0:T(8,128)(2,1)S(1)} collective-permute-done((bf16[112,384]{1,0:T(8,128)(2,1)S(1)}, bf16[112,384]{1,0:T(8,128)(2,1)S(1)}, u32[]{:S(2)}, u32[]{:S(2)}) %collective-permute-start.7) | collective-permute-done | bytes 86048 | tf_op jit(solution)/shard_map/ppermute | solution.py:247
  27.2 1.1 %collective-permute-done.8 = bf16[112,384]{1,0:T(8,128)(2,1)S(1)} collective-permute-done((bf16[112,384]{1,0:T(8,128)(2,1)S(1)}, bf16[112,384]{1,0:T(8,128)(2,1)S(1)}, u32[]{:S(2)}, u32[]{:S(2)}) %collective-permute-start.8) | collective-permute-done | bytes 86048 | tf_op jit(solution)/shard_map/ppermute | solution.py:247
  28.4 3.0 %collective-permute-start.11 = (bf16[112,384]{1,0:T(8,128)(2,1)S(1)}, bf16[112,384]{1,0:T(8,128)(2,1)S(1)}, u32[]{:S(2)}, u32[]{:S(2)}) collective-permute-start(bf16[112,384]{1,0:T(8,128)(2,1)S(1)} %add_convert_fusion), channel_id=1, source_target_pairs={{0,6},{2,4},{4,2},{6,0},{1,7},{3,5},{5,3},{7,1},{8,14},{10,12},{12... | collective-permute-start | bytes 258056 | tf_op jit(solution)/shard_map/ppermute | solution.py:247
  31.4 0.0 collective-permute-start.10
  31.4 1.5 %collective-permute-start.9 = (bf16[112,384]{1,0:T(8,128)(2,1)S(1)}, bf16[112,384]{1,0:T(8,128)(2,1)S(1)}, u32[]{:S(2)}, u32[]{:S(2)}) collective-permute-start(bf16[112,384]{1,0:T(8,128)(2,1)S(1)} %add_convert_fusion), channel_id=1, source_target_pairs={{0,4},{2,6},{4,0},{6,2},{1,5},{3,7},{5,1},{7,3},{8,12},{10,14},{12... | collective-permute-start | bytes 258056 | tf_op jit(solution)/shard_map/ppermute | solution.py:247
  32.8 0.0 copy-done
  32.8 3.1 %features_grad.1 = bf16[2304,384]{1,0:T(8,128)(2,1)} custom-call(bf16[448,1536]{1,0:T(8,128)(2,1)S(1)} %get-tuple-element.35.refs_0_, bf16[448,1536]{1,0:T(8,128)(2,1)S(1)} %get-tuple-element.36.refs_1_, f32[2304,384]{1,0:T(8,128)S(1)} %get-tuple-element.37.refs_2_, bf16[432,384]{1,0:T(8,128)(2,1)S(1)} %copy-done), custom_call_target="tpu_custom_call" | custom-call | flops 1056964608 | bytes 7077888 | tf_op jit(solution)/shard_map/features_grad/pallas_call | solution.py:322
  35.9 0.0 collective-permute-done.11
  35.9 0.0 collective-permute-done.10
  35.9 0.8 %collective-permute-done.9 = bf16[112,384]{1,0:T(8,128)(2,1)S(1)} collective-permute-done((bf16[112,384]{1,0:T(8,128)(2,1)S(1)}, bf16[112,384]{1,0:T(8,128)(2,1)S(1)}, u32[]{:S(2)}, u32[]{:S(2)}) %collective-permute-start.9) | collective-permute-done | bytes 86048 | tf_op jit(solution)/shard_map/ppermute | solution.py:247
  36.8 0.1 multiply_convert_fusion.refs_0_
  36.8 1.0 %collective-permute-start.14 = (bf16[112,384]{1,0:T(8,128)(2,1)S(1)}, bf16[112,384]{1,0:T(8,128)(2,1)S(1)}, u32[]{:S(2)}, u32[]{:S(2)}) collective-permute-start(bf16[112,384]{1,0:T(8,128)(2,1)S(1)} %multiply_convert_fusion.refs_0_), channel_id=1, source_target_pairs={{0,24},{8,16},{16,8},{24,0},{1,25},{9,17},{17,9},{25,1},{2,26},{10... | collective-permute-start | bytes 258056 | tf_op jit(solution)/shard_map/ppermute | solution.py:247
  37.8 1.1 %collective-permute-start.13 = (bf16[112,384]{1,0:T(8,128)(2,1)S(1)}, bf16[112,384]{1,0:T(8,128)(2,1)S(1)}, u32[]{:S(2)}, u32[]{:S(2)}) collective-permute-start(bf16[112,384]{1,0:T(8,128)(2,1)S(1)} %multiply_convert_fusion.refs_0_), channel_id=1, source_target_pairs={{0,16},{8,24},{16,0},{24,8},{1,17},{9,25},{17,1},{25,9},{2,18},{10... | collective-permute-start | bytes 258056 | tf_op jit(solution)/shard_map/ppermute | solution.py:247
  39.0 1.4 %collective-permute-start.12 = (bf16[112,384]{1,0:T(8,128)(2,1)S(1)}, bf16[112,384]{1,0:T(8,128)(2,1)S(1)}, u32[]{:S(2)}, u32[]{:S(2)}) collective-permute-start(bf16[112,384]{1,0:T(8,128)(2,1)S(1)} %multiply_convert_fusion.refs_0_), channel_id=1, source_target_pairs={{0,8},{8,0},{16,24},{24,16},{1,9},{9,1},{17,25},{25,17},{2,10},{10... | collective-permute-start | bytes 258056 | tf_op jit(solution)/shard_map/ppermute | solution.py:247
  40.4 2.0 %collective-permute-done.14.refs_3_ = bf16[112,384]{1,0:T(8,128)(2,1)S(1)} collective-permute-done((bf16[112,384]{1,0:T(8,128)(2,1)S(1)}, bf16[112,384]{1,0:T(8,128)(2,1)S(1)}, u32[]{:S(2)}, u32[]{:S(2)}) %collective-permute-start.14) | collective-permute-done | bytes 86048 | tf_op jit(solution)/shard_map/ppermute | solution.py:247
  42.4 0.8 %collective-permute-done.13.refs_2_ = bf16[112,384]{1,0:T(8,128)(2,1)S(1)} collective-permute-done((bf16[112,384]{1,0:T(8,128)(2,1)S(1)}, bf16[112,384]{1,0:T(8,128)(2,1)S(1)}, u32[]{:S(2)}, u32[]{:S(2)}) %collective-permute-start.13) | collective-permute-done | bytes 86048 | tf_op jit(solution)/shard_map/ppermute | solution.py:247
  43.2 0.2 collective-permute-done.12.refs_1_
  43.4 0.9 %join_pieces.1 = f32[432,384]{1,0:T(8,128)} custom-call(bf16[112,384]{1,0:T(8,128)(2,1)S(1)} %multiply_convert_fusion.refs_0_, bf16[112,384]{1,0:T(8,128)(2,1)S(1)} %collective-permute-done.12.refs_1_, bf16[112,384]{1,0:T(8,128)(2,1)S(1)} %collective-permute-done.13.refs_2_, bf16[112,384]{1,0:T(8,128)(2,1)S(1)} %collective-permute-done.14.refs_3_), custom_call_target="tpu_custom_call" | custom-call | tf_op jit(solution)/shard_map/join_pieces/pallas_call | solution.py:336
  (1 shorter events, 0.0 us)
Async XLA Ops:
  0.6 7.1 %collective-permute-start.2 = (bf16[16,2304]{1,0:T(8,128)(2,1)}, bf16[16,2304]{1,0:T(8,128)(2,1)S(1)}, u32[]{:S(2)}, u32[]{:S(2)}) collective-permute-start(bf16[16,2304]{1,0:T(8,128)(2,1)} %bitcast.5), channel_id=1, source_target_pairs={{0,24},{8,16},{16,8},{24,0},{1,25},{9,17},{17,9},{25,1},{2,26},{10... | collective-permute-start | bytes 221192 | tf_op jit(solution)/shard_map/ppermute | solution.py:247
  4.6 4.6 %collective-permute-start.1 = (bf16[16,2304]{1,0:T(8,128)(2,1)}, bf16[16,2304]{1,0:T(8,128)(2,1)S(1)}, u32[]{:S(2)}, u32[]{:S(2)}) collective-permute-start(bf16[16,2304]{1,0:T(8,128)(2,1)} %bitcast.6), channel_id=1, source_target_pairs={{0,16},{8,24},{16,0},{24,8},{1,17},{9,25},{17,1},{25,9},{2,18},{10... | collective-permute-start | bytes 221192 | tf_op jit(solution)/shard_map/ppermute | solution.py:247
  5.1 4.6 %collective-permute-start = (bf16[16,2304]{1,0:T(8,128)(2,1)}, bf16[16,2304]{1,0:T(8,128)(2,1)S(1)}, u32[]{:S(2)}, u32[]{:S(2)}) collective-permute-start(bf16[16,2304]{1,0:T(8,128)(2,1)} %bitcast.7), channel_id=1, source_target_pairs={{0,8},{8,0},{16,24},{24,16},{1,9},{9,1},{17,25},{25,17},{2,10},{10... | collective-permute-start | bytes 221192 | tf_op jit(solution)/shard_map/ppermute | solution.py:247
  9.9 6.3 %collective-permute-start.3 = (bf16[4,64,128]{2,1,0:T(8,128)(2,1)S(1)}, bf16[4,64,128]{2,1,0:T(8,128)(2,1)S(1)}, u32[]{:S(2)}, u32[]{:S(2)}) collective-permute-start(bf16[4,64,128]{2,1,0:T(8,128)(2,1)S(1)} %get-tuple-element.23), channel_id=1, source_target_pairs={{0,6},{2,4},{4,2},{6,0},{1,7},{3,5},{5,3},{7,1},{8,14},{10,12},{12... | collective-permute-start | bytes 196616 | tf_op jit(solution)/shard_map/ppermute | solution.py:247
  13.5 4.3 %collective-permute-start.4 = (bf16[4,64,128]{2,1,0:T(8,128)(2,1)S(1)}, bf16[4,64,128]{2,1,0:T(8,128)(2,1)S(1)}, u32[]{:S(2)}, u32[]{:S(2)}) collective-permute-start(bf16[4,64,128]{2,1,0:T(8,128)(2,1)S(1)} %get-tuple-element.24), channel_id=1, source_target_pairs={{0,2},{2,0},{4,6},{6,4},{1,3},{3,1},{5,7},{7,5},{8,10},{10,8},{12,... | collective-permute-start | bytes 196616 | tf_op jit(solution)/shard_map/ppermute | solution.py:247
  13.6 5.2 %collective-permute-start.5 = (bf16[4,64,128]{2,1,0:T(8,128)(2,1)S(1)}, bf16[4,64,128]{2,1,0:T(8,128)(2,1)S(1)}, u32[]{:S(2)}, u32[]{:S(2)}) collective-permute-start(bf16[4,64,128]{2,1,0:T(8,128)(2,1)S(1)} %get-tuple-element.25), channel_id=1, source_target_pairs={{0,4},{2,6},{4,0},{6,2},{1,5},{3,7},{5,1},{7,3},{8,12},{10,14},{12... | collective-permute-start | bytes 196616 | tf_op jit(solution)/shard_map/ppermute | solution.py:247
  20.8 5.4 %collective-permute-start.6 = (bf16[112,384]{1,0:T(8,128)(2,1)S(1)}, bf16[112,384]{1,0:T(8,128)(2,1)S(1)}, u32[]{:S(2)}, u32[]{:S(2)}) collective-permute-start(bf16[112,384]{1,0:T(8,128)(2,1)S(1)} %get-tuple-element.31), channel_id=1, source_target_pairs={{0,24},{8,16},{16,8},{24,0},{1,25},{9,17},{17,9},{25,1},{2,26},{10... | collective-permute-start | bytes 258056 | tf_op jit(solution)/shard_map/ppermute | solution.py:247
  22.3 4.9 %collective-permute-start.7 = (bf16[112,384]{1,0:T(8,128)(2,1)S(1)}, bf16[112,384]{1,0:T(8,128)(2,1)S(1)}, u32[]{:S(2)}, u32[]{:S(2)}) collective-permute-start(bf16[112,384]{1,0:T(8,128)(2,1)S(1)} %get-tuple-element.32), channel_id=1, source_target_pairs={{0,8},{8,0},{16,24},{24,16},{1,9},{9,1},{17,25},{25,17},{2,10},{10... | collective-permute-start | bytes 258056 | tf_op jit(solution)/shard_map/ppermute | solution.py:247
  23.8 4.5 %collective-permute-start.8 = (bf16[112,384]{1,0:T(8,128)(2,1)S(1)}, bf16[112,384]{1,0:T(8,128)(2,1)S(1)}, u32[]{:S(2)}, u32[]{:S(2)}) collective-permute-start(bf16[112,384]{1,0:T(8,128)(2,1)S(1)} %get-tuple-element.33), channel_id=1, source_target_pairs={{0,16},{8,24},{16,0},{24,8},{1,17},{9,25},{17,1},{25,9},{2,18},{10... | collective-permute-start | bytes 258056 | tf_op jit(solution)/shard_map/ppermute | solution.py:247
  24.3 8.5 %copy-start = (bf16[432,384]{1,0:T(8,128)(2,1)S(1)}, bf16[432,384]{1,0:T(8,128)(2,1)}, u32[]{:S(2)}) copy-start(bf16[432,384]{1,0:T(8,128)(2,1)} %refs_3_.1) | copy-start | bytes 995332
  28.4 7.6 %collective-permute-start.11 = (bf16[112,384]{1,0:T(8,128)(2,1)S(1)}, bf16[112,384]{1,0:T(8,128)(2,1)S(1)}, u32[]{:S(2)}, u32[]{:S(2)}) collective-permute-start(bf16[112,384]{1,0:T(8,128)(2,1)S(1)} %add_convert_fusion), channel_id=1, source_target_pairs={{0,6},{2,4},{4,2},{6,0},{1,7},{3,5},{5,3},{7,1},{8,14},{10,12},{12... | collective-permute-start | bytes 258056 | tf_op jit(solution)/shard_map/ppermute | solution.py:247
  31.4 4.6 %collective-permute-start.10 = (bf16[112,384]{1,0:T(8,128)(2,1)S(1)}, bf16[112,384]{1,0:T(8,128)(2,1)S(1)}, u32[]{:S(2)}, u32[]{:S(2)}) collective-permute-start(bf16[112,384]{1,0:T(8,128)(2,1)S(1)} %add_convert_fusion), channel_id=1, source_target_pairs={{0,2},{2,0},{4,6},{6,4},{1,3},{3,1},{5,7},{7,5},{8,10},{10,8},{12,... | collective-permute-start | bytes 258056 | tf_op jit(solution)/shard_map/ppermute | solution.py:247
  31.4 5.4 %collective-permute-start.9 = (bf16[112,384]{1,0:T(8,128)(2,1)S(1)}, bf16[112,384]{1,0:T(8,128)(2,1)S(1)}, u32[]{:S(2)}, u32[]{:S(2)}) collective-permute-start(bf16[112,384]{1,0:T(8,128)(2,1)S(1)} %add_convert_fusion), channel_id=1, source_target_pairs={{0,4},{2,6},{4,0},{6,2},{1,5},{3,7},{5,1},{7,3},{8,12},{10,14},{12... | collective-permute-start | bytes 258056 | tf_op jit(solution)/shard_map/ppermute | solution.py:247
  36.8 5.5 %collective-permute-start.14 = (bf16[112,384]{1,0:T(8,128)(2,1)S(1)}, bf16[112,384]{1,0:T(8,128)(2,1)S(1)}, u32[]{:S(2)}, u32[]{:S(2)}) collective-permute-start(bf16[112,384]{1,0:T(8,128)(2,1)S(1)} %multiply_convert_fusion.refs_0_), channel_id=1, source_target_pairs={{0,24},{8,16},{16,8},{24,0},{1,25},{9,17},{17,9},{25,1},{2,26},{10... | collective-permute-start | bytes 258056 | tf_op jit(solution)/shard_map/ppermute | solution.py:247
  37.8 5.4 %collective-permute-start.13 = (bf16[112,384]{1,0:T(8,128)(2,1)S(1)}, bf16[112,384]{1,0:T(8,128)(2,1)S(1)}, u32[]{:S(2)}, u32[]{:S(2)}) collective-permute-start(bf16[112,384]{1,0:T(8,128)(2,1)S(1)} %multiply_convert_fusion.refs_0_), channel_id=1, source_target_pairs={{0,16},{8,24},{16,0},{24,8},{1,17},{9,25},{17,1},{25,9},{2,18},{10... | collective-permute-start | bytes 258056 | tf_op jit(solution)/shard_map/ppermute | solution.py:247
  39.0 4.5 %collective-permute-start.12 = (bf16[112,384]{1,0:T(8,128)(2,1)S(1)}, bf16[112,384]{1,0:T(8,128)(2,1)S(1)}, u32[]{:S(2)}, u32[]{:S(2)}) collective-permute-start(bf16[112,384]{1,0:T(8,128)(2,1)S(1)} %multiply_convert_fusion.refs_0_), channel_id=1, source_target_pairs={{0,8},{8,0},{16,24},{24,16},{1,9},{9,1},{17,25},{25,17},{2,10},{10... | collective-permute-start | bytes 258056 | tf_op jit(solution)/shard_map/ppermute | solution.py:247

commit v5 on v4

--- a/solution.py
+++ b/solution.py
@@ -150,10 +150,14 @@
     return turned
 
 
-def fill_cols(z, turned, frame, cols_ref):
+def fill_cols(z, turned, frame, cols_ref, me=None):
     for tap in range(z.n_time * z.piece_taps):
-        start = slot_start(z, tap // z.piece_taps) + tap % z.piece_taps * z.latent
-        here = pl.ds(pl.multiple_of(start, z.latent), z.latent)
+        if me is None:
+            start = slot_start(z, tap // z.piece_taps) + tap % z.piece_taps * z.latent
+            here = pl.ds(pl.multiple_of(start, z.latent), z.latent)
+        else:
+            start = (tap // z.piece_taps ^ me) * z.piece + tap % z.piece_taps * z.latent
+            here = slice(start, start + z.latent)
         if tap >= TAPS:
             cols_ref[here, :] = jnp.zeros((z.latent, z.rows * LANES), jnp.bfloat16)
             continue
@@ -168,14 +172,22 @@
 def weight_kernel(z, *refs):
     moved_refs, (sort_ref, place_ref, act_ref) = refs[: z.n_rows], refs[z.n_rows : z.n_rows + 3]
     out_refs, cols_refs, held_ref = refs[z.n_rows + 3 : -1 - z.frames], refs[-1 - z.frames : -1], refs[-1]
-    turned = turned_grid(z, moved_refs, sort_ref, place_ref, held_ref)
-    total = 0.0
-    for frame, cols_ref in enumerate(cols_refs):
-        fill_cols(z, turned, frame, cols_ref)
-        act = act_ref[frame * z.rows * LANES : (frame + 1) * z.rows * LANES, :]
-        total = total + jnp.dot(cols_ref[z.piece :, :], act, preferred_element_type=jnp.float32)
-    for step, ref in enumerate(out_refs):
-        ref[...] = total[step * z.piece : (step + 1) * z.piece].astype(jnp.bfloat16)
+
+    def term(me=None):
+        turned = turned_grid(z, moved_refs, sort_ref, place_ref, held_ref)
+        total = 0.0
+        for frame, cols_ref in enumerate(cols_refs):
+            fill_cols(z, turned, frame, cols_ref, me)
+            act = act_ref[frame * z.rows * LANES : (frame + 1) * z.rows * LANES, :]
+            total = total + jnp.dot(cols_ref[z.piece :, :], act, preferred_element_type=jnp.float32)
+        for step, ref in enumerate(out_refs):
+            ref[...] = total[step * z.piece : (step + 1) * z.piece].astype(jnp.bfloat16)
+
+    if z.n_time > 4:
+        term()
+        return
+    for me in range(z.n_time):
+        pl.when(lax.axis_index("tm") == me)(functools.partial(term, me))
 
 
 def own_kernel(z, *refs):

time: 44.5 us -> 44.2 us (level)
  no operation moved by 1% of the time
where the time goes in v5:
time: 44.2 us; the launch traced here: 44 us
  starting transfers between devices  20.6 us (47%)
  waiting for transfers between devices  13.6 us (31%)
  Pallas kernels  9 us (20%)
  between operations  0.69 us (2%)
    ppermute x15, starting transfers between devices, exchange(): lax.ppermute(value, axis, [(i, i ^ step) for i in range(size)])  20.6 us
    ppermute x15, waiting for transfers between devices, exchange(): lax.ppermute(value, axis, [(i, i ^ step) for i in range(size)])  13.6 us
    pallas_call x1, Pallas kernels, shards(): pl.pallas_call(functools.partial(features_kernel, z), out_shape=jax.Shape...  3.11 us
    pallas_call x1, Pallas kernels, shards(): pl.pallas_call(functools.partial(prepare_kernel, z), out_shape=[jax.Shape...  2.46 us
    pallas_call x1, Pallas kernels, shards(): pl.pallas_call(functools.partial(weight_kernel, z), out_shape=[jax.ShapeD...  1.79 us
  transfers between devices with their start and end apart: 15, of which 12 were waited for; matrix products, arithmetic and copies ran while one was open for 0% of the time, Pallas kernels for 14%

profile of v5, /device:TPU:0, one launch (start us, length us, event | category | flops | bytes accessed | tf_op | source)
XLA Modules:
  0.0 44.0 jit_solution(13321611703038814191)
XLA Ops:
  0.6 4.0 %collective-permute-start.2 = (bf16[16,2304]{1,0:T(8,128)(2,1)}, bf16[16,2304]{1,0:T(8,128)(2,1)S(1)}, u32[]{:S(2)}, u32[]{:S(2)}) collective-permute-start(bf16[16,2304]{1,0:T(8,128)(2,1)} %bitcast.5), channel_id=1, source_target_pairs={{0,24},{8,16},{16,8},{24,0},{1,25},{9,17},{17,9},{25,1},{2,26},{10... | collective-permute-start | bytes 221192 | tf_op jit(solution)/shard_map/ppermute | solution.py:259
  4.6 0.5 %collective-permute-start.1 = (bf16[16,2304]{1,0:T(8,128)(2,1)}, bf16[16,2304]{1,0:T(8,128)(2,1)S(1)}, u32[]{:S(2)}, u32[]{:S(2)}) collective-permute-start(bf16[16,2304]{1,0:T(8,128)(2,1)} %bitcast.6), channel_id=1, source_target_pairs={{0,16},{8,24},{16,0},{24,8},{1,17},{9,25},{17,1},{25,9},{2,18},{10... | collective-permute-start | bytes 221192 | tf_op jit(solution)/shard_map/ppermute | solution.py:259
  5.1 0.1 collective-permute-start
  5.2 2.5 %act_and_slope.1 = (bf16[3072,384]{1,0:T(8,128)(2,1)S(1)}, f32[2304,384]{1,0:T(8,128)S(1)}, bf16[256,256]{1,0:T(8,128)(2,1)S(1)}, bf16[1024,1024]{1,0:T(8,128)(2,1)S(1)}, bf16[16,2304]{1,0:T(8,128)(2,1)S(1)}) custom-call(bf16[2304,384]{1,0:T(8,128)(2,1)} %bitcast.3, bf16[256,256]{1,0:T(8,128)(2,1)} %constant.6.clone.sort_ref, ...), custom_call_target="tpu_custom_call" | custom-call | flops 8847360 | bytes 7962624 | tf_op jit(solution)/shard_map/act_and_slope/pallas_call | solution.py:284
  7.7 0.0 collective-permute-done.2.refs_3_
  7.7 1.4 %collective-permute-done.1.refs_2_ = bf16[16,2304]{1,0:T(8,128)(2,1)S(1)} collective-permute-done((bf16[16,2304]{1,0:T(8,128)(2,1)}, bf16[16,2304]{1,0:T(8,128)(2,1)S(1)}, u32[]{:S(2)}, u32[]{:S(2)}) %collective-permute-start.1) | collective-permute-done | bytes 73760 | tf_op jit(solution)/shard_map/ppermute | solution.py:259
  9.2 0.5 %collective-permute-done.refs_1_ = bf16[16,2304]{1,0:T(8,128)(2,1)S(1)} collective-permute-done((bf16[16,2304]{1,0:T(8,128)(2,1)}, bf16[16,2304]{1,0:T(8,128)(2,1)S(1)}, u32[]{:S(2)}, u32[]{:S(2)}) %collective-permute-start) | collective-permute-done | bytes 73760 | tf_op jit(solution)/shard_map/ppermute | solution.py:259
  9.7 0.2 latent_windows.1
  9.9 3.7 %collective-permute-start.3 = (bf16[4,64,128]{2,1,0:T(8,128)(2,1)S(1)}, bf16[4,64,128]{2,1,0:T(8,128)(2,1)S(1)}, u32[]{:S(2)}, u32[]{:S(2)}) collective-permute-start(bf16[4,64,128]{2,1,0:T(8,128)(2,1)S(1)} %get-tuple-element.23), channel_id=1, source_target_pairs={{0,6},{2,4},{4,2},{6,0},{1,7},{3,5},{5,3},{7,1},{8,14},{10,12},{12... | collective-permute-start | bytes 196616 | tf_op jit(solution)/shard_map/ppermute | solution.py:259
  13.5 0.0 collective-permute-start.4
  13.6 0.8 %collective-permute-start.5 = (bf16[4,64,128]{2,1,0:T(8,128)(2,1)S(1)}, bf16[4,64,128]{2,1,0:T(8,128)(2,1)S(1)}, u32[]{:S(2)}, u32[]{:S(2)}) collective-permute-start(bf16[4,64,128]{2,1,0:T(8,128)(2,1)S(1)} %get-tuple-element.25), channel_id=1, source_target_pairs={{0,4},{2,6},{4,0},{6,2},{1,5},{3,7},{5,1},{7,3},{8,12},{10,14},{12... | collective-permute-start | bytes 196616 | tf_op jit(solution)/shard_map/ppermute | solution.py:259
  14.3 1.8 %collective-permute-done.3.refs_1_ = bf16[4,64,128]{2,1,0:T(8,128)(2,1)S(1)} collective-permute-done((bf16[4,64,128]{2,1,0:T(8,128)(2,1)S(1)}, bf16[4,64,128]{2,1,0:T(8,128)(2,1)S(1)}, u32[]{:S(2)}, u32[]{:S(2)}) %collective-permute-start.3) | collective-permute-done | bytes 65568 | tf_op jit(solution)/shard_map/ppermute | solution.py:259
  16.1 1.7 %collective-permute-done.4.refs_2_ = bf16[4,64,128]{2,1,0:T(8,128)(2,1)S(1)} collective-permute-done((bf16[4,64,128]{2,1,0:T(8,128)(2,1)S(1)}, bf16[4,64,128]{2,1,0:T(8,128)(2,1)S(1)}, u32[]{:S(2)}, u32[]{:S(2)}) %collective-permute-start.4) | collective-permute-done | bytes 65568 | tf_op jit(solution)/shard_map/ppermute | solution.py:259
  17.8 0.9 %collective-permute-done.5.refs_3_ = bf16[4,64,128]{2,1,0:T(8,128)(2,1)S(1)} collective-permute-done((bf16[4,64,128]{2,1,0:T(8,128)(2,1)S(1)}, bf16[4,64,128]{2,1,0:T(8,128)(2,1)S(1)}, u32[]{:S(2)}, u32[]{:S(2)}) %collective-permute-start.5) | collective-permute-done | bytes 65568 | tf_op jit(solution)/shard_map/ppermute | solution.py:259
  18.7 1.8 %weight_term.1 = (bf16[112,384]{1,0:T(8,128)(2,1)S(1)}, bf16[112,384]{1,0:T(8,128)(2,1)S(1)}, bf16[112,384]{1,0:T(8,128)(2,1)S(1)}, bf16[448,1536]{1,0:T(8,128)(2,1)S(1)}, bf16[448,1536]{1,0:T(8,128)(2,1)S(1)}) custom-call(bf16[4,64,128]{2,1,0:T(8,128)(2,1)S(1)} %get-tuple-element.22.refs_0_, bf16[4,64,128]{2,1,0:T(8,128)(2,1)S(1)} %collective-permute-done.3.refs_1_, ...), custom_call_target="tpu_custom_call" | custom-call | flops 1056964608 | bytes 3538944 | tf_op jit(solution)/shard_map/weight_term/pallas_call | solution.py:310
  20.5 1.6 %collective-permute-start.6 = (bf16[112,384]{1,0:T(8,128)(2,1)S(1)}, bf16[112,384]{1,0:T(8,128)(2,1)S(1)}, u32[]{:S(2)}, u32[]{:S(2)}) collective-permute-start(bf16[112,384]{1,0:T(8,128)(2,1)S(1)} %get-tuple-element.31), channel_id=1, source_target_pairs={{0,24},{8,16},{16,8},{24,0},{1,25},{9,17},{17,9},{25,1},{2,26},{10... | collective-permute-start | bytes 258056 | tf_op jit(solution)/shard_map/ppermute | solution.py:259
  22.1 1.5 %collective-permute-start.7 = (bf16[112,384]{1,0:T(8,128)(2,1)S(1)}, bf16[112,384]{1,0:T(8,128)(2,1)S(1)}, u32[]{:S(2)}, u32[]{:S(2)}) collective-permute-start(bf16[112,384]{1,0:T(8,128)(2,1)S(1)} %get-tuple-element.32), channel_id=1, source_target_pairs={{0,8},{8,0},{16,24},{24,16},{1,9},{9,1},{17,25},{25,17},{2,10},{10... | collective-permute-start | bytes 258056 | tf_op jit(solution)/shard_map/ppermute | solution.py:259
  23.6 0.5 %collective-permute-start.8 = (bf16[112,384]{1,0:T(8,128)(2,1)S(1)}, bf16[112,384]{1,0:T(8,128)(2,1)S(1)}, u32[]{:S(2)}, u32[]{:S(2)}) collective-permute-start(bf16[112,384]{1,0:T(8,128)(2,1)S(1)} %get-tuple-element.33), channel_id=1, source_target_pairs={{0,16},{8,24},{16,0},{24,8},{1,17},{9,25},{17,1},{25,9},{2,18},{10... | collective-permute-start | bytes 258056 | tf_op jit(solution)/shard_map/ppermute | solution.py:259
  24.1 0.0 copy-start
  24.1 0.5 %own_piece.1 = f32[112,384]{1,0:T(8,128)S(1)} custom-call(bf16[448,1536]{1,0:T(8,128)(2,1)S(1)} %get-tuple-element.35.refs_0_, bf16[448,1536]{1,0:T(8,128)(2,1)S(1)} %get-tuple-element.36.refs_1_, bf16[3072,384]{1,0:T(8,128)(2,1)S(1)} %get-tuple-element.28.refs_6_.refs_2_), custom_call_target="tpu_custom_call" | custom-call | flops 264241152 | bytes 1769472 | tf_op jit(solution)/shard_map/own_piece/pallas_call | solution.py:321
  24.6 1.3 %collective-permute-done.6 = bf16[112,384]{1,0:T(8,128)(2,1)S(1)} collective-permute-done((bf16[112,384]{1,0:T(8,128)(2,1)S(1)}, bf16[112,384]{1,0:T(8,128)(2,1)S(1)}, u32[]{:S(2)}, u32[]{:S(2)}) %collective-permute-start.6) | collective-permute-done | bytes 86048 | tf_op jit(solution)/shard_map/ppermute | solution.py:259
  26.0 1.0 %collective-permute-done.7 = bf16[112,384]{1,0:T(8,128)(2,1)S(1)} collective-permute-done((bf16[112,384]{1,0:T(8,128)(2,1)S(1)}, bf16[112,384]{1,0:T(8,128)(2,1)S(1)}, u32[]{:S(2)}, u32[]{:S(2)}) %collective-permute-start.7) | collective-permute-done | bytes 86048 | tf_op jit(solution)/shard_map/ppermute | solution.py:259
  26.9 1.1 %collective-permute-done.8 = bf16[112,384]{1,0:T(8,128)(2,1)S(1)} collective-permute-done((bf16[112,384]{1,0:T(8,128)(2,1)S(1)}, bf16[112,384]{1,0:T(8,128)(2,1)S(1)}, u32[]{:S(2)}, u32[]{:S(2)}) %collective-permute-start.8) | collective-permute-done | bytes 86048 | tf_op jit(solution)/shard_map/ppermute | solution.py:259
  28.1 3.0 %collective-permute-start.11 = (bf16[112,384]{1,0:T(8,128)(2,1)S(1)}, bf16[112,384]{1,0:T(8,128)(2,1)S(1)}, u32[]{:S(2)}, u32[]{:S(2)}) collective-permute-start(bf16[112,384]{1,0:T(8,128)(2,1)S(1)} %add_convert_fusion), channel_id=1, source_target_pairs={{0,6},{2,4},{4,2},{6,0},{1,7},{3,5},{5,3},{7,1},{8,14},{10,12},{12... | collective-permute-start | bytes 258056 | tf_op jit(solution)/shard_map/ppermute | solution.py:259
  31.1 0.0 collective-permute-start.10
  31.1 1.5 %collective-permute-start.9 = (bf16[112,384]{1,0:T(8,128)(2,1)S(1)}, bf16[112,384]{1,0:T(8,128)(2,1)S(1)}, u32[]{:S(2)}, u32[]{:S(2)}) collective-permute-start(bf16[112,384]{1,0:T(8,128)(2,1)S(1)} %add_convert_fusion), channel_id=1, source_target_pairs={{0,4},{2,6},{4,0},{6,2},{1,5},{3,7},{5,1},{7,3},{8,12},{10,14},{12... | collective-permute-start | bytes 258056 | tf_op jit(solution)/shard_map/ppermute | solution.py:259
  32.6 0.0 copy-done
  32.6 3.1 %features_grad.1 = bf16[2304,384]{1,0:T(8,128)(2,1)} custom-call(bf16[448,1536]{1,0:T(8,128)(2,1)S(1)} %get-tuple-element.35.refs_0_, bf16[448,1536]{1,0:T(8,128)(2,1)S(1)} %get-tuple-element.36.refs_1_, f32[2304,384]{1,0:T(8,128)S(1)} %get-tuple-element.37.refs_2_, bf16[432,384]{1,0:T(8,128)(2,1)S(1)} %copy-done), custom_call_target="tpu_custom_call" | custom-call | flops 1056964608 | bytes 7077888 | tf_op jit(solution)/shard_map/features_grad/pallas_call | solution.py:334
  35.7 0.0 collective-permute-done.11
  35.7 0.0 collective-permute-done.10
  35.7 0.8 %collective-permute-done.9 = bf16[112,384]{1,0:T(8,128)(2,1)S(1)} collective-permute-done((bf16[112,384]{1,0:T(8,128)(2,1)S(1)}, bf16[112,384]{1,0:T(8,128)(2,1)S(1)}, u32[]{:S(2)}, u32[]{:S(2)}) %collective-permute-start.9) | collective-permute-done | bytes 86048 | tf_op jit(solution)/shard_map/ppermute | solution.py:259
  36.5 0.1 multiply_convert_fusion.refs_0_
  36.6 1.0 %collective-permute-start.14 = (bf16[112,384]{1,0:T(8,128)(2,1)S(1)}, bf16[112,384]{1,0:T(8,128)(2,1)S(1)}, u32[]{:S(2)}, u32[]{:S(2)}) collective-permute-start(bf16[112,384]{1,0:T(8,128)(2,1)S(1)} %multiply_convert_fusion.refs_0_), channel_id=1, source_target_pairs={{0,24},{8,16},{16,8},{24,0},{1,25},{9,17},{17,9},{25,1},{2,26},{10... | collective-permute-start | bytes 258056 | tf_op jit(solution)/shard_map/ppermute | solution.py:259
  37.6 1.1 %collective-permute-start.13 = (bf16[112,384]{1,0:T(8,128)(2,1)S(1)}, bf16[112,384]{1,0:T(8,128)(2,1)S(1)}, u32[]{:S(2)}, u32[]{:S(2)}) collective-permute-start(bf16[112,384]{1,0:T(8,128)(2,1)S(1)} %multiply_convert_fusion.refs_0_), channel_id=1, source_target_pairs={{0,16},{8,24},{16,0},{24,8},{1,17},{9,25},{17,1},{25,9},{2,18},{10... | collective-permute-start | bytes 258056 | tf_op jit(solution)/shard_map/ppermute | solution.py:259
  38.7 1.4 %collective-permute-start.12 = (bf16[112,384]{1,0:T(8,128)(2,1)S(1)}, bf16[112,384]{1,0:T(8,128)(2,1)S(1)}, u32[]{:S(2)}, u32[]{:S(2)}) collective-permute-start(bf16[112,384]{1,0:T(8,128)(2,1)S(1)} %multiply_convert_fusion.refs_0_), channel_id=1, source_target_pairs={{0,8},{8,0},{16,24},{24,16},{1,9},{9,1},{17,25},{25,17},{2,10},{10... | collective-permute-start | bytes 258056 | tf_op jit(solution)/shard_map/ppermute | solution.py:259
  40.1 2.0 %collective-permute-done.14.refs_3_ = bf16[112,384]{1,0:T(8,128)(2,1)S(1)} collective-permute-done((bf16[112,384]{1,0:T(8,128)(2,1)S(1)}, bf16[112,384]{1,0:T(8,128)(2,1)S(1)}, u32[]{:S(2)}, u32[]{:S(2)}) %collective-permute-start.14) | collective-permute-done | bytes 86048 | tf_op jit(solution)/shard_map/ppermute | solution.py:259
  42.1 0.8 %collective-permute-done.13.refs_2_ = bf16[112,384]{1,0:T(8,128)(2,1)S(1)} collective-permute-done((bf16[112,384]{1,0:T(8,128)(2,1)S(1)}, bf16[112,384]{1,0:T(8,128)(2,1)S(1)}, u32[]{:S(2)}, u32[]{:S(2)}) %collective-permute-start.13) | collective-permute-done | bytes 86048 | tf_op jit(solution)/shard_map/ppermute | solution.py:259
  42.9 0.2 collective-permute-done.12.refs_1_
  43.2 0.9 %join_pieces.1 = f32[432,384]{1,0:T(8,128)} custom-call(bf16[112,384]{1,0:T(8,128)(2,1)S(1)} %multiply_convert_fusion.refs_0_, bf16[112,384]{1,0:T(8,128)(2,1)S(1)} %collective-permute-done.12.refs_1_, bf16[112,384]{1,0:T(8,128)(2,1)S(1)} %collective-permute-done.13.refs_2_, bf16[112,384]{1,0:T(8,128)(2,1)S(1)} %collective-permute-done.14.refs_3_), custom_call_target="tpu_custom_call" | custom-call | tf_op jit(solution)/shard_map/join_pieces/pallas_call | solution.py:348
  (1 shorter events, 0.0 us)
Async XLA Ops:
  0.6 7.1 %collective-permute-start.2 = (bf16[16,2304]{1,0:T(8,128)(2,1)}, bf16[16,2304]{1,0:T(8,128)(2,1)S(1)}, u32[]{:S(2)}, u32[]{:S(2)}) collective-permute-start(bf16[16,2304]{1,0:T(8,128)(2,1)} %bitcast.5), channel_id=1, source_target_pairs={{0,24},{8,16},{16,8},{24,0},{1,25},{9,17},{17,9},{25,1},{2,26},{10... | collective-permute-start | bytes 221192 | tf_op jit(solution)/shard_map/ppermute | solution.py:259
  4.6 4.6 %collective-permute-start.1 = (bf16[16,2304]{1,0:T(8,128)(2,1)}, bf16[16,2304]{1,0:T(8,128)(2,1)S(1)}, u32[]{:S(2)}, u32[]{:S(2)}) collective-permute-start(bf16[16,2304]{1,0:T(8,128)(2,1)} %bitcast.6), channel_id=1, source_target_pairs={{0,16},{8,24},{16,0},{24,8},{1,17},{9,25},{17,1},{25,9},{2,18},{10... | collective-permute-start | bytes 221192 | tf_op jit(solution)/shard_map/ppermute | solution.py:259
  5.1 4.6 %collective-permute-start = (bf16[16,2304]{1,0:T(8,128)(2,1)}, bf16[16,2304]{1,0:T(8,128)(2,1)S(1)}, u32[]{:S(2)}, u32[]{:S(2)}) collective-permute-start(bf16[16,2304]{1,0:T(8,128)(2,1)} %bitcast.7), channel_id=1, source_target_pairs={{0,8},{8,0},{16,24},{24,16},{1,9},{9,1},{17,25},{25,17},{2,10},{10... | collective-permute-start | bytes 221192 | tf_op jit(solution)/shard_map/ppermute | solution.py:259
  9.9 6.3 %collective-permute-start.3 = (bf16[4,64,128]{2,1,0:T(8,128)(2,1)S(1)}, bf16[4,64,128]{2,1,0:T(8,128)(2,1)S(1)}, u32[]{:S(2)}, u32[]{:S(2)}) collective-permute-start(bf16[4,64,128]{2,1,0:T(8,128)(2,1)S(1)} %get-tuple-element.23), channel_id=1, source_target_pairs={{0,6},{2,4},{4,2},{6,0},{1,7},{3,5},{5,3},{7,1},{8,14},{10,12},{12... | collective-permute-start | bytes 196616 | tf_op jit(solution)/shard_map/ppermute | solution.py:259
  13.5 4.3 %collective-permute-start.4 = (bf16[4,64,128]{2,1,0:T(8,128)(2,1)S(1)}, bf16[4,64,128]{2,1,0:T(8,128)(2,1)S(1)}, u32[]{:S(2)}, u32[]{:S(2)}) collective-permute-start(bf16[4,64,128]{2,1,0:T(8,128)(2,1)S(1)} %get-tuple-element.24), channel_id=1, source_target_pairs={{0,2},{2,0},{4,6},{6,4},{1,3},{3,1},{5,7},{7,5},{8,10},{10,8},{12,... | collective-permute-start | bytes 196616 | tf_op jit(solution)/shard_map/ppermute | solution.py:259
  13.6 5.2 %collective-permute-start.5 = (bf16[4,64,128]{2,1,0:T(8,128)(2,1)S(1)}, bf16[4,64,128]{2,1,0:T(8,128)(2,1)S(1)}, u32[]{:S(2)}, u32[]{:S(2)}) collective-permute-start(bf16[4,64,128]{2,1,0:T(8,128)(2,1)S(1)} %get-tuple-element.25), channel_id=1, source_target_pairs={{0,4},{2,6},{4,0},{6,2},{1,5},{3,7},{5,1},{7,3},{8,12},{10,14},{12... | collective-permute-start | bytes 196616 | tf_op jit(solution)/shard_map/ppermute | solution.py:259
  20.5 5.4 %collective-permute-start.6 = (bf16[112,384]{1,0:T(8,128)(2,1)S(1)}, bf16[112,384]{1,0:T(8,128)(2,1)S(1)}, u32[]{:S(2)}, u32[]{:S(2)}) collective-permute-start(bf16[112,384]{1,0:T(8,128)(2,1)S(1)} %get-tuple-element.31), channel_id=1, source_target_pairs={{0,24},{8,16},{16,8},{24,0},{1,25},{9,17},{17,9},{25,1},{2,26},{10... | collective-permute-start | bytes 258056 | tf_op jit(solution)/shard_map/ppermute | solution.py:259
  22.1 4.9 %collective-permute-start.7 = (bf16[112,384]{1,0:T(8,128)(2,1)S(1)}, bf16[112,384]{1,0:T(8,128)(2,1)S(1)}, u32[]{:S(2)}, u32[]{:S(2)}) collective-permute-start(bf16[112,384]{1,0:T(8,128)(2,1)S(1)} %get-tuple-element.32), channel_id=1, source_target_pairs={{0,8},{8,0},{16,24},{24,16},{1,9},{9,1},{17,25},{25,17},{2,10},{10... | collective-permute-start | bytes 258056 | tf_op jit(solution)/shard_map/ppermute | solution.py:259
  23.6 4.5 %collective-permute-start.8 = (bf16[112,384]{1,0:T(8,128)(2,1)S(1)}, bf16[112,384]{1,0:T(8,128)(2,1)S(1)}, u32[]{:S(2)}, u32[]{:S(2)}) collective-permute-start(bf16[112,384]{1,0:T(8,128)(2,1)S(1)} %get-tuple-element.33), channel_id=1, source_target_pairs={{0,16},{8,24},{16,0},{24,8},{1,17},{9,25},{17,1},{25,9},{2,18},{10... | collective-permute-start | bytes 258056 | tf_op jit(solution)/shard_map/ppermute | solution.py:259
  24.1 8.5 %copy-start = (bf16[432,384]{1,0:T(8,128)(2,1)S(1)}, bf16[432,384]{1,0:T(8,128)(2,1)}, u32[]{:S(2)}) copy-start(bf16[432,384]{1,0:T(8,128)(2,1)} %refs_3_.1) | copy-start | bytes 995332
  28.1 7.6 %collective-permute-start.11 = (bf16[112,384]{1,0:T(8,128)(2,1)S(1)}, bf16[112,384]{1,0:T(8,128)(2,1)S(1)}, u32[]{:S(2)}, u32[]{:S(2)}) collective-permute-start(bf16[112,384]{1,0:T(8,128)(2,1)S(1)} %add_convert_fusion), channel_id=1, source_target_pairs={{0,6},{2,4},{4,2},{6,0},{1,7},{3,5},{5,3},{7,1},{8,14},{10,12},{12... | collective-permute-start | bytes 258056 | tf_op jit(solution)/shard_map/ppermute | solution.py:259
  31.1 4.6 %collective-permute-start.10 = (bf16[112,384]{1,0:T(8,128)(2,1)S(1)}, bf16[112,384]{1,0:T(8,128)(2,1)S(1)}, u32[]{:S(2)}, u32[]{:S(2)}) collective-permute-start(bf16[112,384]{1,0:T(8,128)(2,1)S(1)} %add_convert_fusion), channel_id=1, source_target_pairs={{0,2},{2,0},{4,6},{6,4},{1,3},{3,1},{5,7},{7,5},{8,10},{10,8},{12,... | collective-permute-start | bytes 258056 | tf_op jit(solution)/shard_map/ppermute | solution.py:259
  31.1 5.4 %collective-permute-start.9 = (bf16[112,384]{1,0:T(8,128)(2,1)S(1)}, bf16[112,384]{1,0:T(8,128)(2,1)S(1)}, u32[]{:S(2)}, u32[]{:S(2)}) collective-permute-start(bf16[112,384]{1,0:T(8,128)(2,1)S(1)} %add_convert_fusion), channel_id=1, source_target_pairs={{0,4},{2,6},{4,0},{6,2},{1,5},{3,7},{5,1},{7,3},{8,12},{10,14},{12... | collective-permute-start | bytes 258056 | tf_op jit(solution)/shard_map/ppermute | solution.py:259
  36.6 5.5 %collective-permute-start.14 = (bf16[112,384]{1,0:T(8,128)(2,1)S(1)}, bf16[112,384]{1,0:T(8,128)(2,1)S(1)}, u32[]{:S(2)}, u32[]{:S(2)}) collective-permute-start(bf16[112,384]{1,0:T(8,128)(2,1)S(1)} %multiply_convert_fusion.refs_0_), channel_id=1, source_target_pairs={{0,24},{8,16},{16,8},{24,0},{1,25},{9,17},{17,9},{25,1},{2,26},{10... | collective-permute-start | bytes 258056 | tf_op jit(solution)/shard_map/ppermute | solution.py:259
  37.6 5.3 %collective-permute-start.13 = (bf16[112,384]{1,0:T(8,128)(2,1)S(1)}, bf16[112,384]{1,0:T(8,128)(2,1)S(1)}, u32[]{:S(2)}, u32[]{:S(2)}) collective-permute-start(bf16[112,384]{1,0:T(8,128)(2,1)S(1)} %multiply_convert_fusion.refs_0_), channel_id=1, source_target_pairs={{0,16},{8,24},{16,0},{24,8},{1,17},{9,25},{17,1},{25,9},{2,18},{10... | collective-permute-start | bytes 258056 | tf_op jit(solution)/shard_map/ppermute | solution.py:259
  38.7 4.5 %collective-permute-start.12 = (bf16[112,384]{1,0:T(8,128)(2,1)S(1)}, bf16[112,384]{1,0:T(8,128)(2,1)S(1)}, u32[]{:S(2)}, u32[]{:S(2)}) collective-permute-start(bf16[112,384]{1,0:T(8,128)(2,1)S(1)} %multiply_convert_fusion.refs_0_), channel_id=1, source_target_pairs={{0,8},{8,0},{16,24},{24,16},{1,9},{9,1},{17,25},{25,17},{2,10},{10... | collective-permute-start | bytes 258056 | tf_op jit(solution)/shard_map/ppermute | solution.py:259

commit v6 on v5

--- a/solution.py
+++ b/solution.py
@@ -242,6 +242,23 @@
         if tail:
             pl.when(place == whole)(functools.partial(copy, tail))
 
+    def fixed(index):
+        copies = []
+        for step, ref in enumerate(piece_refs):
+            held_ref[step] = ref[...].astype(jnp.float32)
+            first = (index ^ step) * z.piece
+            count = max(0, min(z.piece, TAPS * z.latent - first))
+            if count:
+                source, target = held_ref.at[step, pl.ds(0, count)], out_ref.at[pl.ds(first, count)]
+                copies.append(pltpu.make_async_copy(source, target, sems.at[step]))
+                copies[-1].start()
+        for copy in copies:
+            copy.wait()
+
+    if z.n_time <= 4:
+        for index in range(z.n_time):
+            pl.when(me == index)(functools.partial(fixed, index))
+        return
     for step, ref in enumerate(piece_refs):
         held_ref[step] = ref[...].astype(jnp.float32)
         each(step, lambda copy: copy.start())

time: 44.2 us -> 44.2 us (level)
  no operation moved by 1% of the time
where the time goes in v6:
time: 44.2 us; the launch traced here: 44 us
  starting transfers between devices  20.6 us (47%)
  waiting for transfers between devices  13.6 us (31%)
  Pallas kernels  9 us (20%)
  between operations  0.69 us (2%)
    ppermute x15, starting transfers between devices, exchange(): lax.ppermute(value, axis, [(i, i ^ step) for i in range(size)])  20.6 us
    ppermute x15, waiting for transfers between devices, exchange(): lax.ppermute(value, axis, [(i, i ^ step) for i in range(size)])  13.6 us
    pallas_call x1, Pallas kernels, shards(): pl.pallas_call(functools.partial(features_kernel, z), out_shape=jax.Shape...  3.11 us
    pallas_call x1, Pallas kernels, shards(): pl.pallas_call(functools.partial(prepare_kernel, z), out_shape=[jax.Shape...  2.46 us
    pallas_call x1, Pallas kernels, shards(): pl.pallas_call(functools.partial(weight_kernel, z), out_shape=[jax.ShapeD...  1.79 us
  transfers between devices with their start and end apart: 15, of which 12 were waited for; matrix products, arithmetic and copies ran while one was open for 0% of the time, Pallas kernels for 14%

profile of v6, /device:TPU:0, one launch (start us, length us, event | category | flops | bytes accessed | tf_op | source)
XLA Modules:
  0.0 44.0 jit_solution(9477773453111190713)
XLA Ops:
  0.6 4.0 %collective-permute-start.2 = (bf16[16,2304]{1,0:T(8,128)(2,1)}, bf16[16,2304]{1,0:T(8,128)(2,1)S(1)}, u32[]{:S(2)}, u32[]{:S(2)}) collective-permute-start(bf16[16,2304]{1,0:T(8,128)(2,1)} %bitcast.5), channel_id=1, source_target_pairs={{0,24},{8,16},{16,8},{24,0},{1,25},{9,17},{17,9},{25,1},{2,26},{10... | collective-permute-start | bytes 221192 | tf_op jit(solution)/shard_map/ppermute | solution.py:276
  4.6 0.5 %collective-permute-start.1 = (bf16[16,2304]{1,0:T(8,128)(2,1)}, bf16[16,2304]{1,0:T(8,128)(2,1)S(1)}, u32[]{:S(2)}, u32[]{:S(2)}) collective-permute-start(bf16[16,2304]{1,0:T(8,128)(2,1)} %bitcast.6), channel_id=1, source_target_pairs={{0,16},{8,24},{16,0},{24,8},{1,17},{9,25},{17,1},{25,9},{2,18},{10... | collective-permute-start | bytes 221192 | tf_op jit(solution)/shard_map/ppermute | solution.py:276
  5.1 0.1 collective-permute-start
  5.2 2.5 %act_and_slope.1 = (bf16[3072,384]{1,0:T(8,128)(2,1)S(1)}, f32[2304,384]{1,0:T(8,128)S(1)}, bf16[256,256]{1,0:T(8,128)(2,1)S(1)}, bf16[1024,1024]{1,0:T(8,128)(2,1)S(1)}, bf16[16,2304]{1,0:T(8,128)(2,1)S(1)}) custom-call(bf16[2304,384]{1,0:T(8,128)(2,1)} %bitcast.3, bf16[256,256]{1,0:T(8,128)(2,1)} %constant.6.clone.sort_ref, ...), custom_call_target="tpu_custom_call" | custom-call | flops 8847360 | bytes 7962624 | tf_op jit(solution)/shard_map/act_and_slope/pallas_call | solution.py:301
  7.7 0.0 collective-permute-done.2.refs_3_
  7.7 1.4 %collective-permute-done.1.refs_2_ = bf16[16,2304]{1,0:T(8,128)(2,1)S(1)} collective-permute-done((bf16[16,2304]{1,0:T(8,128)(2,1)}, bf16[16,2304]{1,0:T(8,128)(2,1)S(1)}, u32[]{:S(2)}, u32[]{:S(2)}) %collective-permute-start.1) | collective-permute-done | bytes 73760 | tf_op jit(solution)/shard_map/ppermute | solution.py:276
  9.2 0.5 %collective-permute-done.refs_1_ = bf16[16,2304]{1,0:T(8,128)(2,1)S(1)} collective-permute-done((bf16[16,2304]{1,0:T(8,128)(2,1)}, bf16[16,2304]{1,0:T(8,128)(2,1)S(1)}, u32[]{:S(2)}, u32[]{:S(2)}) %collective-permute-start) | collective-permute-done | bytes 73760 | tf_op jit(solution)/shard_map/ppermute | solution.py:276
  9.7 0.2 latent_windows.1
  9.9 3.7 %collective-permute-start.3 = (bf16[4,64,128]{2,1,0:T(8,128)(2,1)S(1)}, bf16[4,64,128]{2,1,0:T(8,128)(2,1)S(1)}, u32[]{:S(2)}, u32[]{:S(2)}) collective-permute-start(bf16[4,64,128]{2,1,0:T(8,128)(2,1)S(1)} %get-tuple-element.23), channel_id=1, source_target_pairs={{0,6},{2,4},{4,2},{6,0},{1,7},{3,5},{5,3},{7,1},{8,14},{10,12},{12... | collective-permute-start | bytes 196616 | tf_op jit(solution)/shard_map/ppermute | solution.py:276
  13.5 0.0 collective-permute-start.4
  13.6 0.8 %collective-permute-start.5 = (bf16[4,64,128]{2,1,0:T(8,128)(2,1)S(1)}, bf16[4,64,128]{2,1,0:T(8,128)(2,1)S(1)}, u32[]{:S(2)}, u32[]{:S(2)}) collective-permute-start(bf16[4,64,128]{2,1,0:T(8,128)(2,1)S(1)} %get-tuple-element.25), channel_id=1, source_target_pairs={{0,4},{2,6},{4,0},{6,2},{1,5},{3,7},{5,1},{7,3},{8,12},{10,14},{12... | collective-permute-start | bytes 196616 | tf_op jit(solution)/shard_map/ppermute | solution.py:276
  14.3 1.8 %collective-permute-done.3.refs_1_ = bf16[4,64,128]{2,1,0:T(8,128)(2,1)S(1)} collective-permute-done((bf16[4,64,128]{2,1,0:T(8,128)(2,1)S(1)}, bf16[4,64,128]{2,1,0:T(8,128)(2,1)S(1)}, u32[]{:S(2)}, u32[]{:S(2)}) %collective-permute-start.3) | collective-permute-done | bytes 65568 | tf_op jit(solution)/shard_map/ppermute | solution.py:276
  16.1 1.7 %collective-permute-done.4.refs_2_ = bf16[4,64,128]{2,1,0:T(8,128)(2,1)S(1)} collective-permute-done((bf16[4,64,128]{2,1,0:T(8,128)(2,1)S(1)}, bf16[4,64,128]{2,1,0:T(8,128)(2,1)S(1)}, u32[]{:S(2)}, u32[]{:S(2)}) %collective-permute-start.4) | collective-permute-done | bytes 65568 | tf_op jit(solution)/shard_map/ppermute | solution.py:276
  17.8 0.9 %collective-permute-done.5.refs_3_ = bf16[4,64,128]{2,1,0:T(8,128)(2,1)S(1)} collective-permute-done((bf16[4,64,128]{2,1,0:T(8,128)(2,1)S(1)}, bf16[4,64,128]{2,1,0:T(8,128)(2,1)S(1)}, u32[]{:S(2)}, u32[]{:S(2)}) %collective-permute-start.5) | collective-permute-done | bytes 65568 | tf_op jit(solution)/shard_map/ppermute | solution.py:276
  18.7 1.8 %weight_term.1 = (bf16[112,384]{1,0:T(8,128)(2,1)S(1)}, bf16[112,384]{1,0:T(8,128)(2,1)S(1)}, bf16[112,384]{1,0:T(8,128)(2,1)S(1)}, bf16[448,1536]{1,0:T(8,128)(2,1)S(1)}, bf16[448,1536]{1,0:T(8,128)(2,1)S(1)}) custom-call(bf16[4,64,128]{2,1,0:T(8,128)(2,1)S(1)} %get-tuple-element.22.refs_0_, bf16[4,64,128]{2,1,0:T(8,128)(2,1)S(1)} %collective-permute-done.3.refs_1_, ...), custom_call_target="tpu_custom_call" | custom-call | flops 1056964608 | bytes 3538944 | tf_op jit(solution)/shard_map/weight_term/pallas_call | solution.py:327
  20.5 1.6 %collective-permute-start.6 = (bf16[112,384]{1,0:T(8,128)(2,1)S(1)}, bf16[112,384]{1,0:T(8,128)(2,1)S(1)}, u32[]{:S(2)}, u32[]{:S(2)}) collective-permute-start(bf16[112,384]{1,0:T(8,128)(2,1)S(1)} %get-tuple-element.31), channel_id=1, source_target_pairs={{0,24},{8,16},{16,8},{24,0},{1,25},{9,17},{17,9},{25,1},{2,26},{10... | collective-permute-start | bytes 258056 | tf_op jit(solution)/shard_map/ppermute | solution.py:276
  22.1 1.5 %collective-permute-start.7 = (bf16[112,384]{1,0:T(8,128)(2,1)S(1)}, bf16[112,384]{1,0:T(8,128)(2,1)S(1)}, u32[]{:S(2)}, u32[]{:S(2)}) collective-permute-start(bf16[112,384]{1,0:T(8,128)(2,1)S(1)} %get-tuple-element.32), channel_id=1, source_target_pairs={{0,8},{8,0},{16,24},{24,16},{1,9},{9,1},{17,25},{25,17},{2,10},{10... | collective-permute-start | bytes 258056 | tf_op jit(solution)/shard_map/ppermute | solution.py:276
  23.6 0.5 %collective-permute-start.8 = (bf16[112,384]{1,0:T(8,128)(2,1)S(1)}, bf16[112,384]{1,0:T(8,128)(2,1)S(1)}, u32[]{:S(2)}, u32[]{:S(2)}) collective-permute-start(bf16[112,384]{1,0:T(8,128)(2,1)S(1)} %get-tuple-element.33), channel_id=1, source_target_pairs={{0,16},{8,24},{16,0},{24,8},{1,17},{9,25},{17,1},{25,9},{2,18},{10... | collective-permute-start | bytes 258056 | tf_op jit(solution)/shard_map/ppermute | solution.py:276
  24.1 0.0 copy-start
  24.1 0.5 %own_piece.1 = f32[112,384]{1,0:T(8,128)S(1)} custom-call(bf16[448,1536]{1,0:T(8,128)(2,1)S(1)} %get-tuple-element.35.refs_0_, bf16[448,1536]{1,0:T(8,128)(2,1)S(1)} %get-tuple-element.36.refs_1_, bf16[3072,384]{1,0:T(8,128)(2,1)S(1)} %get-tuple-element.28.refs_6_.refs_2_), custom_call_target="tpu_custom_call" | custom-call | flops 264241152 | bytes 1769472 | tf_op jit(solution)/shard_map/own_piece/pallas_call | solution.py:338
  24.6 1.3 %collective-permute-done.6 = bf16[112,384]{1,0:T(8,128)(2,1)S(1)} collective-permute-done((bf16[112,384]{1,0:T(8,128)(2,1)S(1)}, bf16[112,384]{1,0:T(8,128)(2,1)S(1)}, u32[]{:S(2)}, u32[]{:S(2)}) %collective-permute-start.6) | collective-permute-done | bytes 86048 | tf_op jit(solution)/shard_map/ppermute | solution.py:276
  26.0 1.0 %collective-permute-done.7 = bf16[112,384]{1,0:T(8,128)(2,1)S(1)} collective-permute-done((bf16[112,384]{1,0:T(8,128)(2,1)S(1)}, bf16[112,384]{1,0:T(8,128)(2,1)S(1)}, u32[]{:S(2)}, u32[]{:S(2)}) %collective-permute-start.7) | collective-permute-done | bytes 86048 | tf_op jit(solution)/shard_map/ppermute | solution.py:276
  26.9 1.1 %collective-permute-done.8 = bf16[112,384]{1,0:T(8,128)(2,1)S(1)} collective-permute-done((bf16[112,384]{1,0:T(8,128)(2,1)S(1)}, bf16[112,384]{1,0:T(8,128)(2,1)S(1)}, u32[]{:S(2)}, u32[]{:S(2)}) %collective-permute-start.8) | collective-permute-done | bytes 86048 | tf_op jit(solution)/shard_map/ppermute | solution.py:276
  28.1 3.0 %collective-permute-start.11 = (bf16[112,384]{1,0:T(8,128)(2,1)S(1)}, bf16[112,384]{1,0:T(8,128)(2,1)S(1)}, u32[]{:S(2)}, u32[]{:S(2)}) collective-permute-start(bf16[112,384]{1,0:T(8,128)(2,1)S(1)} %add_convert_fusion), channel_id=1, source_target_pairs={{0,6},{2,4},{4,2},{6,0},{1,7},{3,5},{5,3},{7,1},{8,14},{10,12},{12... | collective-permute-start | bytes 258056 | tf_op jit(solution)/shard_map/ppermute | solution.py:276
  31.1 0.0 collective-permute-start.10
  31.1 1.5 %collective-permute-start.9 = (bf16[112,384]{1,0:T(8,128)(2,1)S(1)}, bf16[112,384]{1,0:T(8,128)(2,1)S(1)}, u32[]{:S(2)}, u32[]{:S(2)}) collective-permute-start(bf16[112,384]{1,0:T(8,128)(2,1)S(1)} %add_convert_fusion), channel_id=1, source_target_pairs={{0,4},{2,6},{4,0},{6,2},{1,5},{3,7},{5,1},{7,3},{8,12},{10,14},{12... | collective-permute-start | bytes 258056 | tf_op jit(solution)/shard_map/ppermute | solution.py:276
  32.6 0.0 copy-done
  32.6 3.1 %features_grad.1 = bf16[2304,384]{1,0:T(8,128)(2,1)} custom-call(bf16[448,1536]{1,0:T(8,128)(2,1)S(1)} %get-tuple-element.35.refs_0_, bf16[448,1536]{1,0:T(8,128)(2,1)S(1)} %get-tuple-element.36.refs_1_, f32[2304,384]{1,0:T(8,128)S(1)} %get-tuple-element.37.refs_2_, bf16[432,384]{1,0:T(8,128)(2,1)S(1)} %copy-done), custom_call_target="tpu_custom_call" | custom-call | flops 1056964608 | bytes 7077888 | tf_op jit(solution)/shard_map/features_grad/pallas_call | solution.py:351
  35.7 0.0 collective-permute-done.11
  35.7 0.0 collective-permute-done.10
  35.7 0.8 %collective-permute-done.9 = bf16[112,384]{1,0:T(8,128)(2,1)S(1)} collective-permute-done((bf16[112,384]{1,0:T(8,128)(2,1)S(1)}, bf16[112,384]{1,0:T(8,128)(2,1)S(1)}, u32[]{:S(2)}, u32[]{:S(2)}) %collective-permute-start.9) | collective-permute-done | bytes 86048 | tf_op jit(solution)/shard_map/ppermute | solution.py:276
  36.5 0.1 multiply_convert_fusion.refs_0_
  36.6 1.0 %collective-permute-start.14 = (bf16[112,384]{1,0:T(8,128)(2,1)S(1)}, bf16[112,384]{1,0:T(8,128)(2,1)S(1)}, u32[]{:S(2)}, u32[]{:S(2)}) collective-permute-start(bf16[112,384]{1,0:T(8,128)(2,1)S(1)} %multiply_convert_fusion.refs_0_), channel_id=1, source_target_pairs={{0,24},{8,16},{16,8},{24,0},{1,25},{9,17},{17,9},{25,1},{2,26},{10... | collective-permute-start | bytes 258056 | tf_op jit(solution)/shard_map/ppermute | solution.py:276
  37.6 1.1 %collective-permute-start.13 = (bf16[112,384]{1,0:T(8,128)(2,1)S(1)}, bf16[112,384]{1,0:T(8,128)(2,1)S(1)}, u32[]{:S(2)}, u32[]{:S(2)}) collective-permute-start(bf16[112,384]{1,0:T(8,128)(2,1)S(1)} %multiply_convert_fusion.refs_0_), channel_id=1, source_target_pairs={{0,16},{8,24},{16,0},{24,8},{1,17},{9,25},{17,1},{25,9},{2,18},{10... | collective-permute-start | bytes 258056 | tf_op jit(solution)/shard_map/ppermute | solution.py:276
  38.7 1.4 %collective-permute-start.12 = (bf16[112,384]{1,0:T(8,128)(2,1)S(1)}, bf16[112,384]{1,0:T(8,128)(2,1)S(1)}, u32[]{:S(2)}, u32[]{:S(2)}) collective-permute-start(bf16[112,384]{1,0:T(8,128)(2,1)S(1)} %multiply_convert_fusion.refs_0_), channel_id=1, source_target_pairs={{0,8},{8,0},{16,24},{24,16},{1,9},{9,1},{17,25},{25,17},{2,10},{10... | collective-permute-start | bytes 258056 | tf_op jit(solution)/shard_map/ppermute | solution.py:276
  40.1 2.0 %collective-permute-done.14.refs_3_ = bf16[112,384]{1,0:T(8,128)(2,1)S(1)} collective-permute-done((bf16[112,384]{1,0:T(8,128)(2,1)S(1)}, bf16[112,384]{1,0:T(8,128)(2,1)S(1)}, u32[]{:S(2)}, u32[]{:S(2)}) %collective-permute-start.14) | collective-permute-done | bytes 86048 | tf_op jit(solution)/shard_map/ppermute | solution.py:276
  42.1 0.8 %collective-permute-done.13.refs_2_ = bf16[112,384]{1,0:T(8,128)(2,1)S(1)} collective-permute-done((bf16[112,384]{1,0:T(8,128)(2,1)S(1)}, bf16[112,384]{1,0:T(8,128)(2,1)S(1)}, u32[]{:S(2)}, u32[]{:S(2)}) %collective-permute-start.13) | collective-permute-done | bytes 86048 | tf_op jit(solution)/shard_map/ppermute | solution.py:276
  42.9 0.2 collective-permute-done.12.refs_1_
  43.2 0.9 %join_pieces.1 = f32[432,384]{1,0:T(8,128)} custom-call(bf16[112,384]{1,0:T(8,128)(2,1)S(1)} %multiply_convert_fusion.refs_0_, bf16[112,384]{1,0:T(8,128)(2,1)S(1)} %collective-permute-done.12.refs_1_, bf16[112,384]{1,0:T(8,128)(2,1)S(1)} %collective-permute-done.13.refs_2_, bf16[112,384]{1,0:T(8,128)(2,1)S(1)} %collective-permute-done.14.refs_3_), custom_call_target="tpu_custom_call" | custom-call | tf_op jit(solution)/shard_map/join_pieces/pallas_call | solution.py:365
  (1 shorter events, 0.0 us)
Async XLA Ops:
  0.6 7.1 %collective-permute-start.2 = (bf16[16,2304]{1,0:T(8,128)(2,1)}, bf16[16,2304]{1,0:T(8,128)(2,1)S(1)}, u32[]{:S(2)}, u32[]{:S(2)}) collective-permute-start(bf16[16,2304]{1,0:T(8,128)(2,1)} %bitcast.5), channel_id=1, source_target_pairs={{0,24},{8,16},{16,8},{24,0},{1,25},{9,17},{17,9},{25,1},{2,26},{10... | collective-permute-start | bytes 221192 | tf_op jit(solution)/shard_map/ppermute | solution.py:276
  4.6 4.6 %collective-permute-start.1 = (bf16[16,2304]{1,0:T(8,128)(2,1)}, bf16[16,2304]{1,0:T(8,128)(2,1)S(1)}, u32[]{:S(2)}, u32[]{:S(2)}) collective-permute-start(bf16[16,2304]{1,0:T(8,128)(2,1)} %bitcast.6), channel_id=1, source_target_pairs={{0,16},{8,24},{16,0},{24,8},{1,17},{9,25},{17,1},{25,9},{2,18},{10... | collective-permute-start | bytes 221192 | tf_op jit(solution)/shard_map/ppermute | solution.py:276
  5.1 4.6 %collective-permute-start = (bf16[16,2304]{1,0:T(8,128)(2,1)}, bf16[16,2304]{1,0:T(8,128)(2,1)S(1)}, u32[]{:S(2)}, u32[]{:S(2)}) collective-permute-start(bf16[16,2304]{1,0:T(8,128)(2,1)} %bitcast.7), channel_id=1, source_target_pairs={{0,8},{8,0},{16,24},{24,16},{1,9},{9,1},{17,25},{25,17},{2,10},{10... | collective-permute-start | bytes 221192 | tf_op jit(solution)/shard_map/ppermute | solution.py:276
  9.9 6.3 %collective-permute-start.3 = (bf16[4,64,128]{2,1,0:T(8,128)(2,1)S(1)}, bf16[4,64,128]{2,1,0:T(8,128)(2,1)S(1)}, u32[]{:S(2)}, u32[]{:S(2)}) collective-permute-start(bf16[4,64,128]{2,1,0:T(8,128)(2,1)S(1)} %get-tuple-element.23), channel_id=1, source_target_pairs={{0,6},{2,4},{4,2},{6,0},{1,7},{3,5},{5,3},{7,1},{8,14},{10,12},{12... | collective-permute-start | bytes 196616 | tf_op jit(solution)/shard_map/ppermute | solution.py:276
  13.5 4.3 %collective-permute-start.4 = (bf16[4,64,128]{2,1,0:T(8,128)(2,1)S(1)}, bf16[4,64,128]{2,1,0:T(8,128)(2,1)S(1)}, u32[]{:S(2)}, u32[]{:S(2)}) collective-permute-start(bf16[4,64,128]{2,1,0:T(8,128)(2,1)S(1)} %get-tuple-element.24), channel_id=1, source_target_pairs={{0,2},{2,0},{4,6},{6,4},{1,3},{3,1},{5,7},{7,5},{8,10},{10,8},{12,... | collective-permute-start | bytes 196616 | tf_op jit(solution)/shard_map/ppermute | solution.py:276
  13.6 5.2 %collective-permute-start.5 = (bf16[4,64,128]{2,1,0:T(8,128)(2,1)S(1)}, bf16[4,64,128]{2,1,0:T(8,128)(2,1)S(1)}, u32[]{:S(2)}, u32[]{:S(2)}) collective-permute-start(bf16[4,64,128]{2,1,0:T(8,128)(2,1)S(1)} %get-tuple-element.25), channel_id=1, source_target_pairs={{0,4},{2,6},{4,0},{6,2},{1,5},{3,7},{5,1},{7,3},{8,12},{10,14},{12... | collective-permute-start | bytes 196616 | tf_op jit(solution)/shard_map/ppermute | solution.py:276
  20.5 5.4 %collective-permute-start.6 = (bf16[112,384]{1,0:T(8,128)(2,1)S(1)}, bf16[112,384]{1,0:T(8,128)(2,1)S(1)}, u32[]{:S(2)}, u32[]{:S(2)}) collective-permute-start(bf16[112,384]{1,0:T(8,128)(2,1)S(1)} %get-tuple-element.31), channel_id=1, source_target_pairs={{0,24},{8,16},{16,8},{24,0},{1,25},{9,17},{17,9},{25,1},{2,26},{10... | collective-permute-start | bytes 258056 | tf_op jit(solution)/shard_map/ppermute | solution.py:276
  22.1 4.9 %collective-permute-start.7 = (bf16[112,384]{1,0:T(8,128)(2,1)S(1)}, bf16[112,384]{1,0:T(8,128)(2,1)S(1)}, u32[]{:S(2)}, u32[]{:S(2)}) collective-permute-start(bf16[112,384]{1,0:T(8,128)(2,1)S(1)} %get-tuple-element.32), channel_id=1, source_target_pairs={{0,8},{8,0},{16,24},{24,16},{1,9},{9,1},{17,25},{25,17},{2,10},{10... | collective-permute-start | bytes 258056 | tf_op jit(solution)/shard_map/ppermute | solution.py:276
  23.6 4.5 %collective-permute-start.8 = (bf16[112,384]{1,0:T(8,128)(2,1)S(1)}, bf16[112,384]{1,0:T(8,128)(2,1)S(1)}, u32[]{:S(2)}, u32[]{:S(2)}) collective-permute-start(bf16[112,384]{1,0:T(8,128)(2,1)S(1)} %get-tuple-element.33), channel_id=1, source_target_pairs={{0,16},{8,24},{16,0},{24,8},{1,17},{9,25},{17,1},{25,9},{2,18},{10... | collective-permute-start | bytes 258056 | tf_op jit(solution)/shard_map/ppermute | solution.py:276
  24.1 8.5 %copy-start = (bf16[432,384]{1,0:T(8,128)(2,1)S(1)}, bf16[432,384]{1,0:T(8,128)(2,1)}, u32[]{:S(2)}) copy-start(bf16[432,384]{1,0:T(8,128)(2,1)} %refs_3_.1) | copy-start | bytes 995332
  28.1 7.6 %collective-permute-start.11 = (bf16[112,384]{1,0:T(8,128)(2,1)S(1)}, bf16[112,384]{1,0:T(8,128)(2,1)S(1)}, u32[]{:S(2)}, u32[]{:S(2)}) collective-permute-start(bf16[112,384]{1,0:T(8,128)(2,1)S(1)} %add_convert_fusion), channel_id=1, source_target_pairs={{0,6},{2,4},{4,2},{6,0},{1,7},{3,5},{5,3},{7,1},{8,14},{10,12},{12... | collective-permute-start | bytes 258056 | tf_op jit(solution)/shard_map/ppermute | solution.py:276
  31.1 4.6 %collective-permute-start.10 = (bf16[112,384]{1,0:T(8,128)(2,1)S(1)}, bf16[112,384]{1,0:T(8,128)(2,1)S(1)}, u32[]{:S(2)}, u32[]{:S(2)}) collective-permute-start(bf16[112,384]{1,0:T(8,128)(2,1)S(1)} %add_convert_fusion), channel_id=1, source_target_pairs={{0,2},{2,0},{4,6},{6,4},{1,3},{3,1},{5,7},{7,5},{8,10},{10,8},{12,... | collective-permute-start | bytes 258056 | tf_op jit(solution)/shard_map/ppermute | solution.py:276
  31.1 5.4 %collective-permute-start.9 = (bf16[112,384]{1,0:T(8,128)(2,1)S(1)}, bf16[112,384]{1,0:T(8,128)(2,1)S(1)}, u32[]{:S(2)}, u32[]{:S(2)}) collective-permute-start(bf16[112,384]{1,0:T(8,128)(2,1)S(1)} %add_convert_fusion), channel_id=1, source_target_pairs={{0,4},{2,6},{4,0},{6,2},{1,5},{3,7},{5,1},{7,3},{8,12},{10,14},{12... | collective-permute-start | bytes 258056 | tf_op jit(solution)/shard_map/ppermute | solution.py:276
  36.6 5.5 %collective-permute-start.14 = (bf16[112,384]{1,0:T(8,128)(2,1)S(1)}, bf16[112,384]{1,0:T(8,128)(2,1)S(1)}, u32[]{:S(2)}, u32[]{:S(2)}) collective-permute-start(bf16[112,384]{1,0:T(8,128)(2,1)S(1)} %multiply_convert_fusion.refs_0_), channel_id=1, source_target_pairs={{0,24},{8,16},{16,8},{24,0},{1,25},{9,17},{17,9},{25,1},{2,26},{10... | collective-permute-start | bytes 258056 | tf_op jit(solution)/shard_map/ppermute | solution.py:276
  37.6 5.3 %collective-permute-start.13 = (bf16[112,384]{1,0:T(8,128)(2,1)S(1)}, bf16[112,384]{1,0:T(8,128)(2,1)S(1)}, u32[]{:S(2)}, u32[]{:S(2)}) collective-permute-start(bf16[112,384]{1,0:T(8,128)(2,1)S(1)} %multiply_convert_fusion.refs_0_), channel_id=1, source_target_pairs={{0,16},{8,24},{16,0},{24,8},{1,17},{9,25},{17,1},{25,9},{2,18},{10... | collective-permute-start | bytes 258056 | tf_op jit(solution)/shard_map/ppermute | solution.py:276
  38.7 4.5 %collective-permute-start.12 = (bf16[112,384]{1,0:T(8,128)(2,1)S(1)}, bf16[112,384]{1,0:T(8,128)(2,1)S(1)}, u32[]{:S(2)}, u32[]{:S(2)}) collective-permute-start(bf16[112,384]{1,0:T(8,128)(2,1)S(1)} %multiply_convert_fusion.refs_0_), channel_id=1, source_target_pairs={{0,8},{8,0},{16,24},{24,16},{1,9},{9,1},{17,25},{25,17},{2,10},{10... | collective-permute-start | bytes 258056 | tf_op jit(solution)/shard_map/ppermute | solution.py:276
